TPU v7x, 128 devices: a whole 4x4x4 slice. The times are simulated.
128 devices in a mesh: pts: 32 (over x, y, core), head: 4 (over z).
Axes of the slice: x: 4, y: 4, z: 4, core: 2. Of those that a mesh axis runs over, the one named last changes fastest.
Arguments:
- points: bfloat16 [262144, 256], P('pts'), may hold values from -6 to 6
- cotangent: bfloat16 [262144, 256], P('pts'), may hold values from -6 to 6
- gain_one: bfloat16 [256], replicated, may hold values from 0.25 to 1.75
- w_in: bfloat16 [256, 256], P(None, 'head'), may hold values from -0.375 to 0.375
- slice_weight: bfloat16 [32, 64], replicated, may hold values from -1 to 1
- sharp: bfloat16 [8], P('head'), may hold values from 0.5 to 3
- w_query: bfloat16 [32, 32], replicated, may hold values from -1 to 1
- w_key: bfloat16 [32, 32], replicated, may hold values from -1 to 1
- w_value: bfloat16 [32, 32], replicated, may hold values from -1 to 1
- w_out: bfloat16 [256, 256], P('head'), may hold values from -0.375 to 0.375
- gain_two: bfloat16 [256], replicated, may hold values from 0.25 to 1.75
- w_up: bfloat16 [256, 1024], P(None, 'head'), may hold values from -0.375 to 0.375
- w_down: bfloat16 [1024, 256], P('head'), may hold values from -0.1875 to 0.1875
Outputs:
- mixed: float32 [262144, 256], P('pts')
- grad_points: float32 [262144, 256], P('pts')
- grad_in: float32 [256, 256], P(None, 'head')
- grad_slice: float32 [32, 64], replicated
- grad_sharp: float32 [8], P('head')
- grad_query: float32 [32, 32], replicated
- grad_key: float32 [32, 32], replicated
- grad_value: float32 [32, 32], replicated
- grad_out: float32 [256, 256], P('head')
- grad_up: float32 [256, 1024], P(None, 'head')
- grad_down: float32 [1024, 256], P('head')
- grad_gain1: float32 [256], replicated
- grad_gain2: float32 [256], replicated
All inputs are finite; a program needn't handle non-finite values.
Results may differ from a plain program's by a relative error of at most 0.024.
Values may be sent and summed in bfloat16 or wider, within the bound.
No kernel may reach another device: no remote copies, remote signals or barrier semaphores. Data moves between devices by JAX's collectives and lax.ppermute only.
A program may use at most 192 MiB of HBM per device.

v0:
```python
import functools
import jax
import jax.numpy as jnp
from jax import lax
from jax.experimental import pallas as pl
from jax.experimental.pallas import tpu as pltpu
from jax.sharding import PartitionSpec as P

HEAD_DIM = 32
SLICES = 64
C = 256
HEADS = 8
BLOCKS = 4
GH = HEADS // BLOCKS
HM = HEADS * SLICES
C0 = 0.7978845608028654
C1 = 0.7978845608028654 * 0.044715
BF = jnp.bfloat16
F32 = jnp.float32
VMEM_LIMIT = 56 * 1024 * 1024


def dot(a, b, precision=None):
    return lax.dot_general(
        a, b, (((1,), (0,)), ((), ())), preferred_element_type=F32, precision=precision
    )


def dot_nt(a, b, precision=None):
    return lax.dot_general(
        a, b, (((1,), (1,)), ((), ())), preferred_element_type=F32, precision=precision
    )


def norm_parts(value):
    centred = value - jnp.mean(value, -1, keepdims=True)
    scale = lax.rsqrt(jnp.mean(centred * centred, -1, keepdims=True) + 1e-05)
    return centred * scale, scale


def norm_back_rows(grad, normed, scale, gain):
    scaled = grad * gain
    return scale * (
        scaled
        - jnp.mean(scaled, -1, keepdims=True)
        - normed * jnp.mean(scaled * normed, -1, keepdims=True)
    )


def sharp_row(block, which, width):
    row = block[which : which + 1, :].astype(F32)
    return jnp.concatenate([row] * (width // C), axis=1)


def softmax_slices(raw, sharp):
    logits = raw * sharp
    grown = jnp.exp(logits - jnp.max(logits, 0, keepdims=True))
    return grown * (1.0 / jnp.sum(grown, 0, keepdims=True))


def fold_rows(value):
    return jnp.sum(value.reshape(value.shape[0] // 8, 8, value.shape[1]), 0)


def prep_kernel(
    w_up, w_down, w_in, w_out, sharp, slice_weight, one, two, pack, slices_t, slices, gain1, gain2, s_scr
):
    gain1[...] = one[...].astype(F32).reshape(1, C)
    gain2[...] = two[...].astype(F32).reshape(1, C)
    pack[0:256, :] = w_up[...].T
    pack[256:512, :] = w_down[...]
    pack[512:576, :] = w_in[...]
    pack[576:640, :] = w_out[...]
    row = lax.broadcasted_iota(jnp.int32, (16, C), 0)
    pack[640:656, :] = jnp.where(row == 0, sharp[0], jnp.where(row == 1, sharp[1], 0.0)).astype(BF)
    s_scr[...] = jnp.zeros_like(s_scr)
    weight = slice_weight[...].astype(F32)
    twice = jnp.concatenate([weight, weight], 1)
    lane = lax.broadcasted_iota(jnp.int32, (HEAD_DIM, 128), 1)
    for k in range(BLOCKS):
        at = slice(k * 128, (k + 1) * 128)
        s_scr[k * 64 : k * 64 + 32, at] = jnp.where(lane < SLICES, twice, 0.0)
        s_scr[k * 64 + 32 : k * 64 + 64, at] = jnp.where(lane < SLICES, 0.0, twice)
    slices[...] = s_scr[...].astype(BF)
    slices_t[...] = s_scr[...].T.astype(BF)


def fill_kernel(z, *refs):
    out = refs[-1]
    for k, ref in enumerate(refs[:-2]):

        @pl.when(pl.program_id(0) == k)
        def _():
            out[...] = ref[...].astype(F32)


def finish_kernel(z, first, second, before, t0, t1, t2, t3, w0, w1, *refs):
    out, gin, gslice, gsharp, gq, gk, gv, gout, gup, gdown, g1, g2 = refs
    fill_kernel(z, first, second, before, out)

    @pl.when(pl.program_id(0) == 0)
    def _():
        a, b, c, d = (t[...].astype(F32) for t in (t0, t1, t2, t3))
        tail = (a + c) + (b + d)
        gin[...] = tail[0:64]
        gslice[...] = tail[64:96, 0:64] + tail[64:96, 64:128]
        gq[...] = tail[64:96, 128:160]
        gk[...] = tail[64:96, 160:192]
        gv[...] = tail[64:96, 192:224]
        gsharp[...] = jnp.concatenate(
            [
                jnp.sum(tail[96:97, 0:128], 1, keepdims=True),
                jnp.sum(tail[96:97, 128:256], 1, keepdims=True),
            ],
            1,
        )
        g1[...] = tail[97:98]
        g2[...] = tail[98:99]
        gout[...] = tail[104:168]

        @pl.when(z[1] == 0)
        def _():
            gdown[...] = w0[...].T
            gup[...] = w1[...]

        @pl.when(z[1] == 1)
        def _():
            gdown[...] = w1[...].T
            gup[...] = w0[...]


def own_sums_kernel(pts, gain, w_in, spread_slices, sharp, out, acc, den):
    step = pl.program_id(0)

    @pl.when(step == 0)
    def _():
        acc[...] = jnp.zeros_like(acc)
        den[...] = jnp.zeros_like(den)

    normed, _ = norm_parts(pts[...].astype(F32))
    normed_in = (normed * gain[...].astype(F32)).astype(BF)
    middle = dot_nt(normed_in, w_in[...]).astype(BF)
    raw = dot_nt(spread_slices[:, 0:64], middle)
    rows = raw.shape[1]
    sharps = sharp[...]
    parts = [
        softmax_slices(raw[h * SLICES : (h + 1) * SLICES], sharp_row(sharps, h, rows))
        for h in range(GH)
    ]
    weights = jnp.concatenate(parts, 0)
    total = weights[:, 0:128]
    for j in range(1, rows // 128):
        total = total + weights[:, j * 128 : (j + 1) * 128]
    den[...] += total
    acc[...] += dot(weights.astype(BF), middle)

    @pl.when(step == pl.num_programs(0) - 1)
    def _():
        flipped = acc[...].T
        lane = lax.broadcasted_iota(jnp.int32, (HEAD_DIM, 128), 1)
        out[0:HEAD_DIM, :] = jnp.where(lane < SLICES, flipped[:HEAD_DIM], flipped[HEAD_DIM:])
        row = jnp.sum(den[...].T, 0, keepdims=True)
        out[HEAD_DIM : HEAD_DIM + 8, :] = jnp.broadcast_to(row, (8, 128))


def weights_kernel(z, pts, gain, in0, in1, in2, in3, spread_slices, s0, s1, s2, s3, *rest):
    wt, mid, w_in = rest

    @pl.when(pl.program_id(0) == 0)
    def _():
        for k, ref in enumerate((in0, in1, in2, in3)):
            w_in[k * 64 : (k + 1) * 64, :] = ref[...]

    normed, _ = norm_parts(pts[...].astype(F32))
    normed_in = (normed * gain[...].astype(F32)).astype(BF)
    middle = dot_nt(normed_in, w_in[...]).astype(BF)
    mid[...] = middle
    raw = dot_nt(spread_slices[...], middle)
    rows = raw.shape[1]
    for h in range(HEADS):
        sharp = sharp_row((s0, s1, s2, s3)[h // GH][...], h % GH, rows)
        wt[h * SLICES : (h + 1) * SLICES, :] = softmax_slices(
            raw[h * SLICES : (h + 1) * SLICES], sharp
        ).astype(BF)


def place_tokens(flat, tokens):
    flat[...] = jnp.zeros_like(flat)
    lane = lax.broadcasted_iota(jnp.int32, (HEAD_DIM, 128), 1)
    for k, ref in enumerate(tokens):
        t = ref[0:HEAD_DIM, :]
        flat[k * 64 : k * 64 + 32, k * 128 : (k + 1) * 128] = jnp.where(lane < SLICES, t, 0.0)
        flat[k * 64 + 32 : k * 64 + 64, k * 128 : (k + 1) * 128] = jnp.where(
            lane < SLICES, 0.0, t
        )


def own_block(flipped, k):
    lane = lax.broadcasted_iota(jnp.int32, (HEAD_DIM, 128), 1)
    block = flipped[k * 64 : (k + 1) * 64, k * 128 : (k + 1) * 128]
    return jnp.where(lane < SLICES, block[:HEAD_DIM], block[HEAD_DIM:])


def mlp_kernel(z, pts, cot, wt, *refs):
    tokens, refs = refs[:4], refs[4:]
    gain, refs = refs[0], refs[1:]
    ups, downs, outs, refs = refs[:4], refs[4:8], refs[8:12], refs[12:]
    mixed, gres, gspread, low_mixed, gt0, gt1, gt2, gt3, wg0, wg1, wg2, wg3, gout, g2 = refs[:14]
    flat, tok_t, w_out, acc_tok, acc_w = refs[14:]
    step = pl.program_id(0)

    @pl.when(step == 0)
    def _():
        place_tokens(flat, tokens)
        tok_t[...] = flat[...].astype(BF)
        for k, ref in enumerate(outs):
            w_out[k * 64 : (k + 1) * 64, :] = ref[...]
        acc_tok[...] = jnp.zeros_like(acc_tok)
        acc_w[...] = jnp.zeros_like(acc_w)
        gout[...] = jnp.zeros_like(gout)
        g2[...] = jnp.zeros_like(g2)

    weights = wt[...]
    spread_t = dot(tok_t[...], weights).astype(BF)
    spread = spread_t.T
    resid = pts[...].astype(F32) + dot(spread, w_out[...])
    normed, scale = norm_parts(resid)
    gain_row = gain[...].astype(F32)
    normed_mid = (normed * gain_row).astype(BF)
    cotangent = cot[...]
    total = resid
    gmid = None
    cot_t = cotangent.T
    normed_t = normed_mid.T
    for k in range(BLOCKS):
        up, down = ups[k][...], downs[k][...]
        hidden = dot_nt(normed_mid, up)
        square = hidden * hidden
        inner = jnp.tanh(hidden * (C0 + C1 * square))
        half = 0.5 + 0.5 * inner
        gelu = hidden * half
        active = gelu.astype(BF)
        total = total + dot(active, down)
        slope = half + gelu * (1.0 - half) * (2.0 * C0 + 6.0 * C1 * square)
        ghid = (dot_nt(cotangent, down) * slope).astype(BF)
        part = dot(ghid, up)
        gmid = part if gmid is None else gmid + part
        acc_w[k, 0:C, :] += dot(cot_t, active)
        acc_w[k, C : 2 * C, :] += dot(normed_t, ghid)
    mixed[...] = total
    grad = cotangent.astype(F32) + norm_back_rows(gmid, normed, scale, gain_row)
    low = grad.astype(BF)
    gres[...] = low
    gsp = dot_nt(low, w_out[...]).astype(BF)
    gspread[...] = gsp
    low_mixed[...] = total.astype(BF)
    acc_tok[...] += dot(weights, gsp)
    gout[...] += dot(spread_t, low)
    g2[...] += fold_rows(gmid * normed)

    @pl.when(step == pl.num_programs(0) - 1)
    def _():
        flipped = acc_tok[...].T
        for k, ref in enumerate((gt0, gt1, gt2, gt3)):
            ref[...] = own_block(flipped, k)
        for k, ref in enumerate((wg0, wg1, wg2, wg3)):
            ref[...] = acc_w[k].astype(ref.dtype)


def points_kernel(z, pts, wt, mid, gspread, gres, *refs):
    tokens, gnums, refs = refs[:4], refs[4:8], refs[8:]
    gain, slices_t, slices, refs = refs[0], refs[1], refs[2], refs[3:]
    ins, sharps, refs = refs[:4], refs[4:8], refs[8:]
    qkv, g2, gout, gpts, low_a, low_b, o0, o1, o2, o3 = refs[:10]
    flat, tok, gn_t, gn, gden, w_in, acc_in, acc_s, acc_g, acc_h = refs[10:]
    step = pl.program_id(0)

    @pl.when(step == 0)
    def _():
        place_tokens(flat, tokens)
        tok[...] = flat[...].T.astype(BF)
        place_tokens(flat, gnums)
        gn_t[...] = flat[...].astype(BF)
        gn[...] = flat[...].T.astype(BF)
        for k, ref in enumerate(gnums):
            row = ref[HEAD_DIM : HEAD_DIM + 1, :]
            gden[k * 128 : (k + 1) * 128, :] = jnp.broadcast_to(row, (128, 128)).T
        for k, ref in enumerate(ins):
            w_in[k * 64 : (k + 1) * 64, :] = ref[...]
        acc_in[...] = jnp.zeros_like(acc_in)
        acc_s[...] = jnp.zeros_like(acc_s)
        acc_g[...] = jnp.zeros_like(acc_g)
        acc_h[...] = jnp.zeros_like(acc_h)

    normed, scale = norm_parts(pts[...].astype(F32))
    gain_row = gain[...].astype(F32)
    weights = wt[...]
    middle = mid[...]
    rows = weights.shape[1]
    gw = dot_nt(tok[...], gspread[...]) + dot_nt(gn[...], middle)
    pieces, sharp_sums = [], []
    raw = dot_nt(slices_t[...], middle)
    for h in range(HEADS):
        at = slice(h * SLICES, (h + 1) * SLICES)
        sharp = sharp_row(sharps[h // GH][...], h % GH, rows)
        w = softmax_slices(raw[at], sharp)
        g = gw[at] + jnp.concatenate([gden[at, :]] * (rows // 128), axis=1)
        gl = w * (g - jnp.sum(w * g, 0, keepdims=True))
        pieces.append((gl * sharp).astype(BF))
        sharp_sums.append(jnp.sum(gl * raw[at], 0, keepdims=True))
    graw = jnp.concatenate(pieces, 0)
    gmid_t = (dot(gn_t[...], weights) + dot(slices[...], graw)).astype(BF)
    gmid = gmid_t.T
    gnormed = dot(gmid, w_in[...])
    result = gres[...].astype(F32) + norm_back_rows(gnormed, normed, scale, gain_row)
    gpts[...] = result

    @pl.when(step < pl.num_programs(0) // 2)
    def _():
        low_a[...] = result.astype(BF)

    @pl.when(step >= pl.num_programs(0) // 2)
    def _():
        low_b[...] = result.astype(BF)

    normed_in = (normed * gain_row).astype(BF)
    acc_in[...] += dot(gmid_t, normed_in)
    acc_s[...] += dot(graw, middle)
    acc_g[...] += fold_rows(gnormed * normed)
    acc_h[...] += jnp.concatenate(sharp_sums, 0)

    @pl.when(step == pl.num_programs(0) - 1)
    def _():
        flipped = acc_s[...].T
        gsharp = acc_h[:, 0:128]
        for j in range(1, rows // 128):
            gsharp = gsharp + acc_h[:, j * 128 : (j + 1) * 128]
        gslice = jnp.zeros((HEAD_DIM, 128), F32)
        for k in range(BLOCKS):
            gslice = gslice + own_block(flipped, k)
        gain1 = jnp.sum(acc_g[...], 0, keepdims=True)
        gain2 = jnp.sum(g2[...], 0, keepdims=True)
        for k, ref in enumerate((o0, o1, o2, o3)):
            ref[0:64, :] = acc_in[k * 64 : (k + 1) * 64, :].astype(ref.dtype)
            ref[64:96, 0:128] = gslice.astype(ref.dtype)
            ref[64:96, 128:256] = qkv[...].astype(ref.dtype)
            wide = jnp.concatenate([gsharp[2 * k : 2 * k + 1], gsharp[2 * k + 1 : 2 * k + 2]], 1)
            ref[96:104, :] = jnp.concatenate(
                [wide, gain1, gain2, jnp.zeros((5, C), F32)], 0
            ).astype(ref.dtype)
            ref[104:168, :] = gout[k * 64 : (k + 1) * 64, :].astype(ref.dtype)


HIGH = lax.Precision.HIGHEST


def token_parts(nd, wq, wk, wv):
    padded = jnp.concatenate([nd, jnp.zeros((88, 128), F32)], 0).T
    denom = padded[:, HEAD_DIM : HEAD_DIM + 1]
    tok = padded[:, :HEAD_DIM] / denom
    q, k, v = dot(tok, wq, HIGH), dot(tok, wk, HIGH), dot(tok, wv, HIGH)
    scores = dot_nt(q, k, HIGH) * (1.0 / HEAD_DIM**0.5)
    row = lax.broadcasted_iota(jnp.int32, (128, 128), 0) < SLICES
    col = lax.broadcasted_iota(jnp.int32, (128, 128), 1) < SLICES
    same = row == col
    scores = jnp.where(same, scores, -jnp.inf)
    p = jnp.exp(scores - jnp.max(scores, -1, keepdims=True))
    p = p / jnp.sum(p, -1, keepdims=True)
    return denom, tok, q, k, v, p


def flip(value):
    n = value.shape[1]
    return jnp.concatenate([value, jnp.zeros((128, 128 - n), F32)], 1).T[:n]


def tokens_kernel(a, b, c, d, wq, wk, wv, total, tokens):
    nd = (a[...] + c[...]) + (b[...] + d[...])
    total[...] = nd
    _, _, _, _, v, p = token_parts(nd, *(w[...].astype(F32) for w in (wq, wk, wv)))
    mixed = dot(p, v, HIGH).astype(BF).astype(F32)
    tokens[...] = flip(mixed)


def tokens_back_kernel(scale, nd, a, b, c, d, wq, wk, wv, gn, qkv):
    gt = (a[...] + c[...]) + (b[...] + d[...])
    g = jnp.concatenate([gt, jnp.zeros((96, 128), F32)], 0).T[:, :HEAD_DIM]
    wq, wk, wv = (w[...].astype(F32) for w in (wq, wk, wv))
    denom, tok, q, k, v, p = token_parts(nd[...], wq, wk, wv)
    dv = dot(p.T, g, HIGH)
    dp = dot_nt(g, v, HIGH)
    ds = p * (dp - jnp.sum(p * dp, -1, keepdims=True)) * (1.0 / HEAD_DIM**0.5)
    dq = dot(ds, k, HIGH)
    dk = dot(ds.T, q, HIGH)
    gmt = dot_nt(dq, wq, HIGH) + dot_nt(dk, wk, HIGH) + dot_nt(dv, wv, HIGH)
    gnum = (gmt / denom).astype(BF).astype(F32)
    gden = -jnp.sum(gmt * tok, -1, keepdims=True) / denom
    gn[0:HEAD_DIM, :] = flip(gnum)
    gn[HEAD_DIM : HEAD_DIM + 8, :] = flip(jnp.broadcast_to(gden, (128, 8)))
    tok_t = flip(tok)
    qkv[...] = scale * jnp.concatenate(
        [dot(tok_t, dq, HIGH), dot(tok_t, dk, HIGH), dot(tok_t, dv, HIGH), jnp.zeros((32, 32), F32)],
        1,
    )


def full(shape):
    return pl.BlockSpec(shape, lambda *_: (0,) * len(shape))


def part(shape, row):
    return pl.BlockSpec(shape, lambda *_: (row, 0))


def shape_of(shape, dtype):
    return jax.ShapeDtypeStruct(shape, dtype)


def cost(us):
    return pl.CostEstimate(flops=int(us * 1.0e6), bytes_accessed=1024, transcendentals=0)


UP, DOWN, WIN, WOUT, SHARP = (256, 0), (256, 1), (64, 8), (64, 9), (16, 40)
WIDE, NARROW = 1024, 512
TAIL = 168


def pack_specs(kind):
    return [part((kind[0], C), kind[1])] * BLOCKS


def local(
    pts_size,
    points,
    cotangent,
    gain_one,
    w_in,
    slice_weight,
    sharp,
    w_query,
    w_key,
    w_value,
    w_out,
    gain_two,
    w_up,
    w_down,
):
    axes = ("pts", "head")
    rows = points.shape[0]
    quarter = rows // BLOCKS

    def pull(value, dx=0, dy=0, dc=0, dz=0):
        pairs = []
        for p in range(pts_size):
            x, y, c = p // 8, (p // 2) % 4, p % 2
            there = p
            if pts_size > 1:
                there = (((x + dx) % 4) * 4 + (y + dy) % 4) * 2 + (c + dc) % 2
            for z in range(BLOCKS):
                pairs.append((there * BLOCKS + (z + dz) % BLOCKS, p * BLOCKS + z))
        return lax.ppermute(value, axes, pairs)

    def pulls(value, axis):
        return [pull(value, **{axis: k}) for k in (1, 2, 3)]

    def tie(*values):
        return lax.optimization_barrier(values)

    def add4(a, r):
        return (a + r[1].astype(F32)) + (r[0].astype(F32) + r[2].astype(F32))

    def core_sum(value):
        return value + pull(value, dc=1) if pts_size > 1 else value

    def rounded(value):
        return lax.reduce_precision(value, 8, 7)

    def axis_peers(value, axis):
        if pts_size == 1:
            return [jnp.zeros_like(value)] * 3
        return pulls(value, axis)

    core = lax.axis_index("pts").astype(jnp.int32) % 2
    z = jnp.stack([lax.axis_index("head").astype(jnp.int32), core])

    def row_spec(size, away, first=0):
        n = quarter // size
        return pl.BlockSpec(
            (size, C), lambda i, z: (lax.rem(z[0] + away, BLOCKS) * n + first // size + i, 0)
        )

    def own_spec(size, first=0):
        return pl.BlockSpec((size, C), lambda i, z: (first // size + i, 0))

    def own_cols(size, first=0):
        return pl.BlockSpec((HM, size), lambda i, z: (0, first // size + i))

    def grid(steps, in_specs, out_specs, scratch=()):
        return pltpu.PrefetchScalarGridSpec(
            num_scalar_prefetch=1,
            grid=steps,
            in_specs=in_specs,
            out_specs=out_specs,
            scratch_shapes=scratch,
        )

    any_spec = pl.BlockSpec(memory_space=pl.ANY)
    params = pltpu.CompilerParams(vmem_limit_bytes=VMEM_LIMIT)

    wq, wk, wv = w_query, w_key, w_value
    pack, slices_t, slices, gain1, gain2 = pl.pallas_call(
        prep_kernel,
        out_shape=[shape_of((656, C), BF), shape_of((HM, C), BF), shape_of((C, HM), BF)]
        + [shape_of((1, C), F32)] * 2,
        in_specs=[pl.BlockSpec(memory_space=pltpu.VMEM)] * 4
        + [pl.BlockSpec(memory_space=pltpu.SMEM)]
        + [pl.BlockSpec(memory_space=pltpu.VMEM)] * 3,
        scratch_shapes=[pltpu.VMEM((C, HM), F32)],
        compiler_params=params,
        cost_estimate=cost(2),
        name="prep",
    )(w_up, w_down, w_in.T, w_out, sharp.astype(F32), slice_weight, gain_one, gain_two)
    packs = [pack] + pulls(pack, "dz")

    nd = pl.pallas_call(
        own_sums_kernel,
        grid=(rows // (2 * WIDE),),
        in_specs=[
            pl.BlockSpec((2 * WIDE, C), lambda i: (i, 0)),
            full((1, C)),
            part((64, C), WIN[1]),
            part((128, C), 0),
            part((16, C), SHARP[1]),
        ],
        out_specs=full((40, 128)),
        out_shape=shape_of((40, 128), F32),
        scratch_shapes=[pltpu.VMEM((128, 64), F32), pltpu.VMEM((128, 128), F32)],
        compiler_params=params,
        cost_estimate=cost(8),
        name="own_sums",
    )(points, gain1, pack, slices_t, pack)

    half = quarter // 2

    def weights_call():
        return pl.pallas_call(
            weights_kernel,
            grid_spec=grid(
                (quarter // WIDE,),
                [row_spec(WIDE, 0), full((1, C))]
                + pack_specs(WIN)
                + [full((HM, C))]
                + pack_specs(SHARP),
                [own_cols(WIDE), own_spec(WIDE)],
                [pltpu.VMEM((C, C), BF)],
            ),
            out_shape=[shape_of((HM, quarter), BF), shape_of((quarter, C), BF)],
            compiler_params=params,
            cost_estimate=cost(5),
            name="weights",
        )(z, points, gain1, *packs, slices_t, *packs)

    def mlp_call(tokens, wt):
        size = WIDE
        out_shape = [shape_of((rows, C), F32)] + [shape_of((quarter, C), BF)] * 3
        out_shape += [shape_of((HEAD_DIM, 128), F32)] * 4
        out_shape += [shape_of((2 * C, C), F32)] + [shape_of((2 * C, C), BF)] * 3
        out_shape += [shape_of((C, C), F32), shape_of((8, C), F32)]
        out_specs = [row_spec(size, 0)] + [own_spec(size)] * 3
        out_specs += [full((HEAD_DIM, 128))] * 4 + [full((2 * C, C))] * 4
        out_specs += [full((C, C)), full((8, C))]
        return pl.pallas_call(
            mlp_kernel,
            grid_spec=grid(
                (quarter // size,),
                [row_spec(size, 0), row_spec(size, 0), own_cols(size)]
                + [full((HEAD_DIM, 128))] * 4
                + [full((1, C))]
                + pack_specs(UP)
                + pack_specs(DOWN)
                + pack_specs(WOUT),
                out_specs,
                [
                    pltpu.VMEM((C, HM), F32),
                    pltpu.VMEM((C, HM), BF),
                    pltpu.VMEM((C, C), BF),
                    pltpu.VMEM((HM, C), F32),
                    pltpu.VMEM((BLOCKS, 2 * C, C), F32),
                ],
            ),
            out_shape=out_shape,
            compiler_params=params,
            cost_estimate=cost(16),
            name="mlp",
        )(z, points, cotangent, wt, *tokens, gain2, *packs, *packs, *packs)

    def points_call(tokens, gnums, wt, mid, gspread, gres, qkv, g2, gout):
        size = NARROW
        steps = quarter // size
        halves = [
            pl.BlockSpec((size, C), lambda i, z: (jnp.minimum(i, steps // 2 - 1), 0)),
            pl.BlockSpec((size, C), lambda i, z: (jnp.maximum(i - steps // 2, 0), 0)),
        ]
        return pl.pallas_call(
            points_kernel,
            grid_spec=grid(
                (steps,),
                [row_spec(size, 0), own_cols(size)]
                + [own_spec(size)] * 3
                + [full((HEAD_DIM, 128))] * 4
                + [full((40, 128))] * 4
                + [full((1, C)), full((HM, C)), full((C, HM))]
                + pack_specs(WIN)
                + pack_specs(SHARP)
                + [full((HEAD_DIM, 128)), full((8, C)), full((C, C))],
                [row_spec(size, 0)] + halves + [full((TAIL, C))] * 4,
                [
                    pltpu.VMEM((C, HM), F32),
                    pltpu.VMEM((HM, C), BF),
                    pltpu.VMEM((C, HM), BF),
                    pltpu.VMEM((HM, C), BF),
                    pltpu.VMEM((HM, 128), F32),
                    pltpu.VMEM((C, C), BF),
                    pltpu.VMEM((C, C), F32),
                    pltpu.VMEM((HM, C), F32),
                    pltpu.VMEM((8, C), F32),
                    pltpu.VMEM((HEADS, size), F32),
                ],
            ),
            out_shape=[shape_of((rows, C), F32)]
            + [shape_of((half, C), BF)] * 2
            + [shape_of((TAIL, C), F32)]
            + [shape_of((TAIL, C), BF)] * 3,
            compiler_params=params,
            cost_estimate=cost(12),
            name="points",
        )(
            z, points, wt, mid, gspread, gres, *tokens, *gnums, gain1, slices_t, slices,
            *packs, *packs, qkv, g2, gout
        )

    half = quarter // 2

    def fill_out(at):
        return pl.BlockSpec(
            (half, C), lambda i, z: (lax.rem(2 * z[0] + at(i), 2 * BLOCKS), 0)
        )

    def fill_call(at, parts, before):
        n = len(parts)
        return pl.pallas_call(
            fill_kernel,
            grid_spec=grid((n,), [s for _, s in parts] + [any_spec], fill_out(at)),
            out_shape=shape_of((rows, C), F32),
            input_output_aliases={n + 1: 0},
            compiler_params=params,
            cost_estimate=cost(3),
            name="fill",
        )(z, *[p for p, _ in parts], before)

    def halves_of(value):
        return [(value, part((half, C), 0)), (value, part((half, C), 1))]

    def whole(*values):
        return [(v, full((half, C))) for v in values]

    nd = core_sum(nd)
    got = axis_peers(nd, "dx")
    nd, packs[0] = tie(nd, packs[0])
    wt, mid = weights_call()
    got, wt = tie(got, wt)
    nd = add4(nd, got)
    got = axis_peers(nd, "dy")
    nd, own_tokens = pl.pallas_call(
        tokens_kernel,
        out_shape=[shape_of((40, 128), F32), shape_of((HEAD_DIM, 128), F32)],
        compiler_params=params,
        cost_estimate=cost(3),
        name="tokens",
    )(nd, *got, wq, wk, wv)
    tokens = [own_tokens] + pulls(own_tokens, "dz")

    result = mlp_call(tokens, wt)
    mixed, gres, gspread, send = result[:4]
    gts, wgs, (gout, g2) = result[4:8], result[8:12], result[12:]

    got = [pull(gts[BLOCKS - k], dz=k) for k in (1, 2, 3)]
    wgot = [pull(wgs[3], dz=1), pull(wgs[2], dz=2)]
    gt = add4(gts[0], got)
    gt, wg1 = tie(gt, wgs[1])
    wgot.append(pull(wg1, dz=3))
    gt = core_sum(gt)
    got = axis_peers(gt, "dx")
    got, wgot = tie(got, wgot)
    gt = add4(gt, got)
    got = axis_peers(gt, "dy")
    gt, send = tie(gt, send)
    near = [pull(send, dz=1), pull(send, dz=3)]
    wsum = add4(wgs[0], wgot)
    wlow = wsum.astype(BF)
    own_gn, qkv = pl.pallas_call(
        functools.partial(tokens_back_kernel, 1.0 / pts_size),
        out_shape=[shape_of((40, 128), F32), shape_of((HEAD_DIM, 128), F32)],
        compiler_params=params,
        cost_estimate=cost(4),
        name="tokens_back",
    )(nd, gt, *got, wq, wk, wv)
    got = pulls(own_gn, "dz")
    own_gn, wsum, wlow = tie(own_gn, wsum, wlow)
    if pts_size > 1:
        wsum = rounded(wsum) + pull(wlow, dc=1).astype(F32)
        wlow = lax.dynamic_slice_in_dim(wsum, core * C, C, 0).astype(BF)
    got, wlow = tie(got, wlow)
    wgot = axis_peers(wlow[:C], "dx")
    got, near = tie(got, near)
    near2 = [pull(near[0][:half], dz=1), pull(near[1][half:], dz=3)]
    gnums = [own_gn] + list(got)

    result = points_call(tokens, gnums, wt, mid, gspread, gres, qkv, g2, gout)
    gpts, low_a, low_b, outs = result[0], result[1], result[2], result[3:]
    gpts, outs, low_a, low_b, wgot, near2 = tie(gpts, outs, low_a, low_b, wgot, near2)

    got = [pull(outs[BLOCKS - k], dz=k) for k in (1, 2, 3)]
    a1, b3 = pull(low_a, dz=1), pull(low_b, dz=3)
    outs, mixed = tie(outs, mixed)
    mixed = fill_call(lambda i: 2 + i, halves_of(near[0]) + whole(*near2), mixed)
    got, mixed = tie(got, mixed)
    tail = core_sum(add4(outs[0], got))
    both = jnp.concatenate([tail, add4(wlow[:C].astype(F32), wgot)], 0).astype(BF)
    both, a1, b3 = tie(both, a1, b3)
    far2 = [pull(a1, dz=1), pull(b3, dz=3)]
    got = axis_peers(both, "dy")
    both, mixed = tie(both, mixed)
    mixed = fill_call(lambda i: 6 + i, halves_of(near[1]), mixed)
    got, mixed, far2 = tie(got, mixed, far2)
    both = add4(both.astype(F32), got)
    both, low_a, low_b = tie(both, low_a, low_b)
    b1, a3 = pull(low_b, dz=1), pull(low_a, dz=3)
    tail, wsum = both[:TAIL].astype(BF), both[TAIL:]
    if pts_size > 1:
        other = pull(wsum, dc=1)
    else:
        other = wlow[C:].astype(F32)
    wsum, other, tail = tie(wsum, other, tail)
    got = axis_peers(tail, "dx")
    tail, gpts = tie(tail, gpts)
    gpts = fill_call(
        lambda i: 2 + i + jnp.minimum(i, 1) + i // 3, whole(a1, *far2, b3), gpts
    )
    got, gpts, b1, a3 = tie(got, gpts, b1, a3)
    shapes = [(64, C), (32, 64), (1, GH), (32, 32), (32, 32), (32, 32)]
    shapes += [(64, C), (C, C), (C, C), (1, C), (1, C)]
    result = pl.pallas_call(
        finish_kernel,
        grid_spec=grid(
            (2,),
            [full((half, C))] * 2 + [any_spec] + [full((TAIL, C))] * 4 + [full((C, C))] * 2,
            [fill_out(lambda i: 3 + 3 * i)] + [full(s) for s in shapes],
        ),
        out_shape=[shape_of((rows, C), F32)] + [shape_of(s, F32) for s in shapes],
        input_output_aliases={3: 0},
        compiler_params=params,
        cost_estimate=cost(4),
        name="finish",
    )(z, b1, a3, gpts, tail, *got, wsum, other)
    gpts, gin, gslice, gsharp, gq, gk, gv, gout, gup, gdown, g1, g2 = result
    return (
        mixed, gpts, gin.T, gslice, gsharp.reshape(GH), gq, gk, gv, gout, gup, gdown,
        g1.reshape(C), g2.reshape(C),
    )


def solution(mesh):
    row, none, cols, heads = P("pts", None), P(), P(None, "head"), P("head")
    down = P("head", None)
    placed = (row, row, none, cols, none, heads, none, none, none, down, none, cols, down)
    given = (row, row, cols, none, heads, none, none, none, down, cols, down, none, none)
    return jax.shard_map(
        functools.partial(local, mesh.shape["pts"]),
        mesh=mesh,
        in_specs=placed,
        out_specs=given,
        check_vma=False,
    )
```

profile of v0, /device:TPU:2, one launch (start us, length us, event | category | flops | bytes accessed | tf_op | source)
XLA Modules:
  0.0 188.8 jit_solution(6336769797176020822)
XLA Ops:
  1.8 2.1 %prep.1 = (bf16[656,256]{1,0:T(8,128)(2,1)}, bf16[512,256]{1,0:T(8,128)(2,1)}, bf16[256,512]{1,0:T(8,128)(2,1)}, f32[1,256]{1,0:T(1,128)}, f32[1,256]{1,0:T(1,128)}) custom-call(bf16[256,256]{1,0:T(8,128)(2,1)} %w_up.1, bf16[256,256]{1,0:T(8,128)(2,1)} %w_down.1, bf16[64,256]{1,0:T(8,128)(2,1)} %bitcast.7, bf16[64,256]{1,0:T(8,128)(2,1)} %w_out.1, ...), custom_call_target="tpu_custom_call" | custom-call | flops 2000000 | bytes 1024 | tf_op jit(solution)/shard_map/prep/pallas_call | solution.py:511
  3.9 4.0 %collective-permute-start.4 = (bf16[656,256]{1,0:T(8,128)(2,1)}, bf16[656,256]{1,0:T(8,128)(2,1)S(1)}, u32[]{:S(2)}, u32[]{:S(2)}) collective-permute-start(bf16[656,256]{1,0:T(8,128)(2,1)} %get-tuple-element.131.w_in.sharp.in0.s0.refs_5_.refs_9_.refs_13_.refs_11_.refs_15_), channel_id=1, source_target_pairs={{1,0},{2,1},{3,2},{0,3},{5,4},{6,5},{7,6},{4,7},{9,8},{10,9},{11,1... | collective-permute-start | bytes 1007624 | tf_op jit(solution)/shard_map/ppermute | solution.py:461
  9.2 8.9 %own_sums.1 = f32[40,128]{1,0:T(8,128)} custom-call(bf16[8192,256]{1,0:T(8,128)(2,1)} %pts.7, f32[1,256]{1,0:T(1,128)} %get-tuple-element.128.gain.refs_8_, bf16[656,256]{1,0:T(8,128)(2,1)} %get-tuple-element.131.w_in.sharp.in0.s0.refs_5_.refs_9_.refs_13_.refs_11_.refs_15_, bf16[512,256]{1,0:T(8,128)(2,1)} %get-tuple-element.130.spread_slices.refs_9_, ...), custom_call_target="tpu_custom_call" | custom-call | flops 8000000 | bytes 1024 | tf_op jit(solution)/shard_map/own_sums/pallas_call | solution.py:525
  18.1 1.4 collective-permute-done
  20.8 2.4 %collective-permute-start.2 = (f32[40,128]{1,0:T(8,128)S(1)}, f32[40,128]{1,0:T(8,128)S(1)}, u32[]{:S(2)}, u32[]{:S(2)}) collective-permute-start(f32[40,128]{1,0:T(8,128)S(1)} %add.83), channel_id=1, source_target_pairs={{64,0},{65,1},{66,2},{67,3},{68,4},{69,5},{70,6},{71,7},{72,8},{73... | collective-permute-start | bytes 61448 | tf_op jit(solution)/shard_map/ppermute | solution.py:461
  23.2 1.8 collective-permute-start.3
  27.1 5.6 %weights.1 = (bf16[512,2048]{1,0:T(8,128)(2,1)}, bf16[2048,256]{1,0:T(8,128)(2,1)}) custom-call(s32[2]{0:T(128)} %pad_add_fusion.z, bf16[8192,256]{1,0:T(8,128)(2,1)} %pts.7, f32[1,256]{1,0:T(1,128)} %get-tuple-element.128.gain.refs_8_, bf16[656,256]{1,0:T(8,128)(2,1)} %get-tuple-element.131.w_in.sharp.in0.s0.refs_5_.refs_9_.refs_13_.refs_11_.refs_15_, ...), custom_call_target="tpu_custom_call" | custom-call | flops 5000000 | bytes 1024 | tf_op jit(solution)/shard_map/weights/pallas_call | solution.py:546
  32.8 3.1 %collective-permute-start.7 = (f32[40,128]{1,0:T(8,128)S(1)}, f32[40,128]{1,0:T(8,128)S(1)}, u32[]{:S(2)}, u32[]{:S(2)}) collective-permute-start(f32[40,128]{1,0:T(8,128)S(1)} %add_add_fusion.3.a), channel_id=1, source_target_pairs={{8,0},{9,1},{10,2},{11,3},{12,4},{13,5},{14,6},{15,7},{16,8},{17,9... | collective-permute-start | bytes 61448 | tf_op jit(solution)/shard_map/ppermute | solution.py:461
  37.5 3.7 %collective-permute-done.8.c = f32[40,128]{1,0:T(8,128)S(1)} collective-permute-done((f32[40,128]{1,0:T(8,128)S(1)}, f32[40,128]{1,0:T(8,128)S(1)}, u32[]{:S(2)}, u32[]{:S(2)}) %collective-permute-start.8) | collective-permute-done | bytes 20512 | tf_op jit(solution)/shard_map/ppermute | solution.py:461
  42.3 2.6 %tokens.1 = (f32[40,128]{1,0:T(8,128)}, f32[32,128]{1,0:T(8,128)}) custom-call(f32[40,128]{1,0:T(8,128)} %copy-done.20, f32[40,128]{1,0:T(8,128)} %copy-done.28, f32[40,128]{1,0:T(8,128)} %copy-done.29, f32[40,128]{1,0:T(8,128)} %copy-done.30, bf16[32,32]{1,0:T(8,128)(2,1)} %wq.3, bf16[32,32]{1,0:T(8,128)(2,1)} %wk.3, bf16[32,32]{1,0:T(8,128)(2,1)} %wv.3), custom_call_target="tpu_custom_call" | custom-call | flops 3000000 | bytes 1024 | tf_op jit(solution)/shard_map/tokens/pallas_call | solution.py:674
  44.9 2.7 %collective-permute-start.10 = (f32[32,128]{1,0:T(8,128)}, f32[32,128]{1,0:T(8,128)S(1)}, u32[]{:S(2)}, u32[]{:S(2)}) collective-permute-start(f32[32,128]{1,0:T(8,128)} %get-tuple-element.139.refs_0_), channel_id=1, source_target_pairs={{1,0},{2,1},{3,2},{0,3},{5,4},{6,5},{7,6},{4,7},{9,8},{10,9},{11,1... | collective-permute-start | bytes 49160 | tf_op jit(solution)/shard_map/ppermute | solution.py:461
  47.6 1.6 collective-permute-start.11
  49.2 3.8 %collective-permute-done.11.refs_2_ = f32[32,128]{1,0:T(8,128)S(1)} collective-permute-done((f32[32,128]{1,0:T(8,128)}, f32[32,128]{1,0:T(8,128)S(1)}, u32[]{:S(2)}, u32[]{:S(2)}) %collective-permute-start.11) | collective-permute-done | bytes 16416 | tf_op jit(solution)/shard_map/ppermute | solution.py:461
  53.0 1.4 collective-permute-done.12.refs_3_
  55.0 16.9 %mlp.1 = (f32[8192,256]{1,0:T(8,128)}, bf16[2048,256]{1,0:T(8,128)(2,1)}, bf16[2048,256]{1,0:T(8,128)(2,1)}, bf16[2048,256]{1,0:T(8,128)(2,1)}, f32[32,128]{1,0:...) custom-call(s32[2]{0:T(128)} %pad_add_fusion.z, ...), custom_call_target="tpu_custom_call" | custom-call | flops 16000000 | bytes 1024 | tf_op jit(solution)/shard_map/mlp/pallas_call | solution.py:572
  72.0 2.0 %collective-permute-start.15 = (f32[32,128]{1,0:T(8,128)}, f32[32,128]{1,0:T(8,128)S(1)}, u32[]{:S(2)}, u32[]{:S(2)}) collective-permute-start(f32[32,128]{1,0:T(8,128)} %get-tuple-element.147), channel_id=1, source_target_pairs={{3,0},{0,1},{1,2},{2,3},{7,4},{4,5},{5,6},{6,7},{11,8},{8,9},{9,10... | collective-permute-start | bytes 49160 | tf_op jit(solution)/shard_map/ppermute | solution.py:461
  74.7 2.0 %collective-permute-start.20 = (bf16[512,256]{1,0:T(8,128)(2,1)}, bf16[512,256]{1,0:T(8,128)(2,1)S(1)}, u32[]{:S(2)}, u32[]{:S(2)}) collective-permute-start(bf16[512,256]{1,0:T(8,128)(2,1)} %get-tuple-element.150), channel_id=1, source_target_pairs={{1,0},{2,1},{3,2},{0,3},{5,4},{6,5},{7,6},{4,7},{9,8},{10,9},{11,1... | collective-permute-start | bytes 786440 | tf_op jit(solution)/shard_map/ppermute | solution.py:461
  76.7 1.5 collective-permute-start.21
  78.2 1.5 collective-permute-done.15
  83.3 2.2 %collective-permute-done.17 = f32[32,128]{1,0:T(8,128)S(1)} collective-permute-done((f32[32,128]{1,0:T(8,128)S(1)}, f32[32,128]{1,0:T(8,128)S(1)}, u32[]{:S(2)}, u32[]{:S(2)}) %collective-permute-start.17) | collective-permute-done | bytes 16416 | tf_op jit(solution)/shard_map/ppermute | solution.py:461
  85.8 1.5 collective-permute-done.18
  87.2 2.0 %collective-permute-done.19 = f32[32,128]{1,0:T(8,128)S(1)} collective-permute-done((f32[32,128]{1,0:T(8,128)S(1)}, f32[32,128]{1,0:T(8,128)S(1)}, u32[]{:S(2)}, u32[]{:S(2)}) %collective-permute-start.19) | collective-permute-done | bytes 16416 | tf_op jit(solution)/shard_map/ppermute | solution.py:461
  89.3 3.2 %collective-permute-start.30 = (bf16[2048,256]{1,0:T(8,128)(2,1)}, bf16[2048,256]{1,0:T(8,128)(2,1)S(1)}, u32[]{:S(2)}, u32[]{:S(2)}) collective-permute-start(bf16[2048,256]{1,0:T(8,128)(2,1)} %get-tuple-element.169), channel_id=1, source_target_pairs={{1,0},{2,1},{3,2},{0,3},{5,4},{6,5},{7,6},{4,7},{9,8},{10,9},{11,1... | collective-permute-start | bytes 3145736 | tf_op jit(solution)/shard_map/ppermute | solution.py:461
  96.5 2.0 %collective-permute-done.24.c = f32[32,128]{1,0:T(8,128)S(1)} collective-permute-done((f32[32,128]{1,0:T(8,128)S(1)}, f32[32,128]{1,0:T(8,128)S(1)}, u32[]{:S(2)}, u32[]{:S(2)}) %collective-permute-start.24) | collective-permute-done | bytes 16416 | tf_op jit(solution)/shard_map/ppermute | solution.py:461
  99.6 3.8 %tokens_back.1 = (f32[40,128]{1,0:T(8,128)}, f32[32,128]{1,0:T(8,128)}) custom-call(f32[40,128]{1,0:T(8,128)} %get-tuple-element.143.nd, f32[32,128]{1,0:T(8,128)} %copy-done.24, f32[32,128]{1,0:T(8,128)} %copy-done.31, f32[32,128]{1,0:T(8,128)} %copy-done.32, f32[32,128]{1,0:T(8,128)} %copy-done.33, bf16[32,32]{1,0:T(8,128)(2,1)} %wq.3, bf16[32,32]{1,0:T(8,128)(2,1)} %wk.3, ...), custom_call_target="tpu_custom_call" | custom-call | flops 4000000 | bytes 1024 | tf_op jit(solution)/shard_map/tokens_back/pallas_call | solution.py:701
  103.4 3.2 %collective-permute-start.26 = (f32[40,128]{1,0:T(8,128)}, f32[40,128]{1,0:T(8,128)S(1)}, u32[]{:S(2)}, u32[]{:S(2)}) collective-permute-start(f32[40,128]{1,0:T(8,128)} %get-tuple-element.163.refs_4_), channel_id=1, source_target_pairs={{1,0},{2,1},{3,2},{0,3},{5,4},{6,5},{7,6},{4,7},{9,8},{10,9},{11,1... | collective-permute-start | bytes 61448 | tf_op jit(solution)/shard_map/ppermute | solution.py:461
  107.6 6.9 %collective-permute-done.26.refs_5_ = f32[40,128]{1,0:T(8,128)S(1)} collective-permute-done((f32[40,128]{1,0:T(8,128)}, f32[40,128]{1,0:T(8,128)S(1)}, u32[]{:S(2)}, u32[]{:S(2)}) %collective-permute-start.26) | collective-permute-done | bytes 20512 | tf_op jit(solution)/shard_map/ppermute | solution.py:461
  114.5 1.9 collective-permute-done.27.refs_6_
  116.4 1.5 collective-permute-done.28.refs_7_
  118.4 1.8 collective-permute-start.36
  120.2 2.1 %collective-permute-start.32 = (bf16[256,256]{1,0:T(8,128)(2,1)S(1)}, bf16[256,256]{1,0:T(8,128)(2,1)S(1)}, u32[]{:S(2)}, u32[]{:S(2)}) collective-permute-start(bf16[256,256]{1,0:T(8,128)(2,1)S(1)} %fusion.1), channel_id=1, source_target_pairs={{32,0},{33,1},{34,2},{35,3},{36,4},{37,5},{38,6},{39,7},{40,8},{41... | collective-permute-start | bytes 393224 | tf_op jit(solution)/shard_map/ppermute | solution.py:461
  122.3 2.6 %collective-permute-start.34 = (bf16[256,256]{1,0:T(8,128)(2,1)S(1)}, bf16[256,256]{1,0:T(8,128)(2,1)S(1)}, u32[]{:S(2)}, u32[]{:S(2)}) collective-permute-start(bf16[256,256]{1,0:T(8,128)(2,1)S(1)} %fusion.1), channel_id=1, source_target_pairs={{96,0},{97,1},{98,2},{99,3},{100,4},{101,5},{102,6},{103,7},{104,8... | collective-permute-start | bytes 393224 | tf_op jit(solution)/shard_map/ppermute | solution.py:461
  124.9 13.6 %points.1 = (f32[8192,256]{1,0:T(8,128)}, bf16[1024,256]{1,0:T(8,128)(2,1)}, bf16[1024,256]{1,0:T(8,128)(2,1)}, f32[168,256]{1,0:T(8,128)}, bf16[168,256]{1,0:T(...) custom-call(s32[2]{0:T(128)} %pad_add_fusion.z, bf16[8192,256]{1,0:T(8,128)(2,1)} %pts.7, ...), custom_call_target="tpu_custom_call" | custom-call | flops 12000000 | bytes 1024 | tf_op jit(solution)/shard_map/points/pallas_call | solution.py:604
  138.6 1.6 collective-permute-start.37
  141.1 2.9 %collective-permute-start.41 = (bf16[1024,256]{1,0:T(8,128)(2,1)}, bf16[1024,256]{1,0:T(8,128)(2,1)S(1)}, u32[]{:S(2)}, u32[]{:S(2)}) collective-permute-start(bf16[1024,256]{1,0:T(8,128)(2,1)} %get-tuple-element.221), channel_id=1, source_target_pairs={{1,0},{2,1},{3,2},{0,3},{5,4},{6,5},{7,6},{4,7},{9,8},{10,9},{11,1... | collective-permute-start | bytes 1572872 | tf_op jit(solution)/shard_map/ppermute | solution.py:461
  144.1 4.7 %fill.3.refs_2_ = f32[8192,256]{1,0:T(8,128)} custom-call(s32[2]{0:T(128)} %pad_add_fusion.z, bf16[2048,256]{1,0:T(8,128)(2,1)} %copy-done.3, bf16[2048,256]{1,0:T(8,128)(2,1)} %copy-done.3, bf16[1024,256]{1,0:T(8,128)(2,1)} %copy-done.8, bf16[1024,256]{1,0:T(8,128)(2,1)} %copy-done.9, ...), custom_call_target="tpu_custom_call", output_to_operand_aliasing={{}: (5, {})} | custom-call | flops 3000000 | bytes 1024 | tf_op jit(solution)/shard_map/fill/pallas_call | solution.py:651
  150.4 1.9 %collective-permute-done.41.refs_0_ = bf16[1024,256]{1,0:T(8,128)(2,1)S(1)} collective-permute-done((bf16[1024,256]{1,0:T(8,128)(2,1)}, bf16[1024,256]{1,0:T(8,128)(2,1)S(1)}, u32[]{:S(2)}, u32[]{:S(2)}) %collective-permute-start.41) | collective-permute-done | bytes 524320 | tf_op jit(solution)/shard_map/ppermute | solution.py:461
  152.3 3.0 %collective-permute-done.42.refs_3_ = bf16[1024,256]{1,0:T(8,128)(2,1)S(1)} collective-permute-done((bf16[1024,256]{1,0:T(8,128)(2,1)}, bf16[1024,256]{1,0:T(8,128)(2,1)S(1)}, u32[]{:S(2)}, u32[]{:S(2)}) %collective-permute-start.42) | collective-permute-done | bytes 524320 | tf_op jit(solution)/shard_map/ppermute | solution.py:461
  155.7 1.7 collective-permute-start.47
  160.2 3.3 %fill.4 = f32[8192,256]{1,0:T(8,128)} custom-call(s32[2]{0:T(128)} %pad_add_fusion.z, bf16[2048,256]{1,0:T(8,128)(2,1)} %copy-done.4, bf16[2048,256]{1,0:T(8,128)(2,1)} %copy-done.4, f32[8192,256]{1,0:T(8,128)} %fill.3.refs_2_), custom_call_target="tpu_custom_call", output_to_operand_aliasing={{}: (3, {})} | custom-call | flops 3000000 | bytes 1024 | tf_op jit(solution)/shard_map/fill/pallas_call | solution.py:651
  163.5 2.1 %collective-permute-done.44 = bf16[424,256]{1,0:T(8,128)(2,1)S(1)} collective-permute-done((bf16[424,256]{1,0:T(8,128)(2,1)S(1)}, bf16[424,256]{1,0:T(8,128)(2,1)S(1)}, u32[]{:S(2)}, u32[]{:S(2)}) %collective-permute-start.44) | collective-permute-done | bytes 217120 | tf_op jit(solution)/shard_map/ppermute | solution.py:461
  165.6 2.2 %collective-permute-done.45 = bf16[424,256]{1,0:T(8,128)(2,1)S(1)} collective-permute-done((bf16[424,256]{1,0:T(8,128)(2,1)S(1)}, bf16[424,256]{1,0:T(8,128)(2,1)S(1)}, u32[]{:S(2)}, u32[]{:S(2)}) %collective-permute-start.45) | collective-permute-done | bytes 217120 | tf_op jit(solution)/shard_map/ppermute | solution.py:461
  168.7 1.9 collective-permute-start.52
  171.0 1.5 collective-permute-done.48.w1
  172.5 2.9 %collective-permute-start.50 = (bf16[168,256]{1,0:T(8,128)(2,1)S(1)}, bf16[168,256]{1,0:T(8,128)(2,1)S(1)}, u32[]{:S(2)}, u32[]{:S(2)}) collective-permute-start(bf16[168,256]{1,0:T(8,128)(2,1)S(1)} %slice.19.t0), channel_id=1, source_target_pairs={{64,0},{65,1},{66,2},{67,3},{68,4},{69,5},{70,6},{71,7},{72,8},{73... | collective-permute-start | bytes 258056 | tf_op jit(solution)/shard_map/ppermute | solution.py:461
  176.6 4.7 %fill.5.before = f32[8192,256]{1,0:T(8,128)} custom-call(s32[2]{0:T(128)} %pad_add_fusion.z, bf16[1024,256]{1,0:T(8,128)(2,1)} %copy-done.6, bf16[1024,256]{1,0:T(8,128)(2,1)} %copy-done.10, bf16[1024,256]{1,0:T(8,128)(2,1)} %copy-done.11, bf16[1024,256]{1,0:T(8,128)(2,1)} %copy-done.7, ...), custom_call_target="tpu_custom_call", output_to_operand_aliasing={{}: (5, {})} | custom-call | flops 3000000 | bytes 1024 | tf_op jit(solution)/shard_map/fill/pallas_call | solution.py:651
  181.4 2.4 %collective-permute-done.53.second = bf16[1024,256]{1,0:T(8,128)(2,1)S(1)} collective-permute-done((bf16[1024,256]{1,0:T(8,128)(2,1)S(1)}, bf16[1024,256]{1,0:T(8,128)(2,1)S(1)}, u32[]{:S(2)}, u32[]{:S(2)}) %collective-permute-start.53) | collective-permute-done | bytes 524320 | tf_op jit(solution)/shard_map/ppermute | solution.py:461
  184.6 4.0 %finish.1 = (f32[8192,256]{1,0:T(8,128)}, f32[64,256]{1,0:T(8,128)}, f32[32,64]{1,0:T(8,128)}, f32[1,2]{1,0:T(1,128)}, f32[32,32]{1,0:T(8,128)}, /*index=5*/f32[...) custom-call(s32[2]{0:T(128)} %pad_add_fusion.z, ...), custom_call_target="tpu_custom_call", output_to_operand_aliasing={{0}: (3, {})} | custom-call | flops 4000000 | bytes 1024 | tf_op jit(solution)/shard_map/finish/pallas_call | solution.py:753
  (161 shorter events, 29.3 us)
Async XLA Ops:
  3.9 19.3 %collective-permute-start.4 = (bf16[656,256]{1,0:T(8,128)(2,1)}, bf16[656,256]{1,0:T(8,128)(2,1)S(1)}, u32[]{:S(2)}, u32[]{:S(2)}) collective-permute-start(bf16[656,256]{1,0:T(8,128)(2,1)} %get-tuple-element.131.w_in.sharp.in0.s0.refs_5_.refs_9_.refs_13_.refs_11_.refs_15_), channel_id=1, source_target_pairs={{1,0},{2,1},{3,2},{0,3},{5,4},{6,5},{7,6},{4,7},{9,8},{10,9},{11,1... | collective-permute-start | bytes 1007624 | tf_op jit(solution)/shard_map/ppermute | solution.py:461
  7.9 17.7 %collective-permute-start.5 = (bf16[656,256]{1,0:T(8,128)(2,1)}, bf16[656,256]{1,0:T(8,128)(2,1)S(1)}, u32[]{:S(2)}, u32[]{:S(2)}) collective-permute-start(bf16[656,256]{1,0:T(8,128)(2,1)} %get-tuple-element.131.w_in.sharp.in0.s0.refs_5_.refs_9_.refs_13_.refs_11_.refs_15_), channel_id=1, source_target_pairs={{2,0},{3,1},{0,2},{1,3},{6,4},{7,5},{4,6},{5,7},{10,8},{11,9},{8,1... | collective-permute-start | bytes 1007624 | tf_op jit(solution)/shard_map/ppermute | solution.py:461
  7.9 18.0 %collective-permute-start.6 = (bf16[656,256]{1,0:T(8,128)(2,1)}, bf16[656,256]{1,0:T(8,128)(2,1)S(1)}, u32[]{:S(2)}, u32[]{:S(2)}) collective-permute-start(bf16[656,256]{1,0:T(8,128)(2,1)} %get-tuple-element.131.w_in.sharp.in0.s0.refs_5_.refs_9_.refs_13_.refs_11_.refs_15_), channel_id=1, source_target_pairs={{3,0},{0,1},{1,2},{2,3},{7,4},{4,5},{5,6},{6,7},{11,8},{8,9},{9,10... | collective-permute-start | bytes 1007624 | tf_op jit(solution)/shard_map/ppermute | solution.py:461
  20.2 12.5 %collective-permute-start.1 = (f32[40,128]{1,0:T(8,128)S(1)}, f32[40,128]{1,0:T(8,128)S(1)}, u32[]{:S(2)}, u32[]{:S(2)}) collective-permute-start(f32[40,128]{1,0:T(8,128)S(1)} %add.83), channel_id=1, source_target_pairs={{32,0},{33,1},{34,2},{35,3},{36,4},{37,5},{38,6},{39,7},{40,8},{41... | collective-permute-start | bytes 61448 | tf_op jit(solution)/shard_map/ppermute | solution.py:461
  20.8 11.9 %collective-permute-start.2 = (f32[40,128]{1,0:T(8,128)S(1)}, f32[40,128]{1,0:T(8,128)S(1)}, u32[]{:S(2)}, u32[]{:S(2)}) collective-permute-start(f32[40,128]{1,0:T(8,128)S(1)} %add.83), channel_id=1, source_target_pairs={{64,0},{65,1},{66,2},{67,3},{68,4},{69,5},{70,6},{71,7},{72,8},{73... | collective-permute-start | bytes 61448 | tf_op jit(solution)/shard_map/ppermute | solution.py:461
  23.2 9.5 %collective-permute-start.3 = (f32[40,128]{1,0:T(8,128)S(1)}, f32[40,128]{1,0:T(8,128)S(1)}, u32[]{:S(2)}, u32[]{:S(2)}) collective-permute-start(f32[40,128]{1,0:T(8,128)S(1)} %add.83), channel_id=1, source_target_pairs={{96,0},{97,1},{98,2},{99,3},{100,4},{101,5},{102,6},{103,7},{104,8... | collective-permute-start | bytes 61448 | tf_op jit(solution)/shard_map/ppermute | solution.py:461
  32.8 4.7 %collective-permute-start.7 = (f32[40,128]{1,0:T(8,128)S(1)}, f32[40,128]{1,0:T(8,128)S(1)}, u32[]{:S(2)}, u32[]{:S(2)}) collective-permute-start(f32[40,128]{1,0:T(8,128)S(1)} %add_add_fusion.3.a), channel_id=1, source_target_pairs={{8,0},{9,1},{10,2},{11,3},{12,4},{13,5},{14,6},{15,7},{16,8},{17,9... | collective-permute-start | bytes 61448 | tf_op jit(solution)/shard_map/ppermute | solution.py:461
  35.8 5.3 %collective-permute-start.8 = (f32[40,128]{1,0:T(8,128)S(1)}, f32[40,128]{1,0:T(8,128)S(1)}, u32[]{:S(2)}, u32[]{:S(2)}) collective-permute-start(f32[40,128]{1,0:T(8,128)S(1)} %add_add_fusion.3.a), channel_id=1, source_target_pairs={{16,0},{17,1},{18,2},{19,3},{20,4},{21,5},{22,6},{23,7},{24,8},{25... | collective-permute-start | bytes 61448 | tf_op jit(solution)/shard_map/ppermute | solution.py:461
  36.5 5.0 %collective-permute-start.9 = (f32[40,128]{1,0:T(8,128)S(1)}, f32[40,128]{1,0:T(8,128)S(1)}, u32[]{:S(2)}, u32[]{:S(2)}) collective-permute-start(f32[40,128]{1,0:T(8,128)S(1)} %add_add_fusion.3.a), channel_id=1, source_target_pairs={{24,0},{25,1},{26,2},{27,3},{28,4},{29,5},{30,6},{31,7},{0,8},{1,9... | collective-permute-start | bytes 61448 | tf_op jit(solution)/shard_map/ppermute | solution.py:461
  44.9 4.3 %collective-permute-start.10 = (f32[32,128]{1,0:T(8,128)}, f32[32,128]{1,0:T(8,128)S(1)}, u32[]{:S(2)}, u32[]{:S(2)}) collective-permute-start(f32[32,128]{1,0:T(8,128)} %get-tuple-element.139.refs_0_), channel_id=1, source_target_pairs={{1,0},{2,1},{3,2},{0,3},{5,4},{6,5},{7,6},{4,7},{9,8},{10,9},{11,1... | collective-permute-start | bytes 49160 | tf_op jit(solution)/shard_map/ppermute | solution.py:461
  47.6 5.5 %collective-permute-start.11 = (f32[32,128]{1,0:T(8,128)}, f32[32,128]{1,0:T(8,128)S(1)}, u32[]{:S(2)}, u32[]{:S(2)}) collective-permute-start(f32[32,128]{1,0:T(8,128)} %get-tuple-element.139.refs_0_), channel_id=1, source_target_pairs={{2,0},{3,1},{0,2},{1,3},{6,4},{7,5},{4,6},{5,7},{10,8},{11,9},{8,1... | collective-permute-start | bytes 49160 | tf_op jit(solution)/shard_map/ppermute | solution.py:461
  49.2 5.2 %collective-permute-start.12 = (f32[32,128]{1,0:T(8,128)}, f32[32,128]{1,0:T(8,128)S(1)}, u32[]{:S(2)}, u32[]{:S(2)}) collective-permute-start(f32[32,128]{1,0:T(8,128)} %get-tuple-element.139.refs_0_), channel_id=1, source_target_pairs={{3,0},{0,1},{1,2},{2,3},{7,4},{4,5},{5,6},{6,7},{11,8},{8,9},{9,10... | collective-permute-start | bytes 49160 | tf_op jit(solution)/shard_map/ppermute | solution.py:461
  71.9 6.3 %collective-permute-start.14 = (f32[32,128]{1,0:T(8,128)}, f32[32,128]{1,0:T(8,128)S(1)}, u32[]{:S(2)}, u32[]{:S(2)}) collective-permute-start(f32[32,128]{1,0:T(8,128)} %get-tuple-element.146), channel_id=1, source_target_pairs={{1,0},{2,1},{3,2},{0,3},{5,4},{6,5},{7,6},{4,7},{9,8},{10,9},{11,1... | collective-permute-start | bytes 49160 | tf_op jit(solution)/shard_map/ppermute | solution.py:461
  72.0 7.8 %collective-permute-start.15 = (f32[32,128]{1,0:T(8,128)}, f32[32,128]{1,0:T(8,128)S(1)}, u32[]{:S(2)}, u32[]{:S(2)}) collective-permute-start(f32[32,128]{1,0:T(8,128)} %get-tuple-element.147), channel_id=1, source_target_pairs={{3,0},{0,1},{1,2},{2,3},{7,4},{4,5},{5,6},{6,7},{11,8},{8,9},{9,10... | collective-permute-start | bytes 49160 | tf_op jit(solution)/shard_map/ppermute | solution.py:461
  74.0 5.8 %collective-permute-start.13 = (f32[32,128]{1,0:T(8,128)}, f32[32,128]{1,0:T(8,128)S(1)}, u32[]{:S(2)}, u32[]{:S(2)}) collective-permute-start(f32[32,128]{1,0:T(8,128)} %get-tuple-element.145), channel_id=1, source_target_pairs={{2,0},{3,1},{0,2},{1,3},{6,4},{7,5},{4,6},{5,7},{10,8},{11,9},{8,1... | collective-permute-start | bytes 49160 | tf_op jit(solution)/shard_map/ppermute | solution.py:461
  74.7 14.6 %collective-permute-start.20 = (bf16[512,256]{1,0:T(8,128)(2,1)}, bf16[512,256]{1,0:T(8,128)(2,1)S(1)}, u32[]{:S(2)}, u32[]{:S(2)}) collective-permute-start(bf16[512,256]{1,0:T(8,128)(2,1)} %get-tuple-element.150), channel_id=1, source_target_pairs={{1,0},{2,1},{3,2},{0,3},{5,4},{6,5},{7,6},{4,7},{9,8},{10,9},{11,1... | collective-permute-start | bytes 786440 | tf_op jit(solution)/shard_map/ppermute | solution.py:461
  76.7 12.6 %collective-permute-start.21 = (bf16[512,256]{1,0:T(8,128)(2,1)}, bf16[512,256]{1,0:T(8,128)(2,1)S(1)}, u32[]{:S(2)}, u32[]{:S(2)}) collective-permute-start(bf16[512,256]{1,0:T(8,128)(2,1)} %get-tuple-element.151), channel_id=1, source_target_pairs={{2,0},{3,1},{0,2},{1,3},{6,4},{7,5},{4,6},{5,7},{10,8},{11,9},{8,1... | collective-permute-start | bytes 786440 | tf_op jit(solution)/shard_map/ppermute | solution.py:461
  80.5 8.8 %collective-permute-start.22 = (bf16[512,256]{1,0:T(8,128)(2,1)}, bf16[512,256]{1,0:T(8,128)(2,1)S(1)}, u32[]{:S(2)}, u32[]{:S(2)}) collective-permute-start(bf16[512,256]{1,0:T(8,128)(2,1)} %get-tuple-element.152), channel_id=1, source_target_pairs={{3,0},{0,1},{1,2},{2,3},{7,4},{4,5},{5,6},{6,7},{11,8},{8,9},{9,10... | collective-permute-start | bytes 786440 | tf_op jit(solution)/shard_map/ppermute | solution.py:461
  81.8 3.7 %collective-permute-start.17 = (f32[32,128]{1,0:T(8,128)S(1)}, f32[32,128]{1,0:T(8,128)S(1)}, u32[]{:S(2)}, u32[]{:S(2)}) collective-permute-start(f32[32,128]{1,0:T(8,128)S(1)} %add.90), channel_id=1, source_target_pairs={{32,0},{33,1},{34,2},{35,3},{36,4},{37,5},{38,6},{39,7},{40,8},{41... | collective-permute-start | bytes 49160 | tf_op jit(solution)/shard_map/ppermute | solution.py:461
  82.0 5.2 %collective-permute-start.18 = (f32[32,128]{1,0:T(8,128)S(1)}, f32[32,128]{1,0:T(8,128)S(1)}, u32[]{:S(2)}, u32[]{:S(2)}) collective-permute-start(f32[32,128]{1,0:T(8,128)S(1)} %add.90), channel_id=1, source_target_pairs={{64,0},{65,1},{66,2},{67,3},{68,4},{69,5},{70,6},{71,7},{72,8},{73... | collective-permute-start | bytes 49160 | tf_op jit(solution)/shard_map/ppermute | solution.py:461
  89.3 28.6 %collective-permute-start.30 = (bf16[2048,256]{1,0:T(8,128)(2,1)}, bf16[2048,256]{1,0:T(8,128)(2,1)S(1)}, u32[]{:S(2)}, u32[]{:S(2)}) collective-permute-start(bf16[2048,256]{1,0:T(8,128)(2,1)} %get-tuple-element.169), channel_id=1, source_target_pairs={{1,0},{2,1},{3,2},{0,3},{5,4},{6,5},{7,6},{4,7},{9,8},{10,9},{11,1... | collective-permute-start | bytes 3145736 | tf_op jit(solution)/shard_map/ppermute | solution.py:461
  92.5 25.4 %collective-permute-start.31 = (bf16[2048,256]{1,0:T(8,128)(2,1)}, bf16[2048,256]{1,0:T(8,128)(2,1)S(1)}, u32[]{:S(2)}, u32[]{:S(2)}) collective-permute-start(bf16[2048,256]{1,0:T(8,128)(2,1)} %get-tuple-element.169), channel_id=1, source_target_pairs={{3,0},{0,1},{1,2},{2,3},{7,4},{4,5},{5,6},{6,7},{11,8},{8,9},{9,10... | collective-permute-start | bytes 3145736 | tf_op jit(solution)/shard_map/ppermute | solution.py:461
  92.5 3.9 %collective-permute-start.23 = (f32[32,128]{1,0:T(8,128)S(1)}, f32[32,128]{1,0:T(8,128)S(1)}, u32[]{:S(2)}, u32[]{:S(2)}) collective-permute-start(f32[32,128]{1,0:T(8,128)S(1)} %add_add_fusion.4.a), channel_id=1, source_target_pairs={{8,0},{9,1},{10,2},{11,3},{12,4},{13,5},{14,6},{15,7},{16,8},{17,9... | collective-permute-start | bytes 49160 | tf_op jit(solution)/shard_map/ppermute | solution.py:461
  93.3 5.2 %collective-permute-start.24 = (f32[32,128]{1,0:T(8,128)S(1)}, f32[32,128]{1,0:T(8,128)S(1)}, u32[]{:S(2)}, u32[]{:S(2)}) collective-permute-start(f32[32,128]{1,0:T(8,128)S(1)} %add_add_fusion.4.a), channel_id=1, source_target_pairs={{16,0},{17,1},{18,2},{19,3},{20,4},{21,5},{22,6},{23,7},{24,8},{25... | collective-permute-start | bytes 49160 | tf_op jit(solution)/shard_map/ppermute | solution.py:461
  94.0 5.0 %collective-permute-start.25 = (f32[32,128]{1,0:T(8,128)S(1)}, f32[32,128]{1,0:T(8,128)S(1)}, u32[]{:S(2)}, u32[]{:S(2)}) collective-permute-start(f32[32,128]{1,0:T(8,128)S(1)} %add_add_fusion.4.a), channel_id=1, source_target_pairs={{24,0},{25,1},{26,2},{27,3},{28,4},{29,5},{30,6},{31,7},{0,8},{1,9... | collective-permute-start | bytes 49160 | tf_op jit(solution)/shard_map/ppermute | solution.py:461
  103.4 11.1 %collective-permute-start.26 = (f32[40,128]{1,0:T(8,128)}, f32[40,128]{1,0:T(8,128)S(1)}, u32[]{:S(2)}, u32[]{:S(2)}) collective-permute-start(f32[40,128]{1,0:T(8,128)} %get-tuple-element.163.refs_4_), channel_id=1, source_target_pairs={{1,0},{2,1},{3,2},{0,3},{5,4},{6,5},{7,6},{4,7},{9,8},{10,9},{11,1... | collective-permute-start | bytes 61448 | tf_op jit(solution)/shard_map/ppermute | solution.py:461
  106.6 9.8 %collective-permute-start.27 = (f32[40,128]{1,0:T(8,128)}, f32[40,128]{1,0:T(8,128)S(1)}, u32[]{:S(2)}, u32[]{:S(2)}) collective-permute-start(f32[40,128]{1,0:T(8,128)} %get-tuple-element.163.refs_4_), channel_id=1, source_target_pairs={{2,0},{3,1},{0,2},{1,3},{6,4},{7,5},{4,6},{5,7},{10,8},{11,9},{8,1... | collective-permute-start | bytes 61448 | tf_op jit(solution)/shard_map/ppermute | solution.py:461
  106.6 11.3 %collective-permute-start.28 = (f32[40,128]{1,0:T(8,128)}, f32[40,128]{1,0:T(8,128)S(1)}, u32[]{:S(2)}, u32[]{:S(2)}) collective-permute-start(f32[40,128]{1,0:T(8,128)} %get-tuple-element.163.refs_4_), channel_id=1, source_target_pairs={{3,0},{0,1},{1,2},{2,3},{7,4},{4,5},{5,6},{6,7},{11,8},{8,9},{9,10... | collective-permute-start | bytes 61448 | tf_op jit(solution)/shard_map/ppermute | solution.py:461
  118.0 20.5 %collective-permute-start.35 = (bf16[1024,256]{1,0:T(8,128)(2,1)S(1)}, bf16[1024,256]{1,0:T(8,128)(2,1)S(1)}, u32[]{:S(2)}, u32[]{:S(2)}) collective-permute-start(bf16[1024,256]{1,0:T(8,128)(2,1)S(1)} %slice.13), channel_id=1, source_target_pairs={{1,0},{2,1},{3,2},{0,3},{5,4},{6,5},{7,6},{4,7},{9,8},{10,9},{11,1... | collective-permute-start | bytes 1572872 | tf_op jit(solution)/shard_map/ppermute | solution.py:461
  118.4 20.1 %collective-permute-start.36 = (bf16[1024,256]{1,0:T(8,128)(2,1)S(1)}, bf16[1024,256]{1,0:T(8,128)(2,1)S(1)}, u32[]{:S(2)}, u32[]{:S(2)}) collective-permute-start(bf16[1024,256]{1,0:T(8,128)(2,1)S(1)} %slice.14), channel_id=1, source_target_pairs={{3,0},{0,1},{1,2},{2,3},{7,4},{4,5},{5,6},{6,7},{11,8},{8,9},{9,10... | collective-permute-start | bytes 1572872 | tf_op jit(solution)/shard_map/ppermute | solution.py:461
  120.2 18.3 %collective-permute-start.32 = (bf16[256,256]{1,0:T(8,128)(2,1)S(1)}, bf16[256,256]{1,0:T(8,128)(2,1)S(1)}, u32[]{:S(2)}, u32[]{:S(2)}) collective-permute-start(bf16[256,256]{1,0:T(8,128)(2,1)S(1)} %fusion.1), channel_id=1, source_target_pairs={{32,0},{33,1},{34,2},{35,3},{36,4},{37,5},{38,6},{39,7},{40,8},{41... | collective-permute-start | bytes 393224 | tf_op jit(solution)/shard_map/ppermute | solution.py:461
  122.3 16.3 %collective-permute-start.33 = (bf16[256,256]{1,0:T(8,128)(2,1)S(1)}, bf16[256,256]{1,0:T(8,128)(2,1)S(1)}, u32[]{:S(2)}, u32[]{:S(2)}) collective-permute-start(bf16[256,256]{1,0:T(8,128)(2,1)S(1)} %fusion.1), channel_id=1, source_target_pairs={{64,0},{65,1},{66,2},{67,3},{68,4},{69,5},{70,6},{71,7},{72,8},{73... | collective-permute-start | bytes 393224 | tf_op jit(solution)/shard_map/ppermute | solution.py:461
  122.3 16.2 %collective-permute-start.34 = (bf16[256,256]{1,0:T(8,128)(2,1)S(1)}, bf16[256,256]{1,0:T(8,128)(2,1)S(1)}, u32[]{:S(2)}, u32[]{:S(2)}) collective-permute-start(bf16[256,256]{1,0:T(8,128)(2,1)S(1)} %fusion.1), channel_id=1, source_target_pairs={{96,0},{97,1},{98,2},{99,3},{100,4},{101,5},{102,6},{103,7},{104,8... | collective-permute-start | bytes 393224 | tf_op jit(solution)/shard_map/ppermute | solution.py:461
  138.6 10.1 %collective-permute-start.37 = (bf16[168,256]{1,0:T(8,128)(2,1)}, bf16[168,256]{1,0:T(8,128)(2,1)S(1)}, u32[]{:S(2)}, u32[]{:S(2)}) collective-permute-start(bf16[168,256]{1,0:T(8,128)(2,1)} %get-tuple-element.190), channel_id=1, source_target_pairs={{1,0},{2,1},{3,2},{0,3},{5,4},{6,5},{7,6},{4,7},{9,8},{10,9},{11,1... | collective-permute-start | bytes 258056 | tf_op jit(solution)/shard_map/ppermute | solution.py:461
  140.2 8.6 %collective-permute-start.38 = (bf16[168,256]{1,0:T(8,128)(2,1)}, bf16[168,256]{1,0:T(8,128)(2,1)S(1)}, u32[]{:S(2)}, u32[]{:S(2)}) collective-permute-start(bf16[168,256]{1,0:T(8,128)(2,1)} %get-tuple-element.189), channel_id=1, source_target_pairs={{2,0},{3,1},{0,2},{1,3},{6,4},{7,5},{4,6},{5,7},{10,8},{11,9},{8,1... | collective-permute-start | bytes 258056 | tf_op jit(solution)/shard_map/ppermute | solution.py:461
  140.8 7.9 %collective-permute-start.39 = (bf16[168,256]{1,0:T(8,128)(2,1)}, bf16[168,256]{1,0:T(8,128)(2,1)S(1)}, u32[]{:S(2)}, u32[]{:S(2)}) collective-permute-start(bf16[168,256]{1,0:T(8,128)(2,1)} %get-tuple-element.188), channel_id=1, source_target_pairs={{3,0},{0,1},{1,2},{2,3},{7,4},{4,5},{5,6},{6,7},{11,8},{8,9},{9,10... | collective-permute-start | bytes 258056 | tf_op jit(solution)/shard_map/ppermute | solution.py:461
  141.1 11.2 %collective-permute-start.41 = (bf16[1024,256]{1,0:T(8,128)(2,1)}, bf16[1024,256]{1,0:T(8,128)(2,1)S(1)}, u32[]{:S(2)}, u32[]{:S(2)}) collective-permute-start(bf16[1024,256]{1,0:T(8,128)(2,1)} %get-tuple-element.221), channel_id=1, source_target_pairs={{1,0},{2,1},{3,2},{0,3},{5,4},{6,5},{7,6},{4,7},{9,8},{10,9},{11,1... | collective-permute-start | bytes 1572872 | tf_op jit(solution)/shard_map/ppermute | solution.py:461
  144.0 11.3 %collective-permute-start.42 = (bf16[1024,256]{1,0:T(8,128)(2,1)}, bf16[1024,256]{1,0:T(8,128)(2,1)S(1)}, u32[]{:S(2)}, u32[]{:S(2)}) collective-permute-start(bf16[1024,256]{1,0:T(8,128)(2,1)} %get-tuple-element.220), channel_id=1, source_target_pairs={{3,0},{0,1},{1,2},{2,3},{7,4},{4,5},{5,6},{6,7},{11,8},{8,9},{9,10... | collective-permute-start | bytes 1572872 | tf_op jit(solution)/shard_map/ppermute | solution.py:461
  155.3 12.5 %collective-permute-start.46 = (bf16[1024,256]{1,0:T(8,128)(2,1)S(1)}, bf16[1024,256]{1,0:T(8,128)(2,1)S(1)}, u32[]{:S(2)}, u32[]{:S(2)}) collective-permute-start(bf16[1024,256]{1,0:T(8,128)(2,1)S(1)} %collective-permute-done.41.refs_0_), channel_id=1, source_target_pairs={{1,0},{2,1},{3,2},{0,3},{5,4},{6,5},{7,6},{4,7},{9,8},{10,9},{11,1... | collective-permute-start | bytes 1572872 | tf_op jit(solution)/shard_map/ppermute | solution.py:461
  155.7 12.9 %collective-permute-start.47 = (bf16[1024,256]{1,0:T(8,128)(2,1)S(1)}, bf16[1024,256]{1,0:T(8,128)(2,1)S(1)}, u32[]{:S(2)}, u32[]{:S(2)}) collective-permute-start(bf16[1024,256]{1,0:T(8,128)(2,1)S(1)} %collective-permute-done.42.refs_3_), channel_id=1, source_target_pairs={{3,0},{0,1},{1,2},{2,3},{7,4},{4,5},{5,6},{6,7},{11,8},{8,9},{9,10... | collective-permute-start | bytes 1572872 | tf_op jit(solution)/shard_map/ppermute | solution.py:461
  157.4 6.2 %collective-permute-start.43 = (bf16[424,256]{1,0:T(8,128)(2,1)S(1)}, bf16[424,256]{1,0:T(8,128)(2,1)S(1)}, u32[]{:S(2)}, u32[]{:S(2)}) collective-permute-start(bf16[424,256]{1,0:T(8,128)(2,1)S(1)} %pad_maximum_fusion), channel_id=1, source_target_pairs={{8,0},{9,1},{10,2},{11,3},{12,4},{13,5},{14,6},{15,7},{16,8},{17,9... | collective-permute-start | bytes 651272 | tf_op jit(solution)/shard_map/ppermute | solution.py:461
  158.1 7.5 %collective-permute-start.44 = (bf16[424,256]{1,0:T(8,128)(2,1)S(1)}, bf16[424,256]{1,0:T(8,128)(2,1)S(1)}, u32[]{:S(2)}, u32[]{:S(2)}) collective-permute-start(bf16[424,256]{1,0:T(8,128)(2,1)S(1)} %pad_maximum_fusion), channel_id=1, source_target_pairs={{16,0},{17,1},{18,2},{19,3},{20,4},{21,5},{22,6},{23,7},{24,8},{25... | collective-permute-start | bytes 651272 | tf_op jit(solution)/shard_map/ppermute | solution.py:461
  158.9 8.9 %collective-permute-start.45 = (bf16[424,256]{1,0:T(8,128)(2,1)S(1)}, bf16[424,256]{1,0:T(8,128)(2,1)S(1)}, u32[]{:S(2)}, u32[]{:S(2)}) collective-permute-start(bf16[424,256]{1,0:T(8,128)(2,1)S(1)} %pad_maximum_fusion), channel_id=1, source_target_pairs={{24,0},{25,1},{26,2},{27,3},{28,4},{29,5},{30,6},{31,7},{0,8},{1,9... | collective-permute-start | bytes 651272 | tf_op jit(solution)/shard_map/ppermute | solution.py:461
  168.7 12.6 %collective-permute-start.52 = (bf16[1024,256]{1,0:T(8,128)(2,1)S(1)}, bf16[1024,256]{1,0:T(8,128)(2,1)S(1)}, u32[]{:S(2)}, u32[]{:S(2)}) collective-permute-start(bf16[1024,256]{1,0:T(8,128)(2,1)S(1)} %copy-done.35), channel_id=1, source_target_pairs={{1,0},{2,1},{3,2},{0,3},{5,4},{6,5},{7,6},{4,7},{9,8},{10,9},{11,1... | collective-permute-start | bytes 1572872 | tf_op jit(solution)/shard_map/ppermute | solution.py:461
  170.6 13.2 %collective-permute-start.53 = (bf16[1024,256]{1,0:T(8,128)(2,1)S(1)}, bf16[1024,256]{1,0:T(8,128)(2,1)S(1)}, u32[]{:S(2)}, u32[]{:S(2)}) collective-permute-start(bf16[1024,256]{1,0:T(8,128)(2,1)S(1)} %copy-done.34), channel_id=1, source_target_pairs={{3,0},{0,1},{1,2},{2,3},{7,4},{4,5},{5,6},{6,7},{11,8},{8,9},{9,10... | collective-permute-start | bytes 1572872 | tf_op jit(solution)/shard_map/ppermute | solution.py:461
  172.5 8.8 %collective-permute-start.49 = (bf16[168,256]{1,0:T(8,128)(2,1)S(1)}, bf16[168,256]{1,0:T(8,128)(2,1)S(1)}, u32[]{:S(2)}, u32[]{:S(2)}) collective-permute-start(bf16[168,256]{1,0:T(8,128)(2,1)S(1)} %slice.19.t0), channel_id=1, source_target_pairs={{32,0},{33,1},{34,2},{35,3},{36,4},{37,5},{38,6},{39,7},{40,8},{41... | collective-permute-start | bytes 258056 | tf_op jit(solution)/shard_map/ppermute | solution.py:461
  172.5 8.8 %collective-permute-start.50 = (bf16[168,256]{1,0:T(8,128)(2,1)S(1)}, bf16[168,256]{1,0:T(8,128)(2,1)S(1)}, u32[]{:S(2)}, u32[]{:S(2)}) collective-permute-start(bf16[168,256]{1,0:T(8,128)(2,1)S(1)} %slice.19.t0), channel_id=1, source_target_pairs={{64,0},{65,1},{66,2},{67,3},{68,4},{69,5},{70,6},{71,7},{72,8},{73... | collective-permute-start | bytes 258056 | tf_op jit(solution)/shard_map/ppermute | solution.py:461
  175.4 6.0 %collective-permute-start.51 = (bf16[168,256]{1,0:T(8,128)(2,1)S(1)}, bf16[168,256]{1,0:T(8,128)(2,1)S(1)}, u32[]{:S(2)}, u32[]{:S(2)}) collective-permute-start(bf16[168,256]{1,0:T(8,128)(2,1)S(1)} %slice.19.t0), channel_id=1, source_target_pairs={{96,0},{97,1},{98,2},{99,3},{100,4},{101,5},{102,6},{103,7},{104,8... | collective-permute-start | bytes 258056 | tf_op jit(solution)/shard_map/ppermute | solution.py:461
  (42 other events, 267.7 us)
where the time goes:
time: 189 us
  Pallas kernels  70.2 us (37%)
  starting transfers between devices  60.9 us (32%)
  waiting for transfers between devices  47.4 us (25%)
  other arithmetic  4.69 us (2%)
  local copies, waits for them, and re-layouts  4.25 us (2%)
    ppermute x54, starting transfers between devices, pull(): return lax.ppermute(value, axes, pairs)  60.9 us
    ppermute x54, waiting for transfers between devices, pull(): return lax.ppermute(value, axes, pairs)  47.4 us
    pallas_call x1, Pallas kernels, mlp_call(): pl.pallas_call(mlp_kernel, grid_spec=grid((quarter // size,), [row_spec(s...  16.9 us
    pallas_call x1, Pallas kernels, points_call(): pl.pallas_call(points_kernel, grid_spec=grid((steps,), [row_spec(size, 0)...  13.6 us
    pallas_call x3, Pallas kernels, fill_call(): pl.pallas_call(fill_kernel, grid_spec=grid((n,), [s for _, s in parts] +...  12.7 us
    pallas_call x1, Pallas kernels, local(): pl.pallas_call(own_sums_kernel, grid=(rows // (2 * WIDE),), in_specs=[pl....  8.94 us
    pallas_call x1, Pallas kernels, weights_call(): pl.pallas_call(weights_kernel, grid_spec=grid((quarter // WIDE,), [row_sp...  5.64 us
    unnamed x72, local copies, waits for them, and re-layouts  4.15 us
  transfers between devices with their start and end apart: 54, of which 24 were waited for; matrix products, arithmetic and copies ran while one was open for 2% of the time, Pallas kernels for 24%

commit v1 on v0

--- a/solution.py
+++ b/solution.py
@@ -72,7 +72,8 @@
     pack[512:576, :] = w_in[...]
     pack[576:640, :] = w_out[...]
     row = lax.broadcasted_iota(jnp.int32, (16, C), 0)
-    pack[640:656, :] = jnp.where(row == 0, sharp[0], jnp.where(row == 1, sharp[1], 0.0)).astype(BF)
+    both = sharp[...].astype(F32).reshape(1, GH)
+    pack[640:656, :] = jnp.where(row == 0, both[:, 0:1], both[:, 1:2]).astype(BF)
     s_scr[...] = jnp.zeros_like(s_scr)
     weight = slice_weight[...].astype(F32)
     twice = jnp.concatenate([weight, weight], 1)
@@ -351,15 +352,26 @@
             ref[104:168, :] = gout[k * 64 : (k + 1) * 64, :].astype(ref.dtype)
 
 
-HIGH = lax.Precision.HIGHEST
+def halves(value):
+    high = value.astype(BF)
+    return high, (value - high.astype(F32)).astype(BF)
+
+
+def dot3(a, b, form=dot):
+    (ah, al), (bh, bl) = halves(a), halves(b)
+    return form(ah, bh) + (form(ah, bl) + form(al, bh))
+
+
+def dot3_nt(a, b):
+    return dot3(a, b, dot_nt)
 
 
 def token_parts(nd, wq, wk, wv):
     padded = jnp.concatenate([nd, jnp.zeros((88, 128), F32)], 0).T
     denom = padded[:, HEAD_DIM : HEAD_DIM + 1]
     tok = padded[:, :HEAD_DIM] / denom
-    q, k, v = dot(tok, wq, HIGH), dot(tok, wk, HIGH), dot(tok, wv, HIGH)
-    scores = dot_nt(q, k, HIGH) * (1.0 / HEAD_DIM**0.5)
+    q, k, v = dot3(tok, wq), dot3(tok, wk), dot3(tok, wv)
+    scores = dot3_nt(q, k) * (1.0 / HEAD_DIM**0.5)
     row = lax.broadcasted_iota(jnp.int32, (128, 128), 0) < SLICES
     col = lax.broadcasted_iota(jnp.int32, (128, 128), 1) < SLICES
     same = row == col
@@ -378,7 +390,7 @@
     nd = (a[...] + c[...]) + (b[...] + d[...])
     total[...] = nd
     _, _, _, _, v, p = token_parts(nd, *(w[...].astype(F32) for w in (wq, wk, wv)))
-    mixed = dot(p, v, HIGH).astype(BF).astype(F32)
+    mixed = dot3(p, v).astype(BF).astype(F32)
     tokens[...] = flip(mixed)
 
 
@@ -387,19 +399,19 @@
     g = jnp.concatenate([gt, jnp.zeros((96, 128), F32)], 0).T[:, :HEAD_DIM]
     wq, wk, wv = (w[...].astype(F32) for w in (wq, wk, wv))
     denom, tok, q, k, v, p = token_parts(nd[...], wq, wk, wv)
-    dv = dot(p.T, g, HIGH)
-    dp = dot_nt(g, v, HIGH)
+    dv = dot3(p.T, g)
+    dp = dot3_nt(g, v)
     ds = p * (dp - jnp.sum(p * dp, -1, keepdims=True)) * (1.0 / HEAD_DIM**0.5)
-    dq = dot(ds, k, HIGH)
-    dk = dot(ds.T, q, HIGH)
-    gmt = dot_nt(dq, wq, HIGH) + dot_nt(dk, wk, HIGH) + dot_nt(dv, wv, HIGH)
+    dq = dot3(ds, k)
+    dk = dot3(ds.T, q)
+    gmt = dot3_nt(dq, wq) + dot3_nt(dk, wk) + dot3_nt(dv, wv)
     gnum = (gmt / denom).astype(BF).astype(F32)
     gden = -jnp.sum(gmt * tok, -1, keepdims=True) / denom
     gn[0:HEAD_DIM, :] = flip(gnum)
     gn[HEAD_DIM : HEAD_DIM + 8, :] = flip(jnp.broadcast_to(gden, (128, 8)))
     tok_t = flip(tok)
     qkv[...] = scale * jnp.concatenate(
-        [dot(tok_t, dq, HIGH), dot(tok_t, dk, HIGH), dot(tok_t, dv, HIGH), jnp.zeros((32, 32), F32)],
+        [dot3(tok_t, dq), dot3(tok_t, dk), dot3(tok_t, dv), jnp.zeros((32, 32), F32)],
         1,
     )
 
@@ -512,15 +524,11 @@
         prep_kernel,
         out_shape=[shape_of((656, C), BF), shape_of((HM, C), BF), shape_of((C, HM), BF)]
         + [shape_of((1, C), F32)] * 2,
-        in_specs=[pl.BlockSpec(memory_space=pltpu.VMEM)] * 4
-        + [pl.BlockSpec(memory_space=pltpu.SMEM)]
-        + [pl.BlockSpec(memory_space=pltpu.VMEM)] * 3,
         scratch_shapes=[pltpu.VMEM((C, HM), F32)],
         compiler_params=params,
         cost_estimate=cost(2),
         name="prep",
-    )(w_up, w_down, w_in.T, w_out, sharp.astype(F32), slice_weight, gain_one, gain_two)
-    packs = [pack] + pulls(pack, "dz")
+    )(w_up, w_down, w_in.T, w_out, sharp, slice_weight, gain_one, gain_two)
 
     nd = pl.pallas_call(
         own_sums_kernel,
@@ -594,13 +602,12 @@
             name="mlp",
         )(z, points, cotangent, wt, *tokens, gain2, *packs, *packs, *packs)
 
+    half = quarter // 2
+
     def points_call(tokens, gnums, wt, mid, gspread, gres, qkv, g2, gout):
-        size = NARROW
+        size = half
         steps = quarter // size
-        halves = [
-            pl.BlockSpec((size, C), lambda i, z: (jnp.minimum(i, steps // 2 - 1), 0)),
-            pl.BlockSpec((size, C), lambda i, z: (jnp.maximum(i - steps // 2, 0), 0)),
-        ]
+        halves = [full((half, C))] * 2
         return pl.pallas_call(
             points_kernel,
             grid_spec=grid(
@@ -639,8 +646,6 @@
             *packs, *packs, qkv, g2, gout
         )
 
-    half = quarter // 2
-
     def fill_out(at):
         return pl.BlockSpec(
             (half, C), lambda i, z: (lax.rem(2 * z[0] + at(i), 2 * BLOCKS), 0)
@@ -665,12 +670,13 @@
         return [(v, full((half, C))) for v in values]
 
     nd = core_sum(nd)
+    nd, sent = tie(nd, pack)
     got = axis_peers(nd, "dx")
-    nd, packs[0] = tie(nd, packs[0])
-    wt, mid = weights_call()
-    got, wt = tie(got, wt)
+    packs = [pack, pull(sent, dz=1), None, pull(sent, dz=3)]
     nd = add4(nd, got)
+    nd, sent = tie(nd, sent)
     got = axis_peers(nd, "dy")
+    packs[2] = pull(sent, dz=2)
     nd, own_tokens = pl.pallas_call(
         tokens_kernel,
         out_shape=[shape_of((40, 128), F32), shape_of((HEAD_DIM, 128), F32)],
@@ -678,7 +684,12 @@
         cost_estimate=cost(3),
         name="tokens",
     )(nd, *got, wq, wk, wv)
-    tokens = [own_tokens] + pulls(own_tokens, "dz")
+    got = pulls(own_tokens, "dz")
+
+    own_tokens, *packs = tie(own_tokens, *packs)
+    wt, mid = weights_call()
+    got, wt = tie(got, wt)
+    tokens = [own_tokens] + list(got)
 
     result = mlp_call(tokens, wt)
     mixed, gres, gspread, send = result[:4]
@@ -690,12 +701,12 @@
     gt, wg1 = tie(gt, wgs[1])
     wgot.append(pull(wg1, dz=3))
     gt = core_sum(gt)
+    gt, send = tie(gt, send)
     got = axis_peers(gt, "dx")
+    near = [pull(send, dz=1), pull(send, dz=3)]
     got, wgot = tie(got, wgot)
     gt = add4(gt, got)
     got = axis_peers(gt, "dy")
-    gt, send = tie(gt, send)
-    near = [pull(send, dz=1), pull(send, dz=3)]
     wsum = add4(wgs[0], wgot)
     wlow = wsum.astype(BF)
     own_gn, qkv = pl.pallas_call(

time: 189 us -> 186 us (0.984)
  waiting for transfers between devices: 47.4 us -> 38.3 us
  starting transfers between devices: 60.9 us -> 68.8 us
    ppermute x54, waiting for transfers between devices: 47.4 us -> 38.3 us  [pull(): return lax.ppermute(value, axes, pairs)]
    ppermute x54, starting transfers between devices: 60.9 us -> 68.8 us  [pull(): return lax.ppermute(value, axes, pairs)]
  transfers between devices with their start and end apart: 54 -> 54, of which waited for: 24 -> 19; matrix products, arithmetic and copies ran while one was open for 2% -> 2% of each run, Pallas kernels for 24% -> 20%
where the time goes in v1:
time: 186 us
  Pallas kernels  69.3 us (37%)
  starting transfers between devices  68.8 us (37%)
  waiting for transfers between devices  38.3 us (21%)
  local copies, waits for them, and re-layouts  4.28 us (2%)
  other arithmetic  3.6 us (2%)
    ppermute x54, starting transfers between devices, pull(): return lax.ppermute(value, axes, pairs)  68.8 us
    ppermute x54, waiting for transfers between devices, pull(): return lax.ppermute(value, axes, pairs)  38.3 us
    pallas_call x1, Pallas kernels, mlp_call(): pl.pallas_call(mlp_kernel, grid_spec=grid((quarter // size,), [row_spec(s...  16.9 us
    pallas_call x1, Pallas kernels, points_call(): pl.pallas_call(points_kernel, grid_spec=grid((steps,), [row_spec(size, 0)...  13.4 us
    pallas_call x3, Pallas kernels, fill_call(): pl.pallas_call(fill_kernel, grid_spec=grid((n,), [s for _, s in parts] +...  12.7 us
    pallas_call x1, Pallas kernels, local(): pl.pallas_call(own_sums_kernel, grid=(rows // (2 * WIDE),), in_specs=[pl....  8.94 us
    pallas_call x1, Pallas kernels, weights_call(): pl.pallas_call(weights_kernel, grid_spec=grid((quarter // WIDE,), [row_sp...  5.64 us
    unnamed x72, local copies, waits for them, and re-layouts  4.18 us
  transfers between devices with their start and end apart: 54, of which 19 were waited for; matrix products, arithmetic and copies ran while one was open for 2% of the time, Pallas kernels for 20%

profile of v1, /device:TPU:2, one launch (start us, length us, event | category | flops | bytes accessed | tf_op | source)
XLA Modules:
  0.0 185.7 jit_solution(17982944575028129880)
XLA Ops:
  0.6 2.1 %prep.1 = (bf16[656,256]{1,0:T(8,128)(2,1)}, bf16[512,256]{1,0:T(8,128)(2,1)}, bf16[256,512]{1,0:T(8,128)(2,1)}, f32[1,256]{1,0:T(1,128)}, f32[1,256]{1,0:T(1,128)}) custom-call(bf16[256,256]{1,0:T(8,128)(2,1)} %w_up.1, bf16[256,256]{1,0:T(8,128)(2,1)} %w_down.1, bf16[64,256]{1,0:T(8,128)(2,1)} %bitcast.7, bf16[64,256]{1,0:T(8,128)(2,1)} %w_out.1, ...), custom_call_target="tpu_custom_call" | custom-call | flops 2000000 | bytes 1024 | tf_op jit(solution)/shard_map/prep/pallas_call | solution.py:523
  2.7 8.9 %own_sums.1 = f32[40,128]{1,0:T(8,128)} custom-call(bf16[8192,256]{1,0:T(8,128)(2,1)} %pts.7, f32[1,256]{1,0:T(1,128)} %get-tuple-element.135.gain.refs_8_, bf16[656,256]{1,0:T(8,128)(2,1)} %get-tuple-element.143.w_in.sharp.in0.s0.refs_5_.refs_9_.refs_13_.refs_11_.refs_15_, bf16[512,256]{1,0:T(8,128)(2,1)} %get-tuple-element.137.spread_slices.refs_9_, ...), custom_call_target="tpu_custom_call" | custom-call | flops 8000000 | bytes 1024 | tf_op jit(solution)/shard_map/own_sums/pallas_call | solution.py:533
  14.2 1.6 collective-permute-start.3
  15.8 3.3 %collective-permute-start.1 = (f32[40,128]{1,0:T(8,128)S(1)}, f32[40,128]{1,0:T(8,128)S(1)}, u32[]{:S(2)}, u32[]{:S(2)}) collective-permute-start(f32[40,128]{1,0:T(8,128)S(1)} %add.83), channel_id=1, source_target_pairs={{64,0},{65,1},{66,2},{67,3},{68,4},{69,5},{70,6},{71,7},{72,8},{73... | collective-permute-start | bytes 61448 | tf_op jit(solution)/shard_map/ppermute | solution.py:473
  19.2 4.0 %collective-permute-start.10 = (bf16[656,256]{1,0:T(8,128)(2,1)}, bf16[656,256]{1,0:T(8,128)(2,1)S(1)}, u32[]{:S(2)}, u32[]{:S(2)}) collective-permute-start(bf16[656,256]{1,0:T(8,128)(2,1)} %get-tuple-element.143.w_in.sharp.in0.s0.refs_5_.refs_9_.refs_13_.refs_11_.refs_15_), channel_id=1, source_target_pairs={{1,0},{2,1},{3,2},{0,3},{5,4},{6,5},{7,6},{4,7},{9,8},{10,9},{11,1... | collective-permute-start | bytes 1007624 | tf_op jit(solution)/shard_map/ppermute | solution.py:473
  23.2 1.9 %collective-permute-start.11 = (bf16[656,256]{1,0:T(8,128)(2,1)}, bf16[656,256]{1,0:T(8,128)(2,1)S(1)}, u32[]{:S(2)}, u32[]{:S(2)}) collective-permute-start(bf16[656,256]{1,0:T(8,128)(2,1)} %get-tuple-element.143.w_in.sharp.in0.s0.refs_5_.refs_9_.refs_13_.refs_11_.refs_15_), channel_id=1, source_target_pairs={{2,0},{3,1},{0,2},{1,3},{6,4},{7,5},{4,6},{5,7},{10,8},{11,9},{8,1... | collective-permute-start | bytes 1007624 | tf_op jit(solution)/shard_map/ppermute | solution.py:473
  25.2 3.0 %collective-permute-start.4 = (f32[40,128]{1,0:T(8,128)S(1)}, f32[40,128]{1,0:T(8,128)S(1)}, u32[]{:S(2)}, u32[]{:S(2)}) collective-permute-start(f32[40,128]{1,0:T(8,128)S(1)} %add_add_fusion.3.a), channel_id=1, source_target_pairs={{8,0},{9,1},{10,2},{11,3},{12,4},{13,5},{14,6},{15,7},{16,8},{17,9... | collective-permute-start | bytes 61448 | tf_op jit(solution)/shard_map/ppermute | solution.py:473
  30.5 2.9 %collective-permute-done.5.c = f32[40,128]{1,0:T(8,128)S(1)} collective-permute-done((f32[40,128]{1,0:T(8,128)S(1)}, f32[40,128]{1,0:T(8,128)S(1)}, u32[]{:S(2)}, u32[]{:S(2)}) %collective-permute-start.5) | collective-permute-done | bytes 20512 | tf_op jit(solution)/shard_map/ppermute | solution.py:473
  33.5 1.5 collective-permute-done.6.d
  35.6 2.4 %tokens.1 = (f32[40,128]{1,0:T(8,128)}, f32[32,128]{1,0:T(8,128)}) custom-call(f32[40,128]{1,0:T(8,128)} %copy-done.20, f32[40,128]{1,0:T(8,128)} %copy-done.28, f32[40,128]{1,0:T(8,128)} %copy-done.29, f32[40,128]{1,0:T(8,128)} %copy-done.30, bf16[32,32]{1,0:T(8,128)(2,1)} %wq.3, bf16[32,32]{1,0:T(8,128)(2,1)} %wk.3, bf16[32,32]{1,0:T(8,128)(2,1)} %wv.3), custom_call_target="tpu_custom_call" | custom-call | flops 3000000 | bytes 1024 | tf_op jit(solution)/shard_map/tokens/pallas_call | solution.py:680
  39.4 2.8 %collective-permute-start.8 = (f32[32,128]{1,0:T(8,128)}, f32[32,128]{1,0:T(8,128)S(1)}, u32[]{:S(2)}, u32[]{:S(2)}) collective-permute-start(f32[32,128]{1,0:T(8,128)} %get-tuple-element.150.refs_0_), channel_id=1, source_target_pairs={{2,0},{3,1},{0,2},{1,3},{6,4},{7,5},{4,6},{5,7},{10,8},{11,9},{8,1... | collective-permute-start | bytes 49160 | tf_op jit(solution)/shard_map/ppermute | solution.py:473
  44.4 5.6 %weights.1 = (bf16[512,2048]{1,0:T(8,128)(2,1)}, bf16[2048,256]{1,0:T(8,128)(2,1)}) custom-call(s32[2]{0:T(128)} %pad_add_fusion.z, bf16[8192,256]{1,0:T(8,128)(2,1)} %pts.7, f32[1,256]{1,0:T(1,128)} %get-tuple-element.135.gain.refs_8_, bf16[656,256]{1,0:T(8,128)(2,1)} %get-tuple-element.143.w_in.sharp.in0.s0.refs_5_.refs_9_.refs_13_.refs_11_.refs_15_, ...), custom_call_target="tpu_custom_call" | custom-call | flops 5000000 | bytes 1024 | tf_op jit(solution)/shard_map/weights/pallas_call | solution.py:554
  50.7 16.9 %mlp.1 = (f32[8192,256]{1,0:T(8,128)}, bf16[2048,256]{1,0:T(8,128)(2,1)}, bf16[2048,256]{1,0:T(8,128)(2,1)}, bf16[2048,256]{1,0:T(8,128)(2,1)}, f32[32,128]{1,0:...) custom-call(s32[2]{0:T(128)} %pad_add_fusion.z, ...), custom_call_target="tpu_custom_call" | custom-call | flops 16000000 | bytes 1024 | tf_op jit(solution)/shard_map/mlp/pallas_call | solution.py:580
  67.7 3.2 %collective-permute-start.14 = (f32[32,128]{1,0:T(8,128)}, f32[32,128]{1,0:T(8,128)S(1)}, u32[]{:S(2)}, u32[]{:S(2)}) collective-permute-start(f32[32,128]{1,0:T(8,128)} %get-tuple-element.160), channel_id=1, source_target_pairs={{1,0},{2,1},{3,2},{0,3},{5,4},{6,5},{7,6},{4,7},{9,8},{10,9},{11,1... | collective-permute-start | bytes 49160 | tf_op jit(solution)/shard_map/ppermute | solution.py:473
  70.9 1.5 collective-permute-start.13
  72.4 1.7 collective-permute-start.20
  74.1 2.9 %collective-permute-start.21 = (bf16[512,256]{1,0:T(8,128)(2,1)}, bf16[512,256]{1,0:T(8,128)(2,1)S(1)}, u32[]{:S(2)}, u32[]{:S(2)}) collective-permute-start(bf16[512,256]{1,0:T(8,128)(2,1)} %get-tuple-element.167), channel_id=1, source_target_pairs={{2,0},{3,1},{0,2},{1,3},{6,4},{7,5},{4,6},{5,7},{10,8},{11,9},{8,1... | collective-permute-start | bytes 786440 | tf_op jit(solution)/shard_map/ppermute | solution.py:473
  79.3 1.9 %collective-permute-start.18 = (f32[32,128]{1,0:T(8,128)S(1)}, f32[32,128]{1,0:T(8,128)S(1)}, u32[]{:S(2)}, u32[]{:S(2)}) collective-permute-start(f32[32,128]{1,0:T(8,128)S(1)} %add.90), channel_id=1, source_target_pairs={{64,0},{65,1},{66,2},{67,3},{68,4},{69,5},{70,6},{71,7},{72,8},{73... | collective-permute-start | bytes 49160 | tf_op jit(solution)/shard_map/ppermute | solution.py:473
  81.2 1.6 collective-permute-done.17
  84.6 3.1 %collective-permute-start.30 = (bf16[2048,256]{1,0:T(8,128)(2,1)}, bf16[2048,256]{1,0:T(8,128)(2,1)S(1)}, u32[]{:S(2)}, u32[]{:S(2)}) collective-permute-start(bf16[2048,256]{1,0:T(8,128)(2,1)} %get-tuple-element.183), channel_id=1, source_target_pairs={{1,0},{2,1},{3,2},{0,3},{5,4},{6,5},{7,6},{4,7},{9,8},{10,9},{11,1... | collective-permute-start | bytes 3145736 | tf_op jit(solution)/shard_map/ppermute | solution.py:473
  87.7 2.3 %collective-permute-start.23 = (f32[32,128]{1,0:T(8,128)S(1)}, f32[32,128]{1,0:T(8,128)S(1)}, u32[]{:S(2)}, u32[]{:S(2)}) collective-permute-start(f32[32,128]{1,0:T(8,128)S(1)} %add_add_fusion.4.a), channel_id=1, source_target_pairs={{8,0},{9,1},{10,2},{11,3},{12,4},{13,5},{14,6},{15,7},{16,8},{17,9... | collective-permute-start | bytes 49160 | tf_op jit(solution)/shard_map/ppermute | solution.py:473
  92.3 3.0 %collective-permute-done.24.c = f32[32,128]{1,0:T(8,128)S(1)} collective-permute-done((f32[32,128]{1,0:T(8,128)S(1)}, f32[32,128]{1,0:T(8,128)S(1)}, u32[]{:S(2)}, u32[]{:S(2)}) %collective-permute-start.24) | collective-permute-done | bytes 16416 | tf_op jit(solution)/shard_map/ppermute | solution.py:473
  95.9 3.3 %tokens_back.1 = (f32[40,128]{1,0:T(8,128)}, f32[32,128]{1,0:T(8,128)}) custom-call(f32[40,128]{1,0:T(8,128)} %get-tuple-element.157.nd, f32[32,128]{1,0:T(8,128)} %copy-done.24, f32[32,128]{1,0:T(8,128)} %copy-done.31, f32[32,128]{1,0:T(8,128)} %copy-done.32, f32[32,128]{1,0:T(8,128)} %copy-done.33, bf16[32,32]{1,0:T(8,128)(2,1)} %wq.3, bf16[32,32]{1,0:T(8,128)(2,1)} %wk.3, ...), custom_call_target="tpu_custom_call" | custom-call | flops 4000000 | bytes 1024 | tf_op jit(solution)/shard_map/tokens_back/pallas_call | solution.py:712
  99.2 3.2 %collective-permute-start.26 = (f32[40,128]{1,0:T(8,128)}, f32[40,128]{1,0:T(8,128)S(1)}, u32[]{:S(2)}, u32[]{:S(2)}) collective-permute-start(f32[40,128]{1,0:T(8,128)} %get-tuple-element.177.refs_4_), channel_id=1, source_target_pairs={{1,0},{2,1},{3,2},{0,3},{5,4},{6,5},{7,6},{4,7},{9,8},{10,9},{11,1... | collective-permute-start | bytes 61448 | tf_op jit(solution)/shard_map/ppermute | solution.py:473
  102.4 1.7 collective-permute-start.27
  104.1 6.0 %collective-permute-done.26.refs_5_ = f32[40,128]{1,0:T(8,128)S(1)} collective-permute-done((f32[40,128]{1,0:T(8,128)}, f32[40,128]{1,0:T(8,128)S(1)}, u32[]{:S(2)}, u32[]{:S(2)}) %collective-permute-start.26) | collective-permute-done | bytes 20512 | tf_op jit(solution)/shard_map/ppermute | solution.py:473
  110.2 3.3 %collective-permute-done.27.refs_6_ = f32[40,128]{1,0:T(8,128)S(1)} collective-permute-done((f32[40,128]{1,0:T(8,128)}, f32[40,128]{1,0:T(8,128)S(1)}, u32[]{:S(2)}, u32[]{:S(2)}) %collective-permute-start.27) | collective-permute-done | bytes 20512 | tf_op jit(solution)/shard_map/ppermute | solution.py:473
  114.3 1.5 collective-permute-start.36
  115.9 2.9 %collective-permute-start.32 = (bf16[256,256]{1,0:T(8,128)(2,1)S(1)}, bf16[256,256]{1,0:T(8,128)(2,1)S(1)}, u32[]{:S(2)}, u32[]{:S(2)}) collective-permute-start(bf16[256,256]{1,0:T(8,128)(2,1)S(1)} %fusion.1), channel_id=1, source_target_pairs={{32,0},{33,1},{34,2},{35,3},{36,4},{37,5},{38,6},{39,7},{40,8},{41... | collective-permute-start | bytes 393224 | tf_op jit(solution)/shard_map/ppermute | solution.py:473
  119.3 1.8 collective-permute-start.34
  121.1 13.4 %points.1 = (f32[8192,256]{1,0:T(8,128)}, bf16[1024,256]{1,0:T(8,128)(2,1)}, bf16[1024,256]{1,0:T(8,128)(2,1)}, f32[168,256]{1,0:T(8,128)}, bf16[168,256]{1,0:T(...) custom-call(s32[2]{0:T(128)} %pad_add_fusion.z, bf16[8192,256]{1,0:T(8,128)(2,1)} %pts.7, ...), custom_call_target="tpu_custom_call" | custom-call | flops 12000000 | bytes 1024 | tf_op jit(solution)/shard_map/points/pallas_call | solution.py:611
  134.5 2.0 %collective-permute-start.37 = (bf16[168,256]{1,0:T(8,128)(2,1)}, bf16[168,256]{1,0:T(8,128)(2,1)S(1)}, u32[]{:S(2)}, u32[]{:S(2)}) collective-permute-start(bf16[168,256]{1,0:T(8,128)(2,1)} %get-tuple-element.204), channel_id=1, source_target_pairs={{1,0},{2,1},{3,2},{0,3},{5,4},{6,5},{7,6},{4,7},{9,8},{10,9},{11,1... | collective-permute-start | bytes 258056 | tf_op jit(solution)/shard_map/ppermute | solution.py:473
  137.5 2.4 %collective-permute-start.41 = (bf16[1024,256]{1,0:T(8,128)(2,1)}, bf16[1024,256]{1,0:T(8,128)(2,1)S(1)}, u32[]{:S(2)}, u32[]{:S(2)}) collective-permute-start(bf16[1024,256]{1,0:T(8,128)(2,1)} %get-tuple-element.235), channel_id=1, source_target_pairs={{1,0},{2,1},{3,2},{0,3},{5,4},{6,5},{7,6},{4,7},{9,8},{10,9},{11,1... | collective-permute-start | bytes 1572872 | tf_op jit(solution)/shard_map/ppermute | solution.py:473
  140.1 4.7 %fill.3.refs_2_ = f32[8192,256]{1,0:T(8,128)} custom-call(s32[2]{0:T(128)} %pad_add_fusion.z, bf16[2048,256]{1,0:T(8,128)(2,1)} %copy-done.3, bf16[2048,256]{1,0:T(8,128)(2,1)} %copy-done.3, bf16[1024,256]{1,0:T(8,128)(2,1)} %copy-done.8, bf16[1024,256]{1,0:T(8,128)(2,1)} %copy-done.9, ...), custom_call_target="tpu_custom_call", output_to_operand_aliasing={{}: (5, {})} | custom-call | flops 3000000 | bytes 1024 | tf_op jit(solution)/shard_map/fill/pallas_call | solution.py:656
  146.4 2.5 %collective-permute-done.41.refs_0_ = bf16[1024,256]{1,0:T(8,128)(2,1)S(1)} collective-permute-done((bf16[1024,256]{1,0:T(8,128)(2,1)}, bf16[1024,256]{1,0:T(8,128)(2,1)S(1)}, u32[]{:S(2)}, u32[]{:S(2)}) %collective-permute-start.41) | collective-permute-done | bytes 524320 | tf_op jit(solution)/shard_map/ppermute | solution.py:473
  148.9 2.8 %collective-permute-done.42.refs_3_ = bf16[1024,256]{1,0:T(8,128)(2,1)S(1)} collective-permute-done((bf16[1024,256]{1,0:T(8,128)(2,1)}, bf16[1024,256]{1,0:T(8,128)(2,1)S(1)}, u32[]{:S(2)}, u32[]{:S(2)}) %collective-permute-start.42) | collective-permute-done | bytes 524320 | tf_op jit(solution)/shard_map/ppermute | solution.py:473
  152.0 1.7 collective-permute-start.47
  153.7 2.0 %collective-permute-start.43 = (bf16[424,256]{1,0:T(8,128)(2,1)S(1)}, bf16[424,256]{1,0:T(8,128)(2,1)S(1)}, u32[]{:S(2)}, u32[]{:S(2)}) collective-permute-start(bf16[424,256]{1,0:T(8,128)(2,1)S(1)} %pad_maximum_fusion), channel_id=1, source_target_pairs={{8,0},{9,1},{10,2},{11,3},{12,4},{13,5},{14,6},{15,7},{16,8},{17,9... | collective-permute-start | bytes 651272 | tf_op jit(solution)/shard_map/ppermute | solution.py:473
  156.6 3.3 %fill.4 = f32[8192,256]{1,0:T(8,128)} custom-call(s32[2]{0:T(128)} %pad_add_fusion.z, bf16[2048,256]{1,0:T(8,128)(2,1)} %copy-done.4, bf16[2048,256]{1,0:T(8,128)(2,1)} %copy-done.4, f32[8192,256]{1,0:T(8,128)} %fill.3.refs_2_), custom_call_target="tpu_custom_call", output_to_operand_aliasing={{}: (3, {})} | custom-call | flops 3000000 | bytes 1024 | tf_op jit(solution)/shard_map/fill/pallas_call | solution.py:656
  159.8 1.6 collective-permute-done.43
  161.5 1.7 collective-permute-done.44
  163.2 1.9 %collective-permute-done.45 = bf16[424,256]{1,0:T(8,128)(2,1)S(1)} collective-permute-done((bf16[424,256]{1,0:T(8,128)(2,1)S(1)}, bf16[424,256]{1,0:T(8,128)(2,1)S(1)}, u32[]{:S(2)}, u32[]{:S(2)}) %collective-permute-start.45) | collective-permute-done | bytes 217120 | tf_op jit(solution)/shard_map/ppermute | solution.py:473
  165.3 2.3 %collective-permute-start.52 = (bf16[1024,256]{1,0:T(8,128)(2,1)S(1)}, bf16[1024,256]{1,0:T(8,128)(2,1)S(1)}, u32[]{:S(2)}, u32[]{:S(2)}) collective-permute-start(bf16[1024,256]{1,0:T(8,128)(2,1)S(1)} %copy-done.35), channel_id=1, source_target_pairs={{1,0},{2,1},{3,2},{0,3},{5,4},{6,5},{7,6},{4,7},{9,8},{10,9},{11,1... | collective-permute-start | bytes 1572872 | tf_op jit(solution)/shard_map/ppermute | solution.py:473
  167.7 1.5 collective-permute-done.48.w1
  169.8 3.0 %collective-permute-start.50 = (bf16[168,256]{1,0:T(8,128)(2,1)S(1)}, bf16[168,256]{1,0:T(8,128)(2,1)S(1)}, u32[]{:S(2)}, u32[]{:S(2)}) collective-permute-start(bf16[168,256]{1,0:T(8,128)(2,1)S(1)} %slice.19.t0), channel_id=1, source_target_pairs={{64,0},{65,1},{66,2},{67,3},{68,4},{69,5},{70,6},{71,7},{72,8},{73... | collective-permute-start | bytes 258056 | tf_op jit(solution)/shard_map/ppermute | solution.py:473
  173.7 4.7 %fill.5.before = f32[8192,256]{1,0:T(8,128)} custom-call(s32[2]{0:T(128)} %pad_add_fusion.z, bf16[1024,256]{1,0:T(8,128)(2,1)} %copy-done.6, bf16[1024,256]{1,0:T(8,128)(2,1)} %copy-done.10, bf16[1024,256]{1,0:T(8,128)(2,1)} %copy-done.11, bf16[1024,256]{1,0:T(8,128)(2,1)} %copy-done.7, ...), custom_call_target="tpu_custom_call", output_to_operand_aliasing={{}: (5, {})} | custom-call | flops 3000000 | bytes 1024 | tf_op jit(solution)/shard_map/fill/pallas_call | solution.py:656
  178.4 2.2 %collective-permute-done.53.second = bf16[1024,256]{1,0:T(8,128)(2,1)S(1)} collective-permute-done((bf16[1024,256]{1,0:T(8,128)(2,1)S(1)}, bf16[1024,256]{1,0:T(8,128)(2,1)S(1)}, u32[]{:S(2)}, u32[]{:S(2)}) %collective-permute-start.53) | collective-permute-done | bytes 524320 | tf_op jit(solution)/shard_map/ppermute | solution.py:473
  181.5 4.0 %finish.1 = (f32[8192,256]{1,0:T(8,128)}, f32[64,256]{1,0:T(8,128)}, f32[32,64]{1,0:T(8,128)}, f32[1,2]{1,0:T(1,128)}, f32[32,32]{1,0:T(8,128)}, /*index=5*/f32[...) custom-call(s32[2]{0:T(128)} %pad_add_fusion.z, ...), custom_call_target="tpu_custom_call", output_to_operand_aliasing={{0}: (3, {})} | custom-call | flops 4000000 | bytes 1024 | tf_op jit(solution)/shard_map/finish/pallas_call | solution.py:764
  (160 shorter events, 24.6 us)
Async XLA Ops:
  13.8 9.4 %collective-permute-start.2 = (f32[40,128]{1,0:T(8,128)S(1)}, f32[40,128]{1,0:T(8,128)S(1)}, u32[]{:S(2)}, u32[]{:S(2)}) collective-permute-start(f32[40,128]{1,0:T(8,128)S(1)} %add.83), channel_id=1, source_target_pairs={{32,0},{33,1},{34,2},{35,3},{36,4},{37,5},{38,6},{39,7},{40,8},{41... | collective-permute-start | bytes 61448 | tf_op jit(solution)/shard_map/ppermute | solution.py:473
  14.2 9.0 %collective-permute-start.3 = (f32[40,128]{1,0:T(8,128)S(1)}, f32[40,128]{1,0:T(8,128)S(1)}, u32[]{:S(2)}, u32[]{:S(2)}) collective-permute-start(f32[40,128]{1,0:T(8,128)S(1)} %add.83), channel_id=1, source_target_pairs={{96,0},{97,1},{98,2},{99,3},{100,4},{101,5},{102,6},{103,7},{104,8... | collective-permute-start | bytes 61448 | tf_op jit(solution)/shard_map/ppermute | solution.py:473
  15.8 7.4 %collective-permute-start.1 = (f32[40,128]{1,0:T(8,128)S(1)}, f32[40,128]{1,0:T(8,128)S(1)}, u32[]{:S(2)}, u32[]{:S(2)}) collective-permute-start(f32[40,128]{1,0:T(8,128)S(1)} %add.83), channel_id=1, source_target_pairs={{64,0},{65,1},{66,2},{67,3},{68,4},{69,5},{70,6},{71,7},{72,8},{73... | collective-permute-start | bytes 61448 | tf_op jit(solution)/shard_map/ppermute | solution.py:473
  19.2 23.1 %collective-permute-start.10 = (bf16[656,256]{1,0:T(8,128)(2,1)}, bf16[656,256]{1,0:T(8,128)(2,1)S(1)}, u32[]{:S(2)}, u32[]{:S(2)}) collective-permute-start(bf16[656,256]{1,0:T(8,128)(2,1)} %get-tuple-element.143.w_in.sharp.in0.s0.refs_5_.refs_9_.refs_13_.refs_11_.refs_15_), channel_id=1, source_target_pairs={{1,0},{2,1},{3,2},{0,3},{5,4},{6,5},{7,6},{4,7},{9,8},{10,9},{11,1... | collective-permute-start | bytes 1007624 | tf_op jit(solution)/shard_map/ppermute | solution.py:473
  23.2 19.7 %collective-permute-start.12 = (bf16[656,256]{1,0:T(8,128)(2,1)}, bf16[656,256]{1,0:T(8,128)(2,1)S(1)}, u32[]{:S(2)}, u32[]{:S(2)}) collective-permute-start(bf16[656,256]{1,0:T(8,128)(2,1)} %get-tuple-element.143.w_in.sharp.in0.s0.refs_5_.refs_9_.refs_13_.refs_11_.refs_15_), channel_id=1, source_target_pairs={{3,0},{0,1},{1,2},{2,3},{7,4},{4,5},{5,6},{6,7},{11,8},{8,9},{9,10... | collective-permute-start | bytes 1007624 | tf_op jit(solution)/shard_map/ppermute | solution.py:473
  23.2 19.7 %collective-permute-start.11 = (bf16[656,256]{1,0:T(8,128)(2,1)}, bf16[656,256]{1,0:T(8,128)(2,1)S(1)}, u32[]{:S(2)}, u32[]{:S(2)}) collective-permute-start(bf16[656,256]{1,0:T(8,128)(2,1)} %get-tuple-element.143.w_in.sharp.in0.s0.refs_5_.refs_9_.refs_13_.refs_11_.refs_15_), channel_id=1, source_target_pairs={{2,0},{3,1},{0,2},{1,3},{6,4},{7,5},{4,6},{5,7},{10,8},{11,9},{8,1... | collective-permute-start | bytes 1007624 | tf_op jit(solution)/shard_map/ppermute | solution.py:473
  28.2 5.3 %collective-permute-start.5 = (f32[40,128]{1,0:T(8,128)S(1)}, f32[40,128]{1,0:T(8,128)S(1)}, u32[]{:S(2)}, u32[]{:S(2)}) collective-permute-start(f32[40,128]{1,0:T(8,128)S(1)} %add_add_fusion.3.a), channel_id=1, source_target_pairs={{16,0},{17,1},{18,2},{19,3},{20,4},{21,5},{22,6},{23,7},{24,8},{25... | collective-permute-start | bytes 61448 | tf_op jit(solution)/shard_map/ppermute | solution.py:473
  29.7 5.3 %collective-permute-start.6 = (f32[40,128]{1,0:T(8,128)S(1)}, f32[40,128]{1,0:T(8,128)S(1)}, u32[]{:S(2)}, u32[]{:S(2)}) collective-permute-start(f32[40,128]{1,0:T(8,128)S(1)} %add_add_fusion.3.a), channel_id=1, source_target_pairs={{24,0},{25,1},{26,2},{27,3},{28,4},{29,5},{30,6},{31,7},{0,8},{1,9... | collective-permute-start | bytes 61448 | tf_op jit(solution)/shard_map/ppermute | solution.py:473
  37.9 12.1 %collective-permute-start.7 = (f32[32,128]{1,0:T(8,128)}, f32[32,128]{1,0:T(8,128)S(1)}, u32[]{:S(2)}, u32[]{:S(2)}) collective-permute-start(f32[32,128]{1,0:T(8,128)} %get-tuple-element.150.refs_0_), channel_id=1, source_target_pairs={{1,0},{2,1},{3,2},{0,3},{5,4},{6,5},{7,6},{4,7},{9,8},{10,9},{11,1... | collective-permute-start | bytes 49160 | tf_op jit(solution)/shard_map/ppermute | solution.py:473
  39.4 10.7 %collective-permute-start.8 = (f32[32,128]{1,0:T(8,128)}, f32[32,128]{1,0:T(8,128)S(1)}, u32[]{:S(2)}, u32[]{:S(2)}) collective-permute-start(f32[32,128]{1,0:T(8,128)} %get-tuple-element.150.refs_0_), channel_id=1, source_target_pairs={{2,0},{3,1},{0,2},{1,3},{6,4},{7,5},{4,6},{5,7},{10,8},{11,9},{8,1... | collective-permute-start | bytes 49160 | tf_op jit(solution)/shard_map/ppermute | solution.py:473
  42.2 7.8 %collective-permute-start.9 = (f32[32,128]{1,0:T(8,128)}, f32[32,128]{1,0:T(8,128)S(1)}, u32[]{:S(2)}, u32[]{:S(2)}) collective-permute-start(f32[32,128]{1,0:T(8,128)} %get-tuple-element.150.refs_0_), channel_id=1, source_target_pairs={{3,0},{0,1},{1,2},{2,3},{7,4},{4,5},{5,6},{6,7},{11,8},{8,9},{9,10... | collective-permute-start | bytes 49160 | tf_op jit(solution)/shard_map/ppermute | solution.py:473
  67.7 9.4 %collective-permute-start.14 = (f32[32,128]{1,0:T(8,128)}, f32[32,128]{1,0:T(8,128)S(1)}, u32[]{:S(2)}, u32[]{:S(2)}) collective-permute-start(f32[32,128]{1,0:T(8,128)} %get-tuple-element.160), channel_id=1, source_target_pairs={{1,0},{2,1},{3,2},{0,3},{5,4},{6,5},{7,6},{4,7},{9,8},{10,9},{11,1... | collective-permute-start | bytes 49160 | tf_op jit(solution)/shard_map/ppermute | solution.py:473
  70.9 6.2 %collective-permute-start.15 = (f32[32,128]{1,0:T(8,128)}, f32[32,128]{1,0:T(8,128)S(1)}, u32[]{:S(2)}, u32[]{:S(2)}) collective-permute-start(f32[32,128]{1,0:T(8,128)} %get-tuple-element.161), channel_id=1, source_target_pairs={{3,0},{0,1},{1,2},{2,3},{7,4},{4,5},{5,6},{6,7},{11,8},{8,9},{9,10... | collective-permute-start | bytes 49160 | tf_op jit(solution)/shard_map/ppermute | solution.py:473
  70.9 6.2 %collective-permute-start.13 = (f32[32,128]{1,0:T(8,128)}, f32[32,128]{1,0:T(8,128)S(1)}, u32[]{:S(2)}, u32[]{:S(2)}) collective-permute-start(f32[32,128]{1,0:T(8,128)} %get-tuple-element.159), channel_id=1, source_target_pairs={{2,0},{3,1},{0,2},{1,3},{6,4},{7,5},{4,6},{5,7},{10,8},{11,9},{8,1... | collective-permute-start | bytes 49160 | tf_op jit(solution)/shard_map/ppermute | solution.py:473
  72.4 15.3 %collective-permute-start.20 = (bf16[512,256]{1,0:T(8,128)(2,1)}, bf16[512,256]{1,0:T(8,128)(2,1)S(1)}, u32[]{:S(2)}, u32[]{:S(2)}) collective-permute-start(bf16[512,256]{1,0:T(8,128)(2,1)} %get-tuple-element.166), channel_id=1, source_target_pairs={{1,0},{2,1},{3,2},{0,3},{5,4},{6,5},{7,6},{4,7},{9,8},{10,9},{11,1... | collective-permute-start | bytes 786440 | tf_op jit(solution)/shard_map/ppermute | solution.py:473
  74.1 13.6 %collective-permute-start.21 = (bf16[512,256]{1,0:T(8,128)(2,1)}, bf16[512,256]{1,0:T(8,128)(2,1)S(1)}, u32[]{:S(2)}, u32[]{:S(2)}) collective-permute-start(bf16[512,256]{1,0:T(8,128)(2,1)} %get-tuple-element.167), channel_id=1, source_target_pairs={{2,0},{3,1},{0,2},{1,3},{6,4},{7,5},{4,6},{5,7},{10,8},{11,9},{8,1... | collective-permute-start | bytes 786440 | tf_op jit(solution)/shard_map/ppermute | solution.py:473
  77.8 9.9 %collective-permute-start.22 = (bf16[512,256]{1,0:T(8,128)(2,1)}, bf16[512,256]{1,0:T(8,128)(2,1)S(1)}, u32[]{:S(2)}, u32[]{:S(2)}) collective-permute-start(bf16[512,256]{1,0:T(8,128)(2,1)} %get-tuple-element.168), channel_id=1, source_target_pairs={{3,0},{0,1},{1,2},{2,3},{7,4},{4,5},{5,6},{6,7},{11,8},{8,9},{9,10... | collective-permute-start | bytes 786440 | tf_op jit(solution)/shard_map/ppermute | solution.py:473
  79.3 5.2 %collective-permute-start.18 = (f32[32,128]{1,0:T(8,128)S(1)}, f32[32,128]{1,0:T(8,128)S(1)}, u32[]{:S(2)}, u32[]{:S(2)}) collective-permute-start(f32[32,128]{1,0:T(8,128)S(1)} %add.90), channel_id=1, source_target_pairs={{64,0},{65,1},{66,2},{67,3},{68,4},{69,5},{70,6},{71,7},{72,8},{73... | collective-permute-start | bytes 49160 | tf_op jit(solution)/shard_map/ppermute | solution.py:473
  82.8 4.8 %collective-permute-start.19 = (f32[32,128]{1,0:T(8,128)S(1)}, f32[32,128]{1,0:T(8,128)S(1)}, u32[]{:S(2)}, u32[]{:S(2)}) collective-permute-start(f32[32,128]{1,0:T(8,128)S(1)} %add.90), channel_id=1, source_target_pairs={{96,0},{97,1},{98,2},{99,3},{100,4},{101,5},{102,6},{103,7},{104,8... | collective-permute-start | bytes 49160 | tf_op jit(solution)/shard_map/ppermute | solution.py:473
  84.6 29.0 %collective-permute-start.30 = (bf16[2048,256]{1,0:T(8,128)(2,1)}, bf16[2048,256]{1,0:T(8,128)(2,1)S(1)}, u32[]{:S(2)}, u32[]{:S(2)}) collective-permute-start(bf16[2048,256]{1,0:T(8,128)(2,1)} %get-tuple-element.183), channel_id=1, source_target_pairs={{1,0},{2,1},{3,2},{0,3},{5,4},{6,5},{7,6},{4,7},{9,8},{10,9},{11,1... | collective-permute-start | bytes 3145736 | tf_op jit(solution)/shard_map/ppermute | solution.py:473
  87.7 25.9 %collective-permute-start.31 = (bf16[2048,256]{1,0:T(8,128)(2,1)}, bf16[2048,256]{1,0:T(8,128)(2,1)S(1)}, u32[]{:S(2)}, u32[]{:S(2)}) collective-permute-start(bf16[2048,256]{1,0:T(8,128)(2,1)} %get-tuple-element.183), channel_id=1, source_target_pairs={{3,0},{0,1},{1,2},{2,3},{7,4},{4,5},{5,6},{6,7},{11,8},{8,9},{9,10... | collective-permute-start | bytes 3145736 | tf_op jit(solution)/shard_map/ppermute | solution.py:473
  87.7 4.6 %collective-permute-start.23 = (f32[32,128]{1,0:T(8,128)S(1)}, f32[32,128]{1,0:T(8,128)S(1)}, u32[]{:S(2)}, u32[]{:S(2)}) collective-permute-start(f32[32,128]{1,0:T(8,128)S(1)} %add_add_fusion.4.a), channel_id=1, source_target_pairs={{8,0},{9,1},{10,2},{11,3},{12,4},{13,5},{14,6},{15,7},{16,8},{17,9... | collective-permute-start | bytes 49160 | tf_op jit(solution)/shard_map/ppermute | solution.py:473
  90.0 5.2 %collective-permute-start.24 = (f32[32,128]{1,0:T(8,128)S(1)}, f32[32,128]{1,0:T(8,128)S(1)}, u32[]{:S(2)}, u32[]{:S(2)}) collective-permute-start(f32[32,128]{1,0:T(8,128)S(1)} %add_add_fusion.4.a), channel_id=1, source_target_pairs={{16,0},{17,1},{18,2},{19,3},{20,4},{21,5},{22,6},{23,7},{24,8},{25... | collective-permute-start | bytes 49160 | tf_op jit(solution)/shard_map/ppermute | solution.py:473
  90.1 5.1 %collective-permute-start.25 = (f32[32,128]{1,0:T(8,128)S(1)}, f32[32,128]{1,0:T(8,128)S(1)}, u32[]{:S(2)}, u32[]{:S(2)}) collective-permute-start(f32[32,128]{1,0:T(8,128)S(1)} %add_add_fusion.4.a), channel_id=1, source_target_pairs={{24,0},{25,1},{26,2},{27,3},{28,4},{29,5},{30,6},{31,7},{0,8},{1,9... | collective-permute-start | bytes 49160 | tf_op jit(solution)/shard_map/ppermute | solution.py:473
  99.2 4.9 %collective-permute-start.29 = (bf16[512,256]{1,0:T(8,128)(2,1)S(1)}, bf16[512,256]{1,0:T(8,128)(2,1)S(1)}, u32[]{:S(2)}, u32[]{:S(2)}) collective-permute-start(bf16[512,256]{1,0:T(8,128)(2,1)S(1)} %get-tuple-element.179), channel_id=1, source_target_pairs={{4,0},{5,1},{6,2},{7,3},{0,4},{1,5},{2,6},{3,7},{12,8},{13,9},{14,... | collective-permute-start | bytes 786440 | tf_op jit(solution)/shard_map/ppermute | solution.py:473
  99.2 11.0 %collective-permute-start.26 = (f32[40,128]{1,0:T(8,128)}, f32[40,128]{1,0:T(8,128)S(1)}, u32[]{:S(2)}, u32[]{:S(2)}) collective-permute-start(f32[40,128]{1,0:T(8,128)} %get-tuple-element.177.refs_4_), channel_id=1, source_target_pairs={{1,0},{2,1},{3,2},{0,3},{5,4},{6,5},{7,6},{4,7},{9,8},{10,9},{11,1... | collective-permute-start | bytes 61448 | tf_op jit(solution)/shard_map/ppermute | solution.py:473
  102.4 11.1 %collective-permute-start.27 = (f32[40,128]{1,0:T(8,128)}, f32[40,128]{1,0:T(8,128)S(1)}, u32[]{:S(2)}, u32[]{:S(2)}) collective-permute-start(f32[40,128]{1,0:T(8,128)} %get-tuple-element.177.refs_4_), channel_id=1, source_target_pairs={{2,0},{3,1},{0,2},{1,3},{6,4},{7,5},{4,6},{5,7},{10,8},{11,9},{8,1... | collective-permute-start | bytes 61448 | tf_op jit(solution)/shard_map/ppermute | solution.py:473
  104.1 9.5 %collective-permute-start.28 = (f32[40,128]{1,0:T(8,128)}, f32[40,128]{1,0:T(8,128)S(1)}, u32[]{:S(2)}, u32[]{:S(2)}) collective-permute-start(f32[40,128]{1,0:T(8,128)} %get-tuple-element.177.refs_4_), channel_id=1, source_target_pairs={{3,0},{0,1},{1,2},{2,3},{7,4},{4,5},{5,6},{6,7},{11,8},{8,9},{9,10... | collective-permute-start | bytes 61448 | tf_op jit(solution)/shard_map/ppermute | solution.py:473
  113.7 20.8 %collective-permute-start.35 = (bf16[1024,256]{1,0:T(8,128)(2,1)S(1)}, bf16[1024,256]{1,0:T(8,128)(2,1)S(1)}, u32[]{:S(2)}, u32[]{:S(2)}) collective-permute-start(bf16[1024,256]{1,0:T(8,128)(2,1)S(1)} %slice.13), channel_id=1, source_target_pairs={{1,0},{2,1},{3,2},{0,3},{5,4},{6,5},{7,6},{4,7},{9,8},{10,9},{11,1... | collective-permute-start | bytes 1572872 | tf_op jit(solution)/shard_map/ppermute | solution.py:473
  114.3 20.2 %collective-permute-start.36 = (bf16[1024,256]{1,0:T(8,128)(2,1)S(1)}, bf16[1024,256]{1,0:T(8,128)(2,1)S(1)}, u32[]{:S(2)}, u32[]{:S(2)}) collective-permute-start(bf16[1024,256]{1,0:T(8,128)(2,1)S(1)} %slice.14), channel_id=1, source_target_pairs={{3,0},{0,1},{1,2},{2,3},{7,4},{4,5},{5,6},{6,7},{11,8},{8,9},{9,10... | collective-permute-start | bytes 1572872 | tf_op jit(solution)/shard_map/ppermute | solution.py:473
  115.9 18.6 %collective-permute-start.32 = (bf16[256,256]{1,0:T(8,128)(2,1)S(1)}, bf16[256,256]{1,0:T(8,128)(2,1)S(1)}, u32[]{:S(2)}, u32[]{:S(2)}) collective-permute-start(bf16[256,256]{1,0:T(8,128)(2,1)S(1)} %fusion.1), channel_id=1, source_target_pairs={{32,0},{33,1},{34,2},{35,3},{36,4},{37,5},{38,6},{39,7},{40,8},{41... | collective-permute-start | bytes 393224 | tf_op jit(solution)/shard_map/ppermute | solution.py:473
  118.7 15.7 %collective-permute-start.33 = (bf16[256,256]{1,0:T(8,128)(2,1)S(1)}, bf16[256,256]{1,0:T(8,128)(2,1)S(1)}, u32[]{:S(2)}, u32[]{:S(2)}) collective-permute-start(bf16[256,256]{1,0:T(8,128)(2,1)S(1)} %fusion.1), channel_id=1, source_target_pairs={{64,0},{65,1},{66,2},{67,3},{68,4},{69,5},{70,6},{71,7},{72,8},{73... | collective-permute-start | bytes 393224 | tf_op jit(solution)/shard_map/ppermute | solution.py:473
  119.3 15.2 %collective-permute-start.34 = (bf16[256,256]{1,0:T(8,128)(2,1)S(1)}, bf16[256,256]{1,0:T(8,128)(2,1)S(1)}, u32[]{:S(2)}, u32[]{:S(2)}) collective-permute-start(bf16[256,256]{1,0:T(8,128)(2,1)S(1)} %fusion.1), channel_id=1, source_target_pairs={{96,0},{97,1},{98,2},{99,3},{100,4},{101,5},{102,6},{103,7},{104,8... | collective-permute-start | bytes 393224 | tf_op jit(solution)/shard_map/ppermute | solution.py:473
  134.5 10.2 %collective-permute-start.37 = (bf16[168,256]{1,0:T(8,128)(2,1)}, bf16[168,256]{1,0:T(8,128)(2,1)S(1)}, u32[]{:S(2)}, u32[]{:S(2)}) collective-permute-start(bf16[168,256]{1,0:T(8,128)(2,1)} %get-tuple-element.204), channel_id=1, source_target_pairs={{1,0},{2,1},{3,2},{0,3},{5,4},{6,5},{7,6},{4,7},{9,8},{10,9},{11,1... | collective-permute-start | bytes 258056 | tf_op jit(solution)/shard_map/ppermute | solution.py:473
  136.6 8.2 %collective-permute-start.38 = (bf16[168,256]{1,0:T(8,128)(2,1)}, bf16[168,256]{1,0:T(8,128)(2,1)S(1)}, u32[]{:S(2)}, u32[]{:S(2)}) collective-permute-start(bf16[168,256]{1,0:T(8,128)(2,1)} %get-tuple-element.203), channel_id=1, source_target_pairs={{2,0},{3,1},{0,2},{1,3},{6,4},{7,5},{4,6},{5,7},{10,8},{11,9},{8,1... | collective-permute-start | bytes 258056 | tf_op jit(solution)/shard_map/ppermute | solution.py:473
  136.8 8.0 %collective-permute-start.39 = (bf16[168,256]{1,0:T(8,128)(2,1)}, bf16[168,256]{1,0:T(8,128)(2,1)S(1)}, u32[]{:S(2)}, u32[]{:S(2)}) collective-permute-start(bf16[168,256]{1,0:T(8,128)(2,1)} %get-tuple-element.202), channel_id=1, source_target_pairs={{3,0},{0,1},{1,2},{2,3},{7,4},{4,5},{5,6},{6,7},{11,8},{8,9},{9,10... | collective-permute-start | bytes 258056 | tf_op jit(solution)/shard_map/ppermute | solution.py:473
  137.5 11.4 %collective-permute-start.41 = (bf16[1024,256]{1,0:T(8,128)(2,1)}, bf16[1024,256]{1,0:T(8,128)(2,1)S(1)}, u32[]{:S(2)}, u32[]{:S(2)}) collective-permute-start(bf16[1024,256]{1,0:T(8,128)(2,1)} %get-tuple-element.235), channel_id=1, source_target_pairs={{1,0},{2,1},{3,2},{0,3},{5,4},{6,5},{7,6},{4,7},{9,8},{10,9},{11,1... | collective-permute-start | bytes 1572872 | tf_op jit(solution)/shard_map/ppermute | solution.py:473
  140.0 11.7 %collective-permute-start.42 = (bf16[1024,256]{1,0:T(8,128)(2,1)}, bf16[1024,256]{1,0:T(8,128)(2,1)S(1)}, u32[]{:S(2)}, u32[]{:S(2)}) collective-permute-start(bf16[1024,256]{1,0:T(8,128)(2,1)} %get-tuple-element.234), channel_id=1, source_target_pairs={{3,0},{0,1},{1,2},{2,3},{7,4},{4,5},{5,6},{6,7},{11,8},{8,9},{9,10... | collective-permute-start | bytes 1572872 | tf_op jit(solution)/shard_map/ppermute | solution.py:473
  151.7 13.5 %collective-permute-start.46 = (bf16[1024,256]{1,0:T(8,128)(2,1)S(1)}, bf16[1024,256]{1,0:T(8,128)(2,1)S(1)}, u32[]{:S(2)}, u32[]{:S(2)}) collective-permute-start(bf16[1024,256]{1,0:T(8,128)(2,1)S(1)} %collective-permute-done.41.refs_0_), channel_id=1, source_target_pairs={{1,0},{2,1},{3,2},{0,3},{5,4},{6,5},{7,6},{4,7},{9,8},{10,9},{11,1... | collective-permute-start | bytes 1572872 | tf_op jit(solution)/shard_map/ppermute | solution.py:473
  152.0 13.1 %collective-permute-start.47 = (bf16[1024,256]{1,0:T(8,128)(2,1)S(1)}, bf16[1024,256]{1,0:T(8,128)(2,1)S(1)}, u32[]{:S(2)}, u32[]{:S(2)}) collective-permute-start(bf16[1024,256]{1,0:T(8,128)(2,1)S(1)} %collective-permute-done.42.refs_3_), channel_id=1, source_target_pairs={{3,0},{0,1},{1,2},{2,3},{7,4},{4,5},{5,6},{6,7},{11,8},{8,9},{9,10... | collective-permute-start | bytes 1572872 | tf_op jit(solution)/shard_map/ppermute | solution.py:473
  153.7 7.8 %collective-permute-start.43 = (bf16[424,256]{1,0:T(8,128)(2,1)S(1)}, bf16[424,256]{1,0:T(8,128)(2,1)S(1)}, u32[]{:S(2)}, u32[]{:S(2)}) collective-permute-start(bf16[424,256]{1,0:T(8,128)(2,1)S(1)} %pad_maximum_fusion), channel_id=1, source_target_pairs={{8,0},{9,1},{10,2},{11,3},{12,4},{13,5},{14,6},{15,7},{16,8},{17,9... | collective-permute-start | bytes 651272 | tf_op jit(solution)/shard_map/ppermute | solution.py:473
  155.7 7.5 %collective-permute-start.44 = (bf16[424,256]{1,0:T(8,128)(2,1)S(1)}, bf16[424,256]{1,0:T(8,128)(2,1)S(1)}, u32[]{:S(2)}, u32[]{:S(2)}) collective-permute-start(bf16[424,256]{1,0:T(8,128)(2,1)S(1)} %pad_maximum_fusion), channel_id=1, source_target_pairs={{16,0},{17,1},{18,2},{19,3},{20,4},{21,5},{22,6},{23,7},{24,8},{25... | collective-permute-start | bytes 651272 | tf_op jit(solution)/shard_map/ppermute | solution.py:473
  155.7 9.4 %collective-permute-start.45 = (bf16[424,256]{1,0:T(8,128)(2,1)S(1)}, bf16[424,256]{1,0:T(8,128)(2,1)S(1)}, u32[]{:S(2)}, u32[]{:S(2)}) collective-permute-start(bf16[424,256]{1,0:T(8,128)(2,1)S(1)} %pad_maximum_fusion), channel_id=1, source_target_pairs={{24,0},{25,1},{26,2},{27,3},{28,4},{29,5},{30,6},{31,7},{0,8},{1,9... | collective-permute-start | bytes 651272 | tf_op jit(solution)/shard_map/ppermute | solution.py:473
  165.3 13.2 %collective-permute-start.52 = (bf16[1024,256]{1,0:T(8,128)(2,1)S(1)}, bf16[1024,256]{1,0:T(8,128)(2,1)S(1)}, u32[]{:S(2)}, u32[]{:S(2)}) collective-permute-start(bf16[1024,256]{1,0:T(8,128)(2,1)S(1)} %copy-done.35), channel_id=1, source_target_pairs={{1,0},{2,1},{3,2},{0,3},{5,4},{6,5},{7,6},{4,7},{9,8},{10,9},{11,1... | collective-permute-start | bytes 1572872 | tf_op jit(solution)/shard_map/ppermute | solution.py:473
  167.5 13.1 %collective-permute-start.53 = (bf16[1024,256]{1,0:T(8,128)(2,1)S(1)}, bf16[1024,256]{1,0:T(8,128)(2,1)S(1)}, u32[]{:S(2)}, u32[]{:S(2)}) collective-permute-start(bf16[1024,256]{1,0:T(8,128)(2,1)S(1)} %copy-done.34), channel_id=1, source_target_pairs={{3,0},{0,1},{1,2},{2,3},{7,4},{4,5},{5,6},{6,7},{11,8},{8,9},{9,10... | collective-permute-start | bytes 1572872 | tf_op jit(solution)/shard_map/ppermute | solution.py:473
  169.2 9.2 %collective-permute-start.49 = (bf16[168,256]{1,0:T(8,128)(2,1)S(1)}, bf16[168,256]{1,0:T(8,128)(2,1)S(1)}, u32[]{:S(2)}, u32[]{:S(2)}) collective-permute-start(bf16[168,256]{1,0:T(8,128)(2,1)S(1)} %slice.19.t0), channel_id=1, source_target_pairs={{32,0},{33,1},{34,2},{35,3},{36,4},{37,5},{38,6},{39,7},{40,8},{41... | collective-permute-start | bytes 258056 | tf_op jit(solution)/shard_map/ppermute | solution.py:473
  169.8 8.6 %collective-permute-start.50 = (bf16[168,256]{1,0:T(8,128)(2,1)S(1)}, bf16[168,256]{1,0:T(8,128)(2,1)S(1)}, u32[]{:S(2)}, u32[]{:S(2)}) collective-permute-start(bf16[168,256]{1,0:T(8,128)(2,1)S(1)} %slice.19.t0), channel_id=1, source_target_pairs={{64,0},{65,1},{66,2},{67,3},{68,4},{69,5},{70,6},{71,7},{72,8},{73... | collective-permute-start | bytes 258056 | tf_op jit(solution)/shard_map/ppermute | solution.py:473
  172.7 5.7 %collective-permute-start.51 = (bf16[168,256]{1,0:T(8,128)(2,1)S(1)}, bf16[168,256]{1,0:T(8,128)(2,1)S(1)}, u32[]{:S(2)}, u32[]{:S(2)}) collective-permute-start(bf16[168,256]{1,0:T(8,128)(2,1)S(1)} %slice.19.t0), channel_id=1, source_target_pairs={{96,0},{97,1},{98,2},{99,3},{100,4},{101,5},{102,6},{103,7},{104,8... | collective-permute-start | bytes 258056 | tf_op jit(solution)/shard_map/ppermute | solution.py:473
  (42 other events, 267.5 us)

commit v2 on v1

--- a/solution.py
+++ b/solution.py
@@ -117,7 +117,7 @@
         )
         g1[...] = tail[97:98]
         g2[...] = tail[98:99]
-        gout[...] = tail[104:168]
+        gout[...] = tail[112:176]
 
         @pl.when(z[1] == 0)
         def _():
@@ -346,10 +346,10 @@
             ref[64:96, 0:128] = gslice.astype(ref.dtype)
             ref[64:96, 128:256] = qkv[...].astype(ref.dtype)
             wide = jnp.concatenate([gsharp[2 * k : 2 * k + 1], gsharp[2 * k + 1 : 2 * k + 2]], 1)
-            ref[96:104, :] = jnp.concatenate(
-                [wide, gain1, gain2, jnp.zeros((5, C), F32)], 0
+            ref[96:112, :] = jnp.concatenate(
+                [wide, gain1, gain2, jnp.zeros((13, C), F32)], 0
             ).astype(ref.dtype)
-            ref[104:168, :] = gout[k * 64 : (k + 1) * 64, :].astype(ref.dtype)
+            ref[112:176, :] = gout[k * 64 : (k + 1) * 64, :].astype(ref.dtype)
 
 
 def halves(value):
@@ -434,7 +434,7 @@
 
 UP, DOWN, WIN, WOUT, SHARP = (256, 0), (256, 1), (64, 8), (64, 9), (16, 40)
 WIDE, NARROW = 1024, 512
-TAIL = 168
+TAIL = 176
 
 
 def pack_specs(kind):

time: 186 us -> 187 us (level)
  no operation moved by 1% of the time
where the time goes in v2:
time: 187 us; the launch traced here: 186 us
  Pallas kernels  69.3 us (37%)
  starting transfers between devices  68.8 us (37%)
  waiting for transfers between devices  38.5 us (21%)
  local copies, waits for them, and re-layouts  4.28 us (2%)
  other arithmetic  3.59 us (2%)
    ppermute x54, starting transfers between devices, pull(): return lax.ppermute(value, axes, pairs)  68.8 us
    ppermute x54, waiting for transfers between devices, pull(): return lax.ppermute(value, axes, pairs)  38.5 us
    pallas_call x1, Pallas kernels, mlp_call(): pl.pallas_call(mlp_kernel, grid_spec=grid((quarter // size,), [row_spec(s...  16.9 us
    pallas_call x1, Pallas kernels, points_call(): pl.pallas_call(points_kernel, grid_spec=grid((steps,), [row_spec(size, 0)...  13.4 us
    pallas_call x3, Pallas kernels, fill_call(): pl.pallas_call(fill_kernel, grid_spec=grid((n,), [s for _, s in parts] +...  12.7 us
    pallas_call x1, Pallas kernels, local(): pl.pallas_call(own_sums_kernel, grid=(rows // (2 * WIDE),), in_specs=[pl....  8.94 us
    pallas_call x1, Pallas kernels, weights_call(): pl.pallas_call(weights_kernel, grid_spec=grid((quarter // WIDE,), [row_sp...  5.64 us
    unnamed x72, local copies, waits for them, and re-layouts  4.18 us
  transfers between devices with their start and end apart: 54, of which 19 were waited for; matrix products, arithmetic and copies ran while one was open for 2% of the time, Pallas kernels for 20%

profile of v2, /device:TPU:2, one launch (start us, length us, event | category | flops | bytes accessed | tf_op | source)
XLA Modules:
  0.0 185.8 jit_solution(8273955611781282721)
XLA Ops:
  0.6 2.1 %prep.1 = (bf16[656,256]{1,0:T(8,128)(2,1)}, bf16[512,256]{1,0:T(8,128)(2,1)}, bf16[256,512]{1,0:T(8,128)(2,1)}, f32[1,256]{1,0:T(1,128)}, f32[1,256]{1,0:T(1,128)}) custom-call(bf16[256,256]{1,0:T(8,128)(2,1)} %w_up.1, bf16[256,256]{1,0:T(8,128)(2,1)} %w_down.1, bf16[64,256]{1,0:T(8,128)(2,1)} %bitcast.7, bf16[64,256]{1,0:T(8,128)(2,1)} %w_out.1, ...), custom_call_target="tpu_custom_call" | custom-call | flops 2000000 | bytes 1024 | tf_op jit(solution)/shard_map/prep/pallas_call | solution.py:523
  2.7 8.9 %own_sums.1 = f32[40,128]{1,0:T(8,128)} custom-call(bf16[8192,256]{1,0:T(8,128)(2,1)} %pts.7, f32[1,256]{1,0:T(1,128)} %get-tuple-element.135.gain.refs_8_, bf16[656,256]{1,0:T(8,128)(2,1)} %get-tuple-element.143.w_in.sharp.in0.s0.refs_5_.refs_9_.refs_13_.refs_11_.refs_15_, bf16[512,256]{1,0:T(8,128)(2,1)} %get-tuple-element.137.spread_slices.refs_9_, ...), custom_call_target="tpu_custom_call" | custom-call | flops 8000000 | bytes 1024 | tf_op jit(solution)/shard_map/own_sums/pallas_call | solution.py:533
  14.2 1.6 collective-permute-start.3
  15.8 3.3 %collective-permute-start.1 = (f32[40,128]{1,0:T(8,128)S(1)}, f32[40,128]{1,0:T(8,128)S(1)}, u32[]{:S(2)}, u32[]{:S(2)}) collective-permute-start(f32[40,128]{1,0:T(8,128)S(1)} %add.83), channel_id=1, source_target_pairs={{64,0},{65,1},{66,2},{67,3},{68,4},{69,5},{70,6},{71,7},{72,8},{73... | collective-permute-start | bytes 61448 | tf_op jit(solution)/shard_map/ppermute | solution.py:473
  19.2 4.0 %collective-permute-start.10 = (bf16[656,256]{1,0:T(8,128)(2,1)}, bf16[656,256]{1,0:T(8,128)(2,1)S(1)}, u32[]{:S(2)}, u32[]{:S(2)}) collective-permute-start(bf16[656,256]{1,0:T(8,128)(2,1)} %get-tuple-element.143.w_in.sharp.in0.s0.refs_5_.refs_9_.refs_13_.refs_11_.refs_15_), channel_id=1, source_target_pairs={{1,0},{2,1},{3,2},{0,3},{5,4},{6,5},{7,6},{4,7},{9,8},{10,9},{11,1... | collective-permute-start | bytes 1007624 | tf_op jit(solution)/shard_map/ppermute | solution.py:473
  23.2 1.9 %collective-permute-start.11 = (bf16[656,256]{1,0:T(8,128)(2,1)}, bf16[656,256]{1,0:T(8,128)(2,1)S(1)}, u32[]{:S(2)}, u32[]{:S(2)}) collective-permute-start(bf16[656,256]{1,0:T(8,128)(2,1)} %get-tuple-element.143.w_in.sharp.in0.s0.refs_5_.refs_9_.refs_13_.refs_11_.refs_15_), channel_id=1, source_target_pairs={{2,0},{3,1},{0,2},{1,3},{6,4},{7,5},{4,6},{5,7},{10,8},{11,9},{8,1... | collective-permute-start | bytes 1007624 | tf_op jit(solution)/shard_map/ppermute | solution.py:473
  25.2 3.0 %collective-permute-start.4 = (f32[40,128]{1,0:T(8,128)S(1)}, f32[40,128]{1,0:T(8,128)S(1)}, u32[]{:S(2)}, u32[]{:S(2)}) collective-permute-start(f32[40,128]{1,0:T(8,128)S(1)} %add_add_fusion.3.a), channel_id=1, source_target_pairs={{8,0},{9,1},{10,2},{11,3},{12,4},{13,5},{14,6},{15,7},{16,8},{17,9... | collective-permute-start | bytes 61448 | tf_op jit(solution)/shard_map/ppermute | solution.py:473
  30.5 2.9 %collective-permute-done.5.c = f32[40,128]{1,0:T(8,128)S(1)} collective-permute-done((f32[40,128]{1,0:T(8,128)S(1)}, f32[40,128]{1,0:T(8,128)S(1)}, u32[]{:S(2)}, u32[]{:S(2)}) %collective-permute-start.5) | collective-permute-done | bytes 20512 | tf_op jit(solution)/shard_map/ppermute | solution.py:473
  33.5 1.5 collective-permute-done.6.d
  35.6 2.4 %tokens.1 = (f32[40,128]{1,0:T(8,128)}, f32[32,128]{1,0:T(8,128)}) custom-call(f32[40,128]{1,0:T(8,128)} %copy-done.20, f32[40,128]{1,0:T(8,128)} %copy-done.28, f32[40,128]{1,0:T(8,128)} %copy-done.29, f32[40,128]{1,0:T(8,128)} %copy-done.30, bf16[32,32]{1,0:T(8,128)(2,1)} %wq.3, bf16[32,32]{1,0:T(8,128)(2,1)} %wk.3, bf16[32,32]{1,0:T(8,128)(2,1)} %wv.3), custom_call_target="tpu_custom_call" | custom-call | flops 3000000 | bytes 1024 | tf_op jit(solution)/shard_map/tokens/pallas_call | solution.py:680
  39.4 2.8 %collective-permute-start.8 = (f32[32,128]{1,0:T(8,128)}, f32[32,128]{1,0:T(8,128)S(1)}, u32[]{:S(2)}, u32[]{:S(2)}) collective-permute-start(f32[32,128]{1,0:T(8,128)} %get-tuple-element.150.refs_0_), channel_id=1, source_target_pairs={{2,0},{3,1},{0,2},{1,3},{6,4},{7,5},{4,6},{5,7},{10,8},{11,9},{8,1... | collective-permute-start | bytes 49160 | tf_op jit(solution)/shard_map/ppermute | solution.py:473
  44.4 5.6 %weights.1 = (bf16[512,2048]{1,0:T(8,128)(2,1)}, bf16[2048,256]{1,0:T(8,128)(2,1)}) custom-call(s32[2]{0:T(128)} %pad_add_fusion.z, bf16[8192,256]{1,0:T(8,128)(2,1)} %pts.7, f32[1,256]{1,0:T(1,128)} %get-tuple-element.135.gain.refs_8_, bf16[656,256]{1,0:T(8,128)(2,1)} %get-tuple-element.143.w_in.sharp.in0.s0.refs_5_.refs_9_.refs_13_.refs_11_.refs_15_, ...), custom_call_target="tpu_custom_call" | custom-call | flops 5000000 | bytes 1024 | tf_op jit(solution)/shard_map/weights/pallas_call | solution.py:554
  50.7 16.9 %mlp.1 = (f32[8192,256]{1,0:T(8,128)}, bf16[2048,256]{1,0:T(8,128)(2,1)}, bf16[2048,256]{1,0:T(8,128)(2,1)}, bf16[2048,256]{1,0:T(8,128)(2,1)}, f32[32,128]{1,0:...) custom-call(s32[2]{0:T(128)} %pad_add_fusion.z, ...), custom_call_target="tpu_custom_call" | custom-call | flops 16000000 | bytes 1024 | tf_op jit(solution)/shard_map/mlp/pallas_call | solution.py:580
  67.7 3.2 %collective-permute-start.14 = (f32[32,128]{1,0:T(8,128)}, f32[32,128]{1,0:T(8,128)S(1)}, u32[]{:S(2)}, u32[]{:S(2)}) collective-permute-start(f32[32,128]{1,0:T(8,128)} %get-tuple-element.160), channel_id=1, source_target_pairs={{1,0},{2,1},{3,2},{0,3},{5,4},{6,5},{7,6},{4,7},{9,8},{10,9},{11,1... | collective-permute-start | bytes 49160 | tf_op jit(solution)/shard_map/ppermute | solution.py:473
  70.9 1.5 collective-permute-start.13
  72.4 1.7 collective-permute-start.20
  74.1 2.9 %collective-permute-start.21 = (bf16[512,256]{1,0:T(8,128)(2,1)}, bf16[512,256]{1,0:T(8,128)(2,1)S(1)}, u32[]{:S(2)}, u32[]{:S(2)}) collective-permute-start(bf16[512,256]{1,0:T(8,128)(2,1)} %get-tuple-element.167), channel_id=1, source_target_pairs={{2,0},{3,1},{0,2},{1,3},{6,4},{7,5},{4,6},{5,7},{10,8},{11,9},{8,1... | collective-permute-start | bytes 786440 | tf_op jit(solution)/shard_map/ppermute | solution.py:473
  79.3 1.9 %collective-permute-start.18 = (f32[32,128]{1,0:T(8,128)S(1)}, f32[32,128]{1,0:T(8,128)S(1)}, u32[]{:S(2)}, u32[]{:S(2)}) collective-permute-start(f32[32,128]{1,0:T(8,128)S(1)} %add.90), channel_id=1, source_target_pairs={{64,0},{65,1},{66,2},{67,3},{68,4},{69,5},{70,6},{71,7},{72,8},{73... | collective-permute-start | bytes 49160 | tf_op jit(solution)/shard_map/ppermute | solution.py:473
  81.2 1.6 collective-permute-done.17
  84.6 3.1 %collective-permute-start.30 = (bf16[2048,256]{1,0:T(8,128)(2,1)}, bf16[2048,256]{1,0:T(8,128)(2,1)S(1)}, u32[]{:S(2)}, u32[]{:S(2)}) collective-permute-start(bf16[2048,256]{1,0:T(8,128)(2,1)} %get-tuple-element.183), channel_id=1, source_target_pairs={{1,0},{2,1},{3,2},{0,3},{5,4},{6,5},{7,6},{4,7},{9,8},{10,9},{11,1... | collective-permute-start | bytes 3145736 | tf_op jit(solution)/shard_map/ppermute | solution.py:473
  87.7 2.3 %collective-permute-start.23 = (f32[32,128]{1,0:T(8,128)S(1)}, f32[32,128]{1,0:T(8,128)S(1)}, u32[]{:S(2)}, u32[]{:S(2)}) collective-permute-start(f32[32,128]{1,0:T(8,128)S(1)} %add_add_fusion.4.a), channel_id=1, source_target_pairs={{8,0},{9,1},{10,2},{11,3},{12,4},{13,5},{14,6},{15,7},{16,8},{17,9... | collective-permute-start | bytes 49160 | tf_op jit(solution)/shard_map/ppermute | solution.py:473
  92.3 3.0 %collective-permute-done.24.c = f32[32,128]{1,0:T(8,128)S(1)} collective-permute-done((f32[32,128]{1,0:T(8,128)S(1)}, f32[32,128]{1,0:T(8,128)S(1)}, u32[]{:S(2)}, u32[]{:S(2)}) %collective-permute-start.24) | collective-permute-done | bytes 16416 | tf_op jit(solution)/shard_map/ppermute | solution.py:473
  95.9 3.3 %tokens_back.1 = (f32[40,128]{1,0:T(8,128)}, f32[32,128]{1,0:T(8,128)}) custom-call(f32[40,128]{1,0:T(8,128)} %get-tuple-element.157.nd, f32[32,128]{1,0:T(8,128)} %copy-done.24, f32[32,128]{1,0:T(8,128)} %copy-done.31, f32[32,128]{1,0:T(8,128)} %copy-done.32, f32[32,128]{1,0:T(8,128)} %copy-done.33, bf16[32,32]{1,0:T(8,128)(2,1)} %wq.3, bf16[32,32]{1,0:T(8,128)(2,1)} %wk.3, ...), custom_call_target="tpu_custom_call" | custom-call | flops 4000000 | bytes 1024 | tf_op jit(solution)/shard_map/tokens_back/pallas_call | solution.py:712
  99.2 3.2 %collective-permute-start.26 = (f32[40,128]{1,0:T(8,128)}, f32[40,128]{1,0:T(8,128)S(1)}, u32[]{:S(2)}, u32[]{:S(2)}) collective-permute-start(f32[40,128]{1,0:T(8,128)} %get-tuple-element.177.refs_4_), channel_id=1, source_target_pairs={{1,0},{2,1},{3,2},{0,3},{5,4},{6,5},{7,6},{4,7},{9,8},{10,9},{11,1... | collective-permute-start | bytes 61448 | tf_op jit(solution)/shard_map/ppermute | solution.py:473
  102.4 1.7 collective-permute-start.27
  104.1 6.0 %collective-permute-done.26.refs_5_ = f32[40,128]{1,0:T(8,128)S(1)} collective-permute-done((f32[40,128]{1,0:T(8,128)}, f32[40,128]{1,0:T(8,128)S(1)}, u32[]{:S(2)}, u32[]{:S(2)}) %collective-permute-start.26) | collective-permute-done | bytes 20512 | tf_op jit(solution)/shard_map/ppermute | solution.py:473
  110.2 3.3 %collective-permute-done.27.refs_6_ = f32[40,128]{1,0:T(8,128)S(1)} collective-permute-done((f32[40,128]{1,0:T(8,128)}, f32[40,128]{1,0:T(8,128)S(1)}, u32[]{:S(2)}, u32[]{:S(2)}) %collective-permute-start.27) | collective-permute-done | bytes 20512 | tf_op jit(solution)/shard_map/ppermute | solution.py:473
  114.3 1.5 collective-permute-start.36
  115.9 2.9 %collective-permute-start.32 = (bf16[256,256]{1,0:T(8,128)(2,1)S(1)}, bf16[256,256]{1,0:T(8,128)(2,1)S(1)}, u32[]{:S(2)}, u32[]{:S(2)}) collective-permute-start(bf16[256,256]{1,0:T(8,128)(2,1)S(1)} %fusion.1), channel_id=1, source_target_pairs={{32,0},{33,1},{34,2},{35,3},{36,4},{37,5},{38,6},{39,7},{40,8},{41... | collective-permute-start | bytes 393224 | tf_op jit(solution)/shard_map/ppermute | solution.py:473
  119.3 1.8 collective-permute-start.34
  121.1 13.4 %points.1 = (f32[8192,256]{1,0:T(8,128)}, bf16[1024,256]{1,0:T(8,128)(2,1)}, bf16[1024,256]{1,0:T(8,128)(2,1)}, f32[176,256]{1,0:T(8,128)}, bf16[176,256]{1,0:T(...) custom-call(s32[2]{0:T(128)} %pad_add_fusion.z, bf16[8192,256]{1,0:T(8,128)(2,1)} %pts.7, ...), custom_call_target="tpu_custom_call" | custom-call | flops 12000000 | bytes 1024 | tf_op jit(solution)/shard_map/points/pallas_call | solution.py:611
  134.5 2.0 %collective-permute-start.37 = (bf16[176,256]{1,0:T(8,128)(2,1)}, bf16[176,256]{1,0:T(8,128)(2,1)S(1)}, u32[]{:S(2)}, u32[]{:S(2)}) collective-permute-start(bf16[176,256]{1,0:T(8,128)(2,1)} %get-tuple-element.204), channel_id=1, source_target_pairs={{1,0},{2,1},{3,2},{0,3},{5,4},{6,5},{7,6},{4,7},{9,8},{10,9},{11,1... | collective-permute-start | bytes 270344 | tf_op jit(solution)/shard_map/ppermute | solution.py:473
  137.6 2.4 %collective-permute-start.41 = (bf16[1024,256]{1,0:T(8,128)(2,1)}, bf16[1024,256]{1,0:T(8,128)(2,1)S(1)}, u32[]{:S(2)}, u32[]{:S(2)}) collective-permute-start(bf16[1024,256]{1,0:T(8,128)(2,1)} %get-tuple-element.235), channel_id=1, source_target_pairs={{1,0},{2,1},{3,2},{0,3},{5,4},{6,5},{7,6},{4,7},{9,8},{10,9},{11,1... | collective-permute-start | bytes 1572872 | tf_op jit(solution)/shard_map/ppermute | solution.py:473
  140.1 4.7 %fill.3.refs_2_ = f32[8192,256]{1,0:T(8,128)} custom-call(s32[2]{0:T(128)} %pad_add_fusion.z, bf16[2048,256]{1,0:T(8,128)(2,1)} %copy-done.3, bf16[2048,256]{1,0:T(8,128)(2,1)} %copy-done.3, bf16[1024,256]{1,0:T(8,128)(2,1)} %copy-done.8, bf16[1024,256]{1,0:T(8,128)(2,1)} %copy-done.9, ...), custom_call_target="tpu_custom_call", output_to_operand_aliasing={{}: (5, {})} | custom-call | flops 3000000 | bytes 1024 | tf_op jit(solution)/shard_map/fill/pallas_call | solution.py:656
  146.4 2.6 %collective-permute-done.41.refs_0_ = bf16[1024,256]{1,0:T(8,128)(2,1)S(1)} collective-permute-done((bf16[1024,256]{1,0:T(8,128)(2,1)}, bf16[1024,256]{1,0:T(8,128)(2,1)S(1)}, u32[]{:S(2)}, u32[]{:S(2)}) %collective-permute-start.41) | collective-permute-done | bytes 524320 | tf_op jit(solution)/shard_map/ppermute | solution.py:473
  149.0 2.8 %collective-permute-done.42.refs_3_ = bf16[1024,256]{1,0:T(8,128)(2,1)S(1)} collective-permute-done((bf16[1024,256]{1,0:T(8,128)(2,1)}, bf16[1024,256]{1,0:T(8,128)(2,1)S(1)}, u32[]{:S(2)}, u32[]{:S(2)}) %collective-permute-start.42) | collective-permute-done | bytes 524320 | tf_op jit(solution)/shard_map/ppermute | solution.py:473
  152.1 1.7 collective-permute-start.47
  153.8 2.0 %collective-permute-start.43 = (bf16[432,256]{1,0:T(8,128)(2,1)S(1)}, bf16[432,256]{1,0:T(8,128)(2,1)S(1)}, u32[]{:S(2)}, u32[]{:S(2)}) collective-permute-start(bf16[432,256]{1,0:T(8,128)(2,1)S(1)} %pad_maximum_fusion), channel_id=1, source_target_pairs={{8,0},{9,1},{10,2},{11,3},{12,4},{13,5},{14,6},{15,7},{16,8},{17,9... | collective-permute-start | bytes 663560 | tf_op jit(solution)/shard_map/ppermute | solution.py:473
  156.7 3.3 %fill.4 = f32[8192,256]{1,0:T(8,128)} custom-call(s32[2]{0:T(128)} %pad_add_fusion.z, bf16[2048,256]{1,0:T(8,128)(2,1)} %copy-done.4, bf16[2048,256]{1,0:T(8,128)(2,1)} %copy-done.4, f32[8192,256]{1,0:T(8,128)} %fill.3.refs_2_), custom_call_target="tpu_custom_call", output_to_operand_aliasing={{}: (3, {})} | custom-call | flops 3000000 | bytes 1024 | tf_op jit(solution)/shard_map/fill/pallas_call | solution.py:656
  159.9 1.7 collective-permute-done.43
  161.6 1.7 collective-permute-done.44
  163.3 2.0 %collective-permute-done.45 = bf16[432,256]{1,0:T(8,128)(2,1)S(1)} collective-permute-done((bf16[432,256]{1,0:T(8,128)(2,1)S(1)}, bf16[432,256]{1,0:T(8,128)(2,1)S(1)}, u32[]{:S(2)}, u32[]{:S(2)}) %collective-permute-start.45) | collective-permute-done | bytes 221216 | tf_op jit(solution)/shard_map/ppermute | solution.py:473
  165.5 2.3 %collective-permute-start.52 = (bf16[1024,256]{1,0:T(8,128)(2,1)S(1)}, bf16[1024,256]{1,0:T(8,128)(2,1)S(1)}, u32[]{:S(2)}, u32[]{:S(2)}) collective-permute-start(bf16[1024,256]{1,0:T(8,128)(2,1)S(1)} %copy-done.35), channel_id=1, source_target_pairs={{1,0},{2,1},{3,2},{0,3},{5,4},{6,5},{7,6},{4,7},{9,8},{10,9},{11,1... | collective-permute-start | bytes 1572872 | tf_op jit(solution)/shard_map/ppermute | solution.py:473
  167.9 1.5 collective-permute-done.48.w1
  170.0 3.0 %collective-permute-start.50 = (bf16[176,256]{1,0:T(8,128)(2,1)S(1)}, bf16[176,256]{1,0:T(8,128)(2,1)S(1)}, u32[]{:S(2)}, u32[]{:S(2)}) collective-permute-start(bf16[176,256]{1,0:T(8,128)(2,1)S(1)} %slice.19.t0), channel_id=1, source_target_pairs={{64,0},{65,1},{66,2},{67,3},{68,4},{69,5},{70,6},{71,7},{72,8},{73... | collective-permute-start | bytes 270344 | tf_op jit(solution)/shard_map/ppermute | solution.py:473
  173.8 4.7 %fill.5.before = f32[8192,256]{1,0:T(8,128)} custom-call(s32[2]{0:T(128)} %pad_add_fusion.z, bf16[1024,256]{1,0:T(8,128)(2,1)} %copy-done.6, bf16[1024,256]{1,0:T(8,128)(2,1)} %copy-done.10, bf16[1024,256]{1,0:T(8,128)(2,1)} %copy-done.11, bf16[1024,256]{1,0:T(8,128)(2,1)} %copy-done.7, ...), custom_call_target="tpu_custom_call", output_to_operand_aliasing={{}: (5, {})} | custom-call | flops 3000000 | bytes 1024 | tf_op jit(solution)/shard_map/fill/pallas_call | solution.py:656
  178.6 2.2 %collective-permute-done.53.second = bf16[1024,256]{1,0:T(8,128)(2,1)S(1)} collective-permute-done((bf16[1024,256]{1,0:T(8,128)(2,1)S(1)}, bf16[1024,256]{1,0:T(8,128)(2,1)S(1)}, u32[]{:S(2)}, u32[]{:S(2)}) %collective-permute-start.53) | collective-permute-done | bytes 524320 | tf_op jit(solution)/shard_map/ppermute | solution.py:473
  181.6 4.0 %finish.1 = (f32[8192,256]{1,0:T(8,128)}, f32[64,256]{1,0:T(8,128)}, f32[32,64]{1,0:T(8,128)}, f32[1,2]{1,0:T(1,128)}, f32[32,32]{1,0:T(8,128)}, /*index=5*/f32[...) custom-call(s32[2]{0:T(128)} %pad_add_fusion.z, ...), custom_call_target="tpu_custom_call", output_to_operand_aliasing={{0}: (3, {})} | custom-call | flops 4000000 | bytes 1024 | tf_op jit(solution)/shard_map/finish/pallas_call | solution.py:764
  (160 shorter events, 24.6 us)
Async XLA Ops:
  13.8 9.4 %collective-permute-start.2 = (f32[40,128]{1,0:T(8,128)S(1)}, f32[40,128]{1,0:T(8,128)S(1)}, u32[]{:S(2)}, u32[]{:S(2)}) collective-permute-start(f32[40,128]{1,0:T(8,128)S(1)} %add.83), channel_id=1, source_target_pairs={{32,0},{33,1},{34,2},{35,3},{36,4},{37,5},{38,6},{39,7},{40,8},{41... | collective-permute-start | bytes 61448 | tf_op jit(solution)/shard_map/ppermute | solution.py:473
  14.2 9.0 %collective-permute-start.3 = (f32[40,128]{1,0:T(8,128)S(1)}, f32[40,128]{1,0:T(8,128)S(1)}, u32[]{:S(2)}, u32[]{:S(2)}) collective-permute-start(f32[40,128]{1,0:T(8,128)S(1)} %add.83), channel_id=1, source_target_pairs={{96,0},{97,1},{98,2},{99,3},{100,4},{101,5},{102,6},{103,7},{104,8... | collective-permute-start | bytes 61448 | tf_op jit(solution)/shard_map/ppermute | solution.py:473
  15.8 7.4 %collective-permute-start.1 = (f32[40,128]{1,0:T(8,128)S(1)}, f32[40,128]{1,0:T(8,128)S(1)}, u32[]{:S(2)}, u32[]{:S(2)}) collective-permute-start(f32[40,128]{1,0:T(8,128)S(1)} %add.83), channel_id=1, source_target_pairs={{64,0},{65,1},{66,2},{67,3},{68,4},{69,5},{70,6},{71,7},{72,8},{73... | collective-permute-start | bytes 61448 | tf_op jit(solution)/shard_map/ppermute | solution.py:473
  19.2 23.1 %collective-permute-start.10 = (bf16[656,256]{1,0:T(8,128)(2,1)}, bf16[656,256]{1,0:T(8,128)(2,1)S(1)}, u32[]{:S(2)}, u32[]{:S(2)}) collective-permute-start(bf16[656,256]{1,0:T(8,128)(2,1)} %get-tuple-element.143.w_in.sharp.in0.s0.refs_5_.refs_9_.refs_13_.refs_11_.refs_15_), channel_id=1, source_target_pairs={{1,0},{2,1},{3,2},{0,3},{5,4},{6,5},{7,6},{4,7},{9,8},{10,9},{11,1... | collective-permute-start | bytes 1007624 | tf_op jit(solution)/shard_map/ppermute | solution.py:473
  23.2 19.7 %collective-permute-start.12 = (bf16[656,256]{1,0:T(8,128)(2,1)}, bf16[656,256]{1,0:T(8,128)(2,1)S(1)}, u32[]{:S(2)}, u32[]{:S(2)}) collective-permute-start(bf16[656,256]{1,0:T(8,128)(2,1)} %get-tuple-element.143.w_in.sharp.in0.s0.refs_5_.refs_9_.refs_13_.refs_11_.refs_15_), channel_id=1, source_target_pairs={{3,0},{0,1},{1,2},{2,3},{7,4},{4,5},{5,6},{6,7},{11,8},{8,9},{9,10... | collective-permute-start | bytes 1007624 | tf_op jit(solution)/shard_map/ppermute | solution.py:473
  23.2 19.7 %collective-permute-start.11 = (bf16[656,256]{1,0:T(8,128)(2,1)}, bf16[656,256]{1,0:T(8,128)(2,1)S(1)}, u32[]{:S(2)}, u32[]{:S(2)}) collective-permute-start(bf16[656,256]{1,0:T(8,128)(2,1)} %get-tuple-element.143.w_in.sharp.in0.s0.refs_5_.refs_9_.refs_13_.refs_11_.refs_15_), channel_id=1, source_target_pairs={{2,0},{3,1},{0,2},{1,3},{6,4},{7,5},{4,6},{5,7},{10,8},{11,9},{8,1... | collective-permute-start | bytes 1007624 | tf_op jit(solution)/shard_map/ppermute | solution.py:473
  28.2 5.3 %collective-permute-start.5 = (f32[40,128]{1,0:T(8,128)S(1)}, f32[40,128]{1,0:T(8,128)S(1)}, u32[]{:S(2)}, u32[]{:S(2)}) collective-permute-start(f32[40,128]{1,0:T(8,128)S(1)} %add_add_fusion.3.a), channel_id=1, source_target_pairs={{16,0},{17,1},{18,2},{19,3},{20,4},{21,5},{22,6},{23,7},{24,8},{25... | collective-permute-start | bytes 61448 | tf_op jit(solution)/shard_map/ppermute | solution.py:473
  29.7 5.3 %collective-permute-start.6 = (f32[40,128]{1,0:T(8,128)S(1)}, f32[40,128]{1,0:T(8,128)S(1)}, u32[]{:S(2)}, u32[]{:S(2)}) collective-permute-start(f32[40,128]{1,0:T(8,128)S(1)} %add_add_fusion.3.a), channel_id=1, source_target_pairs={{24,0},{25,1},{26,2},{27,3},{28,4},{29,5},{30,6},{31,7},{0,8},{1,9... | collective-permute-start | bytes 61448 | tf_op jit(solution)/shard_map/ppermute | solution.py:473
  37.9 12.1 %collective-permute-start.7 = (f32[32,128]{1,0:T(8,128)}, f32[32,128]{1,0:T(8,128)S(1)}, u32[]{:S(2)}, u32[]{:S(2)}) collective-permute-start(f32[32,128]{1,0:T(8,128)} %get-tuple-element.150.refs_0_), channel_id=1, source_target_pairs={{1,0},{2,1},{3,2},{0,3},{5,4},{6,5},{7,6},{4,7},{9,8},{10,9},{11,1... | collective-permute-start | bytes 49160 | tf_op jit(solution)/shard_map/ppermute | solution.py:473
  39.4 10.7 %collective-permute-start.8 = (f32[32,128]{1,0:T(8,128)}, f32[32,128]{1,0:T(8,128)S(1)}, u32[]{:S(2)}, u32[]{:S(2)}) collective-permute-start(f32[32,128]{1,0:T(8,128)} %get-tuple-element.150.refs_0_), channel_id=1, source_target_pairs={{2,0},{3,1},{0,2},{1,3},{6,4},{7,5},{4,6},{5,7},{10,8},{11,9},{8,1... | collective-permute-start | bytes 49160 | tf_op jit(solution)/shard_map/ppermute | solution.py:473
  42.2 7.8 %collective-permute-start.9 = (f32[32,128]{1,0:T(8,128)}, f32[32,128]{1,0:T(8,128)S(1)}, u32[]{:S(2)}, u32[]{:S(2)}) collective-permute-start(f32[32,128]{1,0:T(8,128)} %get-tuple-element.150.refs_0_), channel_id=1, source_target_pairs={{3,0},{0,1},{1,2},{2,3},{7,4},{4,5},{5,6},{6,7},{11,8},{8,9},{9,10... | collective-permute-start | bytes 49160 | tf_op jit(solution)/shard_map/ppermute | solution.py:473
  67.7 9.4 %collective-permute-start.14 = (f32[32,128]{1,0:T(8,128)}, f32[32,128]{1,0:T(8,128)S(1)}, u32[]{:S(2)}, u32[]{:S(2)}) collective-permute-start(f32[32,128]{1,0:T(8,128)} %get-tuple-element.160), channel_id=1, source_target_pairs={{1,0},{2,1},{3,2},{0,3},{5,4},{6,5},{7,6},{4,7},{9,8},{10,9},{11,1... | collective-permute-start | bytes 49160 | tf_op jit(solution)/shard_map/ppermute | solution.py:473
  70.9 6.2 %collective-permute-start.15 = (f32[32,128]{1,0:T(8,128)}, f32[32,128]{1,0:T(8,128)S(1)}, u32[]{:S(2)}, u32[]{:S(2)}) collective-permute-start(f32[32,128]{1,0:T(8,128)} %get-tuple-element.161), channel_id=1, source_target_pairs={{3,0},{0,1},{1,2},{2,3},{7,4},{4,5},{5,6},{6,7},{11,8},{8,9},{9,10... | collective-permute-start | bytes 49160 | tf_op jit(solution)/shard_map/ppermute | solution.py:473
  70.9 6.2 %collective-permute-start.13 = (f32[32,128]{1,0:T(8,128)}, f32[32,128]{1,0:T(8,128)S(1)}, u32[]{:S(2)}, u32[]{:S(2)}) collective-permute-start(f32[32,128]{1,0:T(8,128)} %get-tuple-element.159), channel_id=1, source_target_pairs={{2,0},{3,1},{0,2},{1,3},{6,4},{7,5},{4,6},{5,7},{10,8},{11,9},{8,1... | collective-permute-start | bytes 49160 | tf_op jit(solution)/shard_map/ppermute | solution.py:473
  72.4 15.3 %collective-permute-start.20 = (bf16[512,256]{1,0:T(8,128)(2,1)}, bf16[512,256]{1,0:T(8,128)(2,1)S(1)}, u32[]{:S(2)}, u32[]{:S(2)}) collective-permute-start(bf16[512,256]{1,0:T(8,128)(2,1)} %get-tuple-element.166), channel_id=1, source_target_pairs={{1,0},{2,1},{3,2},{0,3},{5,4},{6,5},{7,6},{4,7},{9,8},{10,9},{11,1... | collective-permute-start | bytes 786440 | tf_op jit(solution)/shard_map/ppermute | solution.py:473
  74.1 13.6 %collective-permute-start.21 = (bf16[512,256]{1,0:T(8,128)(2,1)}, bf16[512,256]{1,0:T(8,128)(2,1)S(1)}, u32[]{:S(2)}, u32[]{:S(2)}) collective-permute-start(bf16[512,256]{1,0:T(8,128)(2,1)} %get-tuple-element.167), channel_id=1, source_target_pairs={{2,0},{3,1},{0,2},{1,3},{6,4},{7,5},{4,6},{5,7},{10,8},{11,9},{8,1... | collective-permute-start | bytes 786440 | tf_op jit(solution)/shard_map/ppermute | solution.py:473
  77.8 9.9 %collective-permute-start.22 = (bf16[512,256]{1,0:T(8,128)(2,1)}, bf16[512,256]{1,0:T(8,128)(2,1)S(1)}, u32[]{:S(2)}, u32[]{:S(2)}) collective-permute-start(bf16[512,256]{1,0:T(8,128)(2,1)} %get-tuple-element.168), channel_id=1, source_target_pairs={{3,0},{0,1},{1,2},{2,3},{7,4},{4,5},{5,6},{6,7},{11,8},{8,9},{9,10... | collective-permute-start | bytes 786440 | tf_op jit(solution)/shard_map/ppermute | solution.py:473
  79.3 5.2 %collective-permute-start.18 = (f32[32,128]{1,0:T(8,128)S(1)}, f32[32,128]{1,0:T(8,128)S(1)}, u32[]{:S(2)}, u32[]{:S(2)}) collective-permute-start(f32[32,128]{1,0:T(8,128)S(1)} %add.90), channel_id=1, source_target_pairs={{64,0},{65,1},{66,2},{67,3},{68,4},{69,5},{70,6},{71,7},{72,8},{73... | collective-permute-start | bytes 49160 | tf_op jit(solution)/shard_map/ppermute | solution.py:473
  82.8 4.8 %collective-permute-start.19 = (f32[32,128]{1,0:T(8,128)S(1)}, f32[32,128]{1,0:T(8,128)S(1)}, u32[]{:S(2)}, u32[]{:S(2)}) collective-permute-start(f32[32,128]{1,0:T(8,128)S(1)} %add.90), channel_id=1, source_target_pairs={{96,0},{97,1},{98,2},{99,3},{100,4},{101,5},{102,6},{103,7},{104,8... | collective-permute-start | bytes 49160 | tf_op jit(solution)/shard_map/ppermute | solution.py:473
  84.6 29.0 %collective-permute-start.30 = (bf16[2048,256]{1,0:T(8,128)(2,1)}, bf16[2048,256]{1,0:T(8,128)(2,1)S(1)}, u32[]{:S(2)}, u32[]{:S(2)}) collective-permute-start(bf16[2048,256]{1,0:T(8,128)(2,1)} %get-tuple-element.183), channel_id=1, source_target_pairs={{1,0},{2,1},{3,2},{0,3},{5,4},{6,5},{7,6},{4,7},{9,8},{10,9},{11,1... | collective-permute-start | bytes 3145736 | tf_op jit(solution)/shard_map/ppermute | solution.py:473
  87.7 25.9 %collective-permute-start.31 = (bf16[2048,256]{1,0:T(8,128)(2,1)}, bf16[2048,256]{1,0:T(8,128)(2,1)S(1)}, u32[]{:S(2)}, u32[]{:S(2)}) collective-permute-start(bf16[2048,256]{1,0:T(8,128)(2,1)} %get-tuple-element.183), channel_id=1, source_target_pairs={{3,0},{0,1},{1,2},{2,3},{7,4},{4,5},{5,6},{6,7},{11,8},{8,9},{9,10... | collective-permute-start | bytes 3145736 | tf_op jit(solution)/shard_map/ppermute | solution.py:473
  87.7 4.6 %collective-permute-start.23 = (f32[32,128]{1,0:T(8,128)S(1)}, f32[32,128]{1,0:T(8,128)S(1)}, u32[]{:S(2)}, u32[]{:S(2)}) collective-permute-start(f32[32,128]{1,0:T(8,128)S(1)} %add_add_fusion.4.a), channel_id=1, source_target_pairs={{8,0},{9,1},{10,2},{11,3},{12,4},{13,5},{14,6},{15,7},{16,8},{17,9... | collective-permute-start | bytes 49160 | tf_op jit(solution)/shard_map/ppermute | solution.py:473
  90.0 5.2 %collective-permute-start.24 = (f32[32,128]{1,0:T(8,128)S(1)}, f32[32,128]{1,0:T(8,128)S(1)}, u32[]{:S(2)}, u32[]{:S(2)}) collective-permute-start(f32[32,128]{1,0:T(8,128)S(1)} %add_add_fusion.4.a), channel_id=1, source_target_pairs={{16,0},{17,1},{18,2},{19,3},{20,4},{21,5},{22,6},{23,7},{24,8},{25... | collective-permute-start | bytes 49160 | tf_op jit(solution)/shard_map/ppermute | solution.py:473
  90.1 5.1 %collective-permute-start.25 = (f32[32,128]{1,0:T(8,128)S(1)}, f32[32,128]{1,0:T(8,128)S(1)}, u32[]{:S(2)}, u32[]{:S(2)}) collective-permute-start(f32[32,128]{1,0:T(8,128)S(1)} %add_add_fusion.4.a), channel_id=1, source_target_pairs={{24,0},{25,1},{26,2},{27,3},{28,4},{29,5},{30,6},{31,7},{0,8},{1,9... | collective-permute-start | bytes 49160 | tf_op jit(solution)/shard_map/ppermute | solution.py:473
  99.2 4.9 %collective-permute-start.29 = (bf16[512,256]{1,0:T(8,128)(2,1)S(1)}, bf16[512,256]{1,0:T(8,128)(2,1)S(1)}, u32[]{:S(2)}, u32[]{:S(2)}) collective-permute-start(bf16[512,256]{1,0:T(8,128)(2,1)S(1)} %get-tuple-element.179), channel_id=1, source_target_pairs={{4,0},{5,1},{6,2},{7,3},{0,4},{1,5},{2,6},{3,7},{12,8},{13,9},{14,... | collective-permute-start | bytes 786440 | tf_op jit(solution)/shard_map/ppermute | solution.py:473
  99.2 11.0 %collective-permute-start.26 = (f32[40,128]{1,0:T(8,128)}, f32[40,128]{1,0:T(8,128)S(1)}, u32[]{:S(2)}, u32[]{:S(2)}) collective-permute-start(f32[40,128]{1,0:T(8,128)} %get-tuple-element.177.refs_4_), channel_id=1, source_target_pairs={{1,0},{2,1},{3,2},{0,3},{5,4},{6,5},{7,6},{4,7},{9,8},{10,9},{11,1... | collective-permute-start | bytes 61448 | tf_op jit(solution)/shard_map/ppermute | solution.py:473
  102.4 11.1 %collective-permute-start.27 = (f32[40,128]{1,0:T(8,128)}, f32[40,128]{1,0:T(8,128)S(1)}, u32[]{:S(2)}, u32[]{:S(2)}) collective-permute-start(f32[40,128]{1,0:T(8,128)} %get-tuple-element.177.refs_4_), channel_id=1, source_target_pairs={{2,0},{3,1},{0,2},{1,3},{6,4},{7,5},{4,6},{5,7},{10,8},{11,9},{8,1... | collective-permute-start | bytes 61448 | tf_op jit(solution)/shard_map/ppermute | solution.py:473
  104.1 9.5 %collective-permute-start.28 = (f32[40,128]{1,0:T(8,128)}, f32[40,128]{1,0:T(8,128)S(1)}, u32[]{:S(2)}, u32[]{:S(2)}) collective-permute-start(f32[40,128]{1,0:T(8,128)} %get-tuple-element.177.refs_4_), channel_id=1, source_target_pairs={{3,0},{0,1},{1,2},{2,3},{7,4},{4,5},{5,6},{6,7},{11,8},{8,9},{9,10... | collective-permute-start | bytes 61448 | tf_op jit(solution)/shard_map/ppermute | solution.py:473
  113.7 20.8 %collective-permute-start.35 = (bf16[1024,256]{1,0:T(8,128)(2,1)S(1)}, bf16[1024,256]{1,0:T(8,128)(2,1)S(1)}, u32[]{:S(2)}, u32[]{:S(2)}) collective-permute-start(bf16[1024,256]{1,0:T(8,128)(2,1)S(1)} %slice.13), channel_id=1, source_target_pairs={{1,0},{2,1},{3,2},{0,3},{5,4},{6,5},{7,6},{4,7},{9,8},{10,9},{11,1... | collective-permute-start | bytes 1572872 | tf_op jit(solution)/shard_map/ppermute | solution.py:473
  114.3 20.2 %collective-permute-start.36 = (bf16[1024,256]{1,0:T(8,128)(2,1)S(1)}, bf16[1024,256]{1,0:T(8,128)(2,1)S(1)}, u32[]{:S(2)}, u32[]{:S(2)}) collective-permute-start(bf16[1024,256]{1,0:T(8,128)(2,1)S(1)} %slice.14), channel_id=1, source_target_pairs={{3,0},{0,1},{1,2},{2,3},{7,4},{4,5},{5,6},{6,7},{11,8},{8,9},{9,10... | collective-permute-start | bytes 1572872 | tf_op jit(solution)/shard_map/ppermute | solution.py:473
  115.9 18.6 %collective-permute-start.32 = (bf16[256,256]{1,0:T(8,128)(2,1)S(1)}, bf16[256,256]{1,0:T(8,128)(2,1)S(1)}, u32[]{:S(2)}, u32[]{:S(2)}) collective-permute-start(bf16[256,256]{1,0:T(8,128)(2,1)S(1)} %fusion.1), channel_id=1, source_target_pairs={{32,0},{33,1},{34,2},{35,3},{36,4},{37,5},{38,6},{39,7},{40,8},{41... | collective-permute-start | bytes 393224 | tf_op jit(solution)/shard_map/ppermute | solution.py:473
  118.7 15.7 %collective-permute-start.33 = (bf16[256,256]{1,0:T(8,128)(2,1)S(1)}, bf16[256,256]{1,0:T(8,128)(2,1)S(1)}, u32[]{:S(2)}, u32[]{:S(2)}) collective-permute-start(bf16[256,256]{1,0:T(8,128)(2,1)S(1)} %fusion.1), channel_id=1, source_target_pairs={{64,0},{65,1},{66,2},{67,3},{68,4},{69,5},{70,6},{71,7},{72,8},{73... | collective-permute-start | bytes 393224 | tf_op jit(solution)/shard_map/ppermute | solution.py:473
  119.3 15.2 %collective-permute-start.34 = (bf16[256,256]{1,0:T(8,128)(2,1)S(1)}, bf16[256,256]{1,0:T(8,128)(2,1)S(1)}, u32[]{:S(2)}, u32[]{:S(2)}) collective-permute-start(bf16[256,256]{1,0:T(8,128)(2,1)S(1)} %fusion.1), channel_id=1, source_target_pairs={{96,0},{97,1},{98,2},{99,3},{100,4},{101,5},{102,6},{103,7},{104,8... | collective-permute-start | bytes 393224 | tf_op jit(solution)/shard_map/ppermute | solution.py:473
  134.5 10.2 %collective-permute-start.37 = (bf16[176,256]{1,0:T(8,128)(2,1)}, bf16[176,256]{1,0:T(8,128)(2,1)S(1)}, u32[]{:S(2)}, u32[]{:S(2)}) collective-permute-start(bf16[176,256]{1,0:T(8,128)(2,1)} %get-tuple-element.204), channel_id=1, source_target_pairs={{1,0},{2,1},{3,2},{0,3},{5,4},{6,5},{7,6},{4,7},{9,8},{10,9},{11,1... | collective-permute-start | bytes 270344 | tf_op jit(solution)/shard_map/ppermute | solution.py:473
  136.6 8.2 %collective-permute-start.38 = (bf16[176,256]{1,0:T(8,128)(2,1)}, bf16[176,256]{1,0:T(8,128)(2,1)S(1)}, u32[]{:S(2)}, u32[]{:S(2)}) collective-permute-start(bf16[176,256]{1,0:T(8,128)(2,1)} %get-tuple-element.203), channel_id=1, source_target_pairs={{2,0},{3,1},{0,2},{1,3},{6,4},{7,5},{4,6},{5,7},{10,8},{11,9},{8,1... | collective-permute-start | bytes 270344 | tf_op jit(solution)/shard_map/ppermute | solution.py:473
  136.8 8.0 %collective-permute-start.39 = (bf16[176,256]{1,0:T(8,128)(2,1)}, bf16[176,256]{1,0:T(8,128)(2,1)S(1)}, u32[]{:S(2)}, u32[]{:S(2)}) collective-permute-start(bf16[176,256]{1,0:T(8,128)(2,1)} %get-tuple-element.202), channel_id=1, source_target_pairs={{3,0},{0,1},{1,2},{2,3},{7,4},{4,5},{5,6},{6,7},{11,8},{8,9},{9,10... | collective-permute-start | bytes 270344 | tf_op jit(solution)/shard_map/ppermute | solution.py:473
  137.6 11.4 %collective-permute-start.41 = (bf16[1024,256]{1,0:T(8,128)(2,1)}, bf16[1024,256]{1,0:T(8,128)(2,1)S(1)}, u32[]{:S(2)}, u32[]{:S(2)}) collective-permute-start(bf16[1024,256]{1,0:T(8,128)(2,1)} %get-tuple-element.235), channel_id=1, source_target_pairs={{1,0},{2,1},{3,2},{0,3},{5,4},{6,5},{7,6},{4,7},{9,8},{10,9},{11,1... | collective-permute-start | bytes 1572872 | tf_op jit(solution)/shard_map/ppermute | solution.py:473
  140.0 11.8 %collective-permute-start.42 = (bf16[1024,256]{1,0:T(8,128)(2,1)}, bf16[1024,256]{1,0:T(8,128)(2,1)S(1)}, u32[]{:S(2)}, u32[]{:S(2)}) collective-permute-start(bf16[1024,256]{1,0:T(8,128)(2,1)} %get-tuple-element.234), channel_id=1, source_target_pairs={{3,0},{0,1},{1,2},{2,3},{7,4},{4,5},{5,6},{6,7},{11,8},{8,9},{9,10... | collective-permute-start | bytes 1572872 | tf_op jit(solution)/shard_map/ppermute | solution.py:473
  151.8 13.6 %collective-permute-start.46 = (bf16[1024,256]{1,0:T(8,128)(2,1)S(1)}, bf16[1024,256]{1,0:T(8,128)(2,1)S(1)}, u32[]{:S(2)}, u32[]{:S(2)}) collective-permute-start(bf16[1024,256]{1,0:T(8,128)(2,1)S(1)} %collective-permute-done.41.refs_0_), channel_id=1, source_target_pairs={{1,0},{2,1},{3,2},{0,3},{5,4},{6,5},{7,6},{4,7},{9,8},{10,9},{11,1... | collective-permute-start | bytes 1572872 | tf_op jit(solution)/shard_map/ppermute | solution.py:473
  152.1 13.2 %collective-permute-start.47 = (bf16[1024,256]{1,0:T(8,128)(2,1)S(1)}, bf16[1024,256]{1,0:T(8,128)(2,1)S(1)}, u32[]{:S(2)}, u32[]{:S(2)}) collective-permute-start(bf16[1024,256]{1,0:T(8,128)(2,1)S(1)} %collective-permute-done.42.refs_3_), channel_id=1, source_target_pairs={{3,0},{0,1},{1,2},{2,3},{7,4},{4,5},{5,6},{6,7},{11,8},{8,9},{9,10... | collective-permute-start | bytes 1572872 | tf_op jit(solution)/shard_map/ppermute | solution.py:473
  153.8 7.9 %collective-permute-start.43 = (bf16[432,256]{1,0:T(8,128)(2,1)S(1)}, bf16[432,256]{1,0:T(8,128)(2,1)S(1)}, u32[]{:S(2)}, u32[]{:S(2)}) collective-permute-start(bf16[432,256]{1,0:T(8,128)(2,1)S(1)} %pad_maximum_fusion), channel_id=1, source_target_pairs={{8,0},{9,1},{10,2},{11,3},{12,4},{13,5},{14,6},{15,7},{16,8},{17,9... | collective-permute-start | bytes 663560 | tf_op jit(solution)/shard_map/ppermute | solution.py:473
  155.8 7.5 %collective-permute-start.44 = (bf16[432,256]{1,0:T(8,128)(2,1)S(1)}, bf16[432,256]{1,0:T(8,128)(2,1)S(1)}, u32[]{:S(2)}, u32[]{:S(2)}) collective-permute-start(bf16[432,256]{1,0:T(8,128)(2,1)S(1)} %pad_maximum_fusion), channel_id=1, source_target_pairs={{16,0},{17,1},{18,2},{19,3},{20,4},{21,5},{22,6},{23,7},{24,8},{25... | collective-permute-start | bytes 663560 | tf_op jit(solution)/shard_map/ppermute | solution.py:473
  155.8 9.5 %collective-permute-start.45 = (bf16[432,256]{1,0:T(8,128)(2,1)S(1)}, bf16[432,256]{1,0:T(8,128)(2,1)S(1)}, u32[]{:S(2)}, u32[]{:S(2)}) collective-permute-start(bf16[432,256]{1,0:T(8,128)(2,1)S(1)} %pad_maximum_fusion), channel_id=1, source_target_pairs={{24,0},{25,1},{26,2},{27,3},{28,4},{29,5},{30,6},{31,7},{0,8},{1,9... | collective-permute-start | bytes 663560 | tf_op jit(solution)/shard_map/ppermute | solution.py:473
  165.5 13.2 %collective-permute-start.52 = (bf16[1024,256]{1,0:T(8,128)(2,1)S(1)}, bf16[1024,256]{1,0:T(8,128)(2,1)S(1)}, u32[]{:S(2)}, u32[]{:S(2)}) collective-permute-start(bf16[1024,256]{1,0:T(8,128)(2,1)S(1)} %copy-done.35), channel_id=1, source_target_pairs={{1,0},{2,1},{3,2},{0,3},{5,4},{6,5},{7,6},{4,7},{9,8},{10,9},{11,1... | collective-permute-start | bytes 1572872 | tf_op jit(solution)/shard_map/ppermute | solution.py:473
  167.7 13.1 %collective-permute-start.53 = (bf16[1024,256]{1,0:T(8,128)(2,1)S(1)}, bf16[1024,256]{1,0:T(8,128)(2,1)S(1)}, u32[]{:S(2)}, u32[]{:S(2)}) collective-permute-start(bf16[1024,256]{1,0:T(8,128)(2,1)S(1)} %copy-done.34), channel_id=1, source_target_pairs={{3,0},{0,1},{1,2},{2,3},{7,4},{4,5},{5,6},{6,7},{11,8},{8,9},{9,10... | collective-permute-start | bytes 1572872 | tf_op jit(solution)/shard_map/ppermute | solution.py:473
  169.4 9.2 %collective-permute-start.49 = (bf16[176,256]{1,0:T(8,128)(2,1)S(1)}, bf16[176,256]{1,0:T(8,128)(2,1)S(1)}, u32[]{:S(2)}, u32[]{:S(2)}) collective-permute-start(bf16[176,256]{1,0:T(8,128)(2,1)S(1)} %slice.19.t0), channel_id=1, source_target_pairs={{32,0},{33,1},{34,2},{35,3},{36,4},{37,5},{38,6},{39,7},{40,8},{41... | collective-permute-start | bytes 270344 | tf_op jit(solution)/shard_map/ppermute | solution.py:473
  170.0 8.6 %collective-permute-start.50 = (bf16[176,256]{1,0:T(8,128)(2,1)S(1)}, bf16[176,256]{1,0:T(8,128)(2,1)S(1)}, u32[]{:S(2)}, u32[]{:S(2)}) collective-permute-start(bf16[176,256]{1,0:T(8,128)(2,1)S(1)} %slice.19.t0), channel_id=1, source_target_pairs={{64,0},{65,1},{66,2},{67,3},{68,4},{69,5},{70,6},{71,7},{72,8},{73... | collective-permute-start | bytes 270344 | tf_op jit(solution)/shard_map/ppermute | solution.py:473
  172.9 5.7 %collective-permute-start.51 = (bf16[176,256]{1,0:T(8,128)(2,1)S(1)}, bf16[176,256]{1,0:T(8,128)(2,1)S(1)}, u32[]{:S(2)}, u32[]{:S(2)}) collective-permute-start(bf16[176,256]{1,0:T(8,128)(2,1)S(1)} %slice.19.t0), channel_id=1, source_target_pairs={{96,0},{97,1},{98,2},{99,3},{100,4},{101,5},{102,6},{103,7},{104,8... | collective-permute-start | bytes 270344 | tf_op jit(solution)/shard_map/ppermute | solution.py:473
  (42 other events, 267.7 us)

commit v3 on v2

--- a/solution.py
+++ b/solution.py
@@ -235,15 +235,15 @@
     normed_t = normed_mid.T
     for k in range(BLOCKS):
         up, down = ups[k][...], downs[k][...]
-        hidden = dot_nt(normed_mid, up)
+        hidden = dot_nt(normed_mid, up).astype(BF)
         square = hidden * hidden
         inner = jnp.tanh(hidden * (C0 + C1 * square))
         half = 0.5 + 0.5 * inner
         gelu = hidden * half
-        active = gelu.astype(BF)
+        active = gelu
         total = total + dot(active, down)
         slope = half + gelu * (1.0 - half) * (2.0 * C0 + 6.0 * C1 * square)
-        ghid = (dot_nt(cotangent, down) * slope).astype(BF)
+        ghid = dot_nt(cotangent, down).astype(BF) * slope
         part = dot(ghid, up)
         gmid = part if gmid is None else gmid + part
         acc_w[k, 0:C, :] += dot(cot_t, active)

time: 187 us -> 185 us (0.989)
  no operation moved by 1% of the time
where the time goes in v3:
time: 185 us
  starting transfers between devices  68.6 us (37%)
  Pallas kernels  68 us (37%)
  waiting for transfers between devices  38.7 us (21%)
  local copies, waits for them, and re-layouts  4.28 us (2%)
  other arithmetic  3.59 us (2%)
    ppermute x54, starting transfers between devices, pull(): return lax.ppermute(value, axes, pairs)  68.6 us
    ppermute x54, waiting for transfers between devices, pull(): return lax.ppermute(value, axes, pairs)  38.7 us
    pallas_call x1, Pallas kernels, mlp_call(): pl.pallas_call(mlp_kernel, grid_spec=grid((quarter // size,), [row_spec(s...  15.7 us
    pallas_call x1, Pallas kernels, points_call(): pl.pallas_call(points_kernel, grid_spec=grid((steps,), [row_spec(size, 0)...  13.4 us
    pallas_call x3, Pallas kernels, fill_call(): pl.pallas_call(fill_kernel, grid_spec=grid((n,), [s for _, s in parts] +...  12.7 us
    pallas_call x1, Pallas kernels, local(): pl.pallas_call(own_sums_kernel, grid=(rows // (2 * WIDE),), in_specs=[pl....  8.94 us
    pallas_call x1, Pallas kernels, weights_call(): pl.pallas_call(weights_kernel, grid_spec=grid((quarter // WIDE,), [row_sp...  5.64 us
    unnamed x72, local copies, waits for them, and re-layouts  4.18 us
  transfers between devices with their start and end apart: 54, of which 19 were waited for; matrix products, arithmetic and copies ran while one was open for 2% of the time, Pallas kernels for 20%

profile of v3, /device:TPU:2, one launch (start us, length us, event | category | flops | bytes accessed | tf_op | source)
XLA Modules:
  0.0 184.5 jit_solution(7007082527573279898)
XLA Ops:
  0.6 2.1 %prep.1 = (bf16[656,256]{1,0:T(8,128)(2,1)}, bf16[512,256]{1,0:T(8,128)(2,1)}, bf16[256,512]{1,0:T(8,128)(2,1)}, f32[1,256]{1,0:T(1,128)}, f32[1,256]{1,0:T(1,128)}) custom-call(bf16[256,256]{1,0:T(8,128)(2,1)} %w_up.1, bf16[256,256]{1,0:T(8,128)(2,1)} %w_down.1, bf16[64,256]{1,0:T(8,128)(2,1)} %bitcast.7, bf16[64,256]{1,0:T(8,128)(2,1)} %w_out.1, ...), custom_call_target="tpu_custom_call" | custom-call | flops 2000000 | bytes 1024 | tf_op jit(solution)/shard_map/prep/pallas_call | solution.py:523
  2.7 8.9 %own_sums.1 = f32[40,128]{1,0:T(8,128)} custom-call(bf16[8192,256]{1,0:T(8,128)(2,1)} %pts.7, f32[1,256]{1,0:T(1,128)} %get-tuple-element.135.gain.refs_8_, bf16[656,256]{1,0:T(8,128)(2,1)} %get-tuple-element.143.w_in.sharp.in0.s0.refs_5_.refs_9_.refs_13_.refs_11_.refs_15_, bf16[512,256]{1,0:T(8,128)(2,1)} %get-tuple-element.137.spread_slices.refs_9_, ...), custom_call_target="tpu_custom_call" | custom-call | flops 8000000 | bytes 1024 | tf_op jit(solution)/shard_map/own_sums/pallas_call | solution.py:533
  14.2 1.6 collective-permute-start.3
  15.8 3.3 %collective-permute-start.1 = (f32[40,128]{1,0:T(8,128)S(1)}, f32[40,128]{1,0:T(8,128)S(1)}, u32[]{:S(2)}, u32[]{:S(2)}) collective-permute-start(f32[40,128]{1,0:T(8,128)S(1)} %add.83), channel_id=1, source_target_pairs={{64,0},{65,1},{66,2},{67,3},{68,4},{69,5},{70,6},{71,7},{72,8},{73... | collective-permute-start | bytes 61448 | tf_op jit(solution)/shard_map/ppermute | solution.py:473
  19.2 4.0 %collective-permute-start.10 = (bf16[656,256]{1,0:T(8,128)(2,1)}, bf16[656,256]{1,0:T(8,128)(2,1)S(1)}, u32[]{:S(2)}, u32[]{:S(2)}) collective-permute-start(bf16[656,256]{1,0:T(8,128)(2,1)} %get-tuple-element.143.w_in.sharp.in0.s0.refs_5_.refs_9_.refs_13_.refs_11_.refs_15_), channel_id=1, source_target_pairs={{1,0},{2,1},{3,2},{0,3},{5,4},{6,5},{7,6},{4,7},{9,8},{10,9},{11,1... | collective-permute-start | bytes 1007624 | tf_op jit(solution)/shard_map/ppermute | solution.py:473
  23.2 1.9 %collective-permute-start.11 = (bf16[656,256]{1,0:T(8,128)(2,1)}, bf16[656,256]{1,0:T(8,128)(2,1)S(1)}, u32[]{:S(2)}, u32[]{:S(2)}) collective-permute-start(bf16[656,256]{1,0:T(8,128)(2,1)} %get-tuple-element.143.w_in.sharp.in0.s0.refs_5_.refs_9_.refs_13_.refs_11_.refs_15_), channel_id=1, source_target_pairs={{2,0},{3,1},{0,2},{1,3},{6,4},{7,5},{4,6},{5,7},{10,8},{11,9},{8,1... | collective-permute-start | bytes 1007624 | tf_op jit(solution)/shard_map/ppermute | solution.py:473
  25.2 3.0 %collective-permute-start.4 = (f32[40,128]{1,0:T(8,128)S(1)}, f32[40,128]{1,0:T(8,128)S(1)}, u32[]{:S(2)}, u32[]{:S(2)}) collective-permute-start(f32[40,128]{1,0:T(8,128)S(1)} %add_add_fusion.3.a), channel_id=1, source_target_pairs={{8,0},{9,1},{10,2},{11,3},{12,4},{13,5},{14,6},{15,7},{16,8},{17,9... | collective-permute-start | bytes 61448 | tf_op jit(solution)/shard_map/ppermute | solution.py:473
  30.5 2.9 %collective-permute-done.5.c = f32[40,128]{1,0:T(8,128)S(1)} collective-permute-done((f32[40,128]{1,0:T(8,128)S(1)}, f32[40,128]{1,0:T(8,128)S(1)}, u32[]{:S(2)}, u32[]{:S(2)}) %collective-permute-start.5) | collective-permute-done | bytes 20512 | tf_op jit(solution)/shard_map/ppermute | solution.py:473
  33.5 1.5 collective-permute-done.6.d
  35.6 2.4 %tokens.1 = (f32[40,128]{1,0:T(8,128)}, f32[32,128]{1,0:T(8,128)}) custom-call(f32[40,128]{1,0:T(8,128)} %copy-done.20, f32[40,128]{1,0:T(8,128)} %copy-done.28, f32[40,128]{1,0:T(8,128)} %copy-done.29, f32[40,128]{1,0:T(8,128)} %copy-done.30, bf16[32,32]{1,0:T(8,128)(2,1)} %wq.3, bf16[32,32]{1,0:T(8,128)(2,1)} %wk.3, bf16[32,32]{1,0:T(8,128)(2,1)} %wv.3), custom_call_target="tpu_custom_call" | custom-call | flops 3000000 | bytes 1024 | tf_op jit(solution)/shard_map/tokens/pallas_call | solution.py:680
  39.4 2.8 %collective-permute-start.8 = (f32[32,128]{1,0:T(8,128)}, f32[32,128]{1,0:T(8,128)S(1)}, u32[]{:S(2)}, u32[]{:S(2)}) collective-permute-start(f32[32,128]{1,0:T(8,128)} %get-tuple-element.150.refs_0_), channel_id=1, source_target_pairs={{2,0},{3,1},{0,2},{1,3},{6,4},{7,5},{4,6},{5,7},{10,8},{11,9},{8,1... | collective-permute-start | bytes 49160 | tf_op jit(solution)/shard_map/ppermute | solution.py:473
  44.4 5.6 %weights.1 = (bf16[512,2048]{1,0:T(8,128)(2,1)}, bf16[2048,256]{1,0:T(8,128)(2,1)}) custom-call(s32[2]{0:T(128)} %pad_add_fusion.z, bf16[8192,256]{1,0:T(8,128)(2,1)} %pts.7, f32[1,256]{1,0:T(1,128)} %get-tuple-element.135.gain.refs_8_, bf16[656,256]{1,0:T(8,128)(2,1)} %get-tuple-element.143.w_in.sharp.in0.s0.refs_5_.refs_9_.refs_13_.refs_11_.refs_15_, ...), custom_call_target="tpu_custom_call" | custom-call | flops 5000000 | bytes 1024 | tf_op jit(solution)/shard_map/weights/pallas_call | solution.py:554
  50.7 15.7 %mlp.1 = (f32[8192,256]{1,0:T(8,128)}, bf16[2048,256]{1,0:T(8,128)(2,1)}, bf16[2048,256]{1,0:T(8,128)(2,1)}, bf16[2048,256]{1,0:T(8,128)(2,1)}, f32[32,128]{1,0:...) custom-call(s32[2]{0:T(128)} %pad_add_fusion.z, ...), custom_call_target="tpu_custom_call" | custom-call | flops 16000000 | bytes 1024 | tf_op jit(solution)/shard_map/mlp/pallas_call | solution.py:580
  66.4 3.2 %collective-permute-start.14 = (f32[32,128]{1,0:T(8,128)}, f32[32,128]{1,0:T(8,128)S(1)}, u32[]{:S(2)}, u32[]{:S(2)}) collective-permute-start(f32[32,128]{1,0:T(8,128)} %get-tuple-element.160), channel_id=1, source_target_pairs={{1,0},{2,1},{3,2},{0,3},{5,4},{6,5},{7,6},{4,7},{9,8},{10,9},{11,1... | collective-permute-start | bytes 49160 | tf_op jit(solution)/shard_map/ppermute | solution.py:473
  69.6 1.5 collective-permute-start.13
  71.2 1.7 collective-permute-start.20
  72.9 2.9 %collective-permute-start.21 = (bf16[512,256]{1,0:T(8,128)(2,1)}, bf16[512,256]{1,0:T(8,128)(2,1)S(1)}, u32[]{:S(2)}, u32[]{:S(2)}) collective-permute-start(bf16[512,256]{1,0:T(8,128)(2,1)} %get-tuple-element.167), channel_id=1, source_target_pairs={{2,0},{3,1},{0,2},{1,3},{6,4},{7,5},{4,6},{5,7},{10,8},{11,9},{8,1... | collective-permute-start | bytes 786440 | tf_op jit(solution)/shard_map/ppermute | solution.py:473
  78.1 1.9 %collective-permute-start.18 = (f32[32,128]{1,0:T(8,128)S(1)}, f32[32,128]{1,0:T(8,128)S(1)}, u32[]{:S(2)}, u32[]{:S(2)}) collective-permute-start(f32[32,128]{1,0:T(8,128)S(1)} %add.90), channel_id=1, source_target_pairs={{64,0},{65,1},{66,2},{67,3},{68,4},{69,5},{70,6},{71,7},{72,8},{73... | collective-permute-start | bytes 49160 | tf_op jit(solution)/shard_map/ppermute | solution.py:473
  80.0 1.6 collective-permute-done.17
  83.3 3.1 %collective-permute-start.30 = (bf16[2048,256]{1,0:T(8,128)(2,1)}, bf16[2048,256]{1,0:T(8,128)(2,1)S(1)}, u32[]{:S(2)}, u32[]{:S(2)}) collective-permute-start(bf16[2048,256]{1,0:T(8,128)(2,1)} %get-tuple-element.183), channel_id=1, source_target_pairs={{1,0},{2,1},{3,2},{0,3},{5,4},{6,5},{7,6},{4,7},{9,8},{10,9},{11,1... | collective-permute-start | bytes 3145736 | tf_op jit(solution)/shard_map/ppermute | solution.py:473
  86.5 2.1 %collective-permute-start.23 = (f32[32,128]{1,0:T(8,128)S(1)}, f32[32,128]{1,0:T(8,128)S(1)}, u32[]{:S(2)}, u32[]{:S(2)}) collective-permute-start(f32[32,128]{1,0:T(8,128)S(1)} %add_add_fusion.4.a), channel_id=1, source_target_pairs={{8,0},{9,1},{10,2},{11,3},{12,4},{13,5},{14,6},{15,7},{16,8},{17,9... | collective-permute-start | bytes 49160 | tf_op jit(solution)/shard_map/ppermute | solution.py:473
  90.8 3.0 %collective-permute-done.24.c = f32[32,128]{1,0:T(8,128)S(1)} collective-permute-done((f32[32,128]{1,0:T(8,128)S(1)}, f32[32,128]{1,0:T(8,128)S(1)}, u32[]{:S(2)}, u32[]{:S(2)}) %collective-permute-start.24) | collective-permute-done | bytes 16416 | tf_op jit(solution)/shard_map/ppermute | solution.py:473
  94.4 3.3 %tokens_back.1 = (f32[40,128]{1,0:T(8,128)}, f32[32,128]{1,0:T(8,128)}) custom-call(f32[40,128]{1,0:T(8,128)} %get-tuple-element.157.nd, f32[32,128]{1,0:T(8,128)} %copy-done.24, f32[32,128]{1,0:T(8,128)} %copy-done.31, f32[32,128]{1,0:T(8,128)} %copy-done.32, f32[32,128]{1,0:T(8,128)} %copy-done.33, bf16[32,32]{1,0:T(8,128)(2,1)} %wq.3, bf16[32,32]{1,0:T(8,128)(2,1)} %wk.3, ...), custom_call_target="tpu_custom_call" | custom-call | flops 4000000 | bytes 1024 | tf_op jit(solution)/shard_map/tokens_back/pallas_call | solution.py:712
  97.7 3.2 %collective-permute-start.26 = (f32[40,128]{1,0:T(8,128)}, f32[40,128]{1,0:T(8,128)S(1)}, u32[]{:S(2)}, u32[]{:S(2)}) collective-permute-start(f32[40,128]{1,0:T(8,128)} %get-tuple-element.177.refs_4_), channel_id=1, source_target_pairs={{1,0},{2,1},{3,2},{0,3},{5,4},{6,5},{7,6},{4,7},{9,8},{10,9},{11,1... | collective-permute-start | bytes 61448 | tf_op jit(solution)/shard_map/ppermute | solution.py:473
  100.9 1.7 collective-permute-start.27
  102.6 6.3 %collective-permute-done.26.refs_5_ = f32[40,128]{1,0:T(8,128)S(1)} collective-permute-done((f32[40,128]{1,0:T(8,128)}, f32[40,128]{1,0:T(8,128)S(1)}, u32[]{:S(2)}, u32[]{:S(2)}) %collective-permute-start.26) | collective-permute-done | bytes 20512 | tf_op jit(solution)/shard_map/ppermute | solution.py:473
  108.9 3.3 %collective-permute-done.27.refs_6_ = f32[40,128]{1,0:T(8,128)S(1)} collective-permute-done((f32[40,128]{1,0:T(8,128)}, f32[40,128]{1,0:T(8,128)S(1)}, u32[]{:S(2)}, u32[]{:S(2)}) %collective-permute-start.27) | collective-permute-done | bytes 20512 | tf_op jit(solution)/shard_map/ppermute | solution.py:473
  113.1 1.5 collective-permute-start.36
  114.6 2.9 %collective-permute-start.32 = (bf16[256,256]{1,0:T(8,128)(2,1)S(1)}, bf16[256,256]{1,0:T(8,128)(2,1)S(1)}, u32[]{:S(2)}, u32[]{:S(2)}) collective-permute-start(bf16[256,256]{1,0:T(8,128)(2,1)S(1)} %fusion.1), channel_id=1, source_target_pairs={{32,0},{33,1},{34,2},{35,3},{36,4},{37,5},{38,6},{39,7},{40,8},{41... | collective-permute-start | bytes 393224 | tf_op jit(solution)/shard_map/ppermute | solution.py:473
  118.0 1.8 collective-permute-start.34
  119.8 13.4 %points.1 = (f32[8192,256]{1,0:T(8,128)}, bf16[1024,256]{1,0:T(8,128)(2,1)}, bf16[1024,256]{1,0:T(8,128)(2,1)}, f32[176,256]{1,0:T(8,128)}, bf16[176,256]{1,0:T(...) custom-call(s32[2]{0:T(128)} %pad_add_fusion.z, bf16[8192,256]{1,0:T(8,128)(2,1)} %pts.7, ...), custom_call_target="tpu_custom_call" | custom-call | flops 12000000 | bytes 1024 | tf_op jit(solution)/shard_map/points/pallas_call | solution.py:611
  133.3 2.0 %collective-permute-start.37 = (bf16[176,256]{1,0:T(8,128)(2,1)}, bf16[176,256]{1,0:T(8,128)(2,1)S(1)}, u32[]{:S(2)}, u32[]{:S(2)}) collective-permute-start(bf16[176,256]{1,0:T(8,128)(2,1)} %get-tuple-element.204), channel_id=1, source_target_pairs={{1,0},{2,1},{3,2},{0,3},{5,4},{6,5},{7,6},{4,7},{9,8},{10,9},{11,1... | collective-permute-start | bytes 270344 | tf_op jit(solution)/shard_map/ppermute | solution.py:473
  136.3 2.4 %collective-permute-start.41 = (bf16[1024,256]{1,0:T(8,128)(2,1)}, bf16[1024,256]{1,0:T(8,128)(2,1)S(1)}, u32[]{:S(2)}, u32[]{:S(2)}) collective-permute-start(bf16[1024,256]{1,0:T(8,128)(2,1)} %get-tuple-element.235), channel_id=1, source_target_pairs={{1,0},{2,1},{3,2},{0,3},{5,4},{6,5},{7,6},{4,7},{9,8},{10,9},{11,1... | collective-permute-start | bytes 1572872 | tf_op jit(solution)/shard_map/ppermute | solution.py:473
  138.8 4.7 %fill.3.refs_2_ = f32[8192,256]{1,0:T(8,128)} custom-call(s32[2]{0:T(128)} %pad_add_fusion.z, bf16[2048,256]{1,0:T(8,128)(2,1)} %copy-done.3, bf16[2048,256]{1,0:T(8,128)(2,1)} %copy-done.3, bf16[1024,256]{1,0:T(8,128)(2,1)} %copy-done.8, bf16[1024,256]{1,0:T(8,128)(2,1)} %copy-done.9, ...), custom_call_target="tpu_custom_call", output_to_operand_aliasing={{}: (5, {})} | custom-call | flops 3000000 | bytes 1024 | tf_op jit(solution)/shard_map/fill/pallas_call | solution.py:656
  145.1 2.6 %collective-permute-done.41.refs_0_ = bf16[1024,256]{1,0:T(8,128)(2,1)S(1)} collective-permute-done((bf16[1024,256]{1,0:T(8,128)(2,1)}, bf16[1024,256]{1,0:T(8,128)(2,1)S(1)}, u32[]{:S(2)}, u32[]{:S(2)}) %collective-permute-start.41) | collective-permute-done | bytes 524320 | tf_op jit(solution)/shard_map/ppermute | solution.py:473
  147.7 2.7 %collective-permute-done.42.refs_3_ = bf16[1024,256]{1,0:T(8,128)(2,1)S(1)} collective-permute-done((bf16[1024,256]{1,0:T(8,128)(2,1)}, bf16[1024,256]{1,0:T(8,128)(2,1)S(1)}, u32[]{:S(2)}, u32[]{:S(2)}) %collective-permute-start.42) | collective-permute-done | bytes 524320 | tf_op jit(solution)/shard_map/ppermute | solution.py:473
  150.8 1.7 collective-permute-start.47
  152.5 2.0 %collective-permute-start.43 = (bf16[432,256]{1,0:T(8,128)(2,1)S(1)}, bf16[432,256]{1,0:T(8,128)(2,1)S(1)}, u32[]{:S(2)}, u32[]{:S(2)}) collective-permute-start(bf16[432,256]{1,0:T(8,128)(2,1)S(1)} %pad_maximum_fusion), channel_id=1, source_target_pairs={{8,0},{9,1},{10,2},{11,3},{12,4},{13,5},{14,6},{15,7},{16,8},{17,9... | collective-permute-start | bytes 663560 | tf_op jit(solution)/shard_map/ppermute | solution.py:473
  155.4 3.3 %fill.4 = f32[8192,256]{1,0:T(8,128)} custom-call(s32[2]{0:T(128)} %pad_add_fusion.z, bf16[2048,256]{1,0:T(8,128)(2,1)} %copy-done.4, bf16[2048,256]{1,0:T(8,128)(2,1)} %copy-done.4, f32[8192,256]{1,0:T(8,128)} %fill.3.refs_2_), custom_call_target="tpu_custom_call", output_to_operand_aliasing={{}: (3, {})} | custom-call | flops 3000000 | bytes 1024 | tf_op jit(solution)/shard_map/fill/pallas_call | solution.py:656
  158.7 1.7 collective-permute-done.43
  160.4 1.7 collective-permute-done.44
  162.1 2.0 %collective-permute-done.45 = bf16[432,256]{1,0:T(8,128)(2,1)S(1)} collective-permute-done((bf16[432,256]{1,0:T(8,128)(2,1)S(1)}, bf16[432,256]{1,0:T(8,128)(2,1)S(1)}, u32[]{:S(2)}, u32[]{:S(2)}) %collective-permute-start.45) | collective-permute-done | bytes 221216 | tf_op jit(solution)/shard_map/ppermute | solution.py:473
  164.2 2.3 %collective-permute-start.52 = (bf16[1024,256]{1,0:T(8,128)(2,1)S(1)}, bf16[1024,256]{1,0:T(8,128)(2,1)S(1)}, u32[]{:S(2)}, u32[]{:S(2)}) collective-permute-start(bf16[1024,256]{1,0:T(8,128)(2,1)S(1)} %copy-done.35), channel_id=1, source_target_pairs={{1,0},{2,1},{3,2},{0,3},{5,4},{6,5},{7,6},{4,7},{9,8},{10,9},{11,1... | collective-permute-start | bytes 1572872 | tf_op jit(solution)/shard_map/ppermute | solution.py:473
  166.6 1.5 collective-permute-done.48.w1
  168.7 3.0 %collective-permute-start.50 = (bf16[176,256]{1,0:T(8,128)(2,1)S(1)}, bf16[176,256]{1,0:T(8,128)(2,1)S(1)}, u32[]{:S(2)}, u32[]{:S(2)}) collective-permute-start(bf16[176,256]{1,0:T(8,128)(2,1)S(1)} %slice.19.t0), channel_id=1, source_target_pairs={{64,0},{65,1},{66,2},{67,3},{68,4},{69,5},{70,6},{71,7},{72,8},{73... | collective-permute-start | bytes 270344 | tf_op jit(solution)/shard_map/ppermute | solution.py:473
  172.6 4.7 %fill.5.before = f32[8192,256]{1,0:T(8,128)} custom-call(s32[2]{0:T(128)} %pad_add_fusion.z, bf16[1024,256]{1,0:T(8,128)(2,1)} %copy-done.6, bf16[1024,256]{1,0:T(8,128)(2,1)} %copy-done.10, bf16[1024,256]{1,0:T(8,128)(2,1)} %copy-done.11, bf16[1024,256]{1,0:T(8,128)(2,1)} %copy-done.7, ...), custom_call_target="tpu_custom_call", output_to_operand_aliasing={{}: (5, {})} | custom-call | flops 3000000 | bytes 1024 | tf_op jit(solution)/shard_map/fill/pallas_call | solution.py:656
  177.4 2.2 %collective-permute-done.53.second = bf16[1024,256]{1,0:T(8,128)(2,1)S(1)} collective-permute-done((bf16[1024,256]{1,0:T(8,128)(2,1)S(1)}, bf16[1024,256]{1,0:T(8,128)(2,1)S(1)}, u32[]{:S(2)}, u32[]{:S(2)}) %collective-permute-start.53) | collective-permute-done | bytes 524320 | tf_op jit(solution)/shard_map/ppermute | solution.py:473
  180.3 4.0 %finish.1 = (f32[8192,256]{1,0:T(8,128)}, f32[64,256]{1,0:T(8,128)}, f32[32,64]{1,0:T(8,128)}, f32[1,2]{1,0:T(1,128)}, f32[32,32]{1,0:T(8,128)}, /*index=5*/f32[...) custom-call(s32[2]{0:T(128)} %pad_add_fusion.z, ...), custom_call_target="tpu_custom_call", output_to_operand_aliasing={{0}: (3, {})} | custom-call | flops 4000000 | bytes 1024 | tf_op jit(solution)/shard_map/finish/pallas_call | solution.py:764
  (160 shorter events, 24.6 us)
Async XLA Ops:
  13.8 9.4 %collective-permute-start.2 = (f32[40,128]{1,0:T(8,128)S(1)}, f32[40,128]{1,0:T(8,128)S(1)}, u32[]{:S(2)}, u32[]{:S(2)}) collective-permute-start(f32[40,128]{1,0:T(8,128)S(1)} %add.83), channel_id=1, source_target_pairs={{32,0},{33,1},{34,2},{35,3},{36,4},{37,5},{38,6},{39,7},{40,8},{41... | collective-permute-start | bytes 61448 | tf_op jit(solution)/shard_map/ppermute | solution.py:473
  14.2 9.0 %collective-permute-start.3 = (f32[40,128]{1,0:T(8,128)S(1)}, f32[40,128]{1,0:T(8,128)S(1)}, u32[]{:S(2)}, u32[]{:S(2)}) collective-permute-start(f32[40,128]{1,0:T(8,128)S(1)} %add.83), channel_id=1, source_target_pairs={{96,0},{97,1},{98,2},{99,3},{100,4},{101,5},{102,6},{103,7},{104,8... | collective-permute-start | bytes 61448 | tf_op jit(solution)/shard_map/ppermute | solution.py:473
  15.8 7.4 %collective-permute-start.1 = (f32[40,128]{1,0:T(8,128)S(1)}, f32[40,128]{1,0:T(8,128)S(1)}, u32[]{:S(2)}, u32[]{:S(2)}) collective-permute-start(f32[40,128]{1,0:T(8,128)S(1)} %add.83), channel_id=1, source_target_pairs={{64,0},{65,1},{66,2},{67,3},{68,4},{69,5},{70,6},{71,7},{72,8},{73... | collective-permute-start | bytes 61448 | tf_op jit(solution)/shard_map/ppermute | solution.py:473
  19.2 23.1 %collective-permute-start.10 = (bf16[656,256]{1,0:T(8,128)(2,1)}, bf16[656,256]{1,0:T(8,128)(2,1)S(1)}, u32[]{:S(2)}, u32[]{:S(2)}) collective-permute-start(bf16[656,256]{1,0:T(8,128)(2,1)} %get-tuple-element.143.w_in.sharp.in0.s0.refs_5_.refs_9_.refs_13_.refs_11_.refs_15_), channel_id=1, source_target_pairs={{1,0},{2,1},{3,2},{0,3},{5,4},{6,5},{7,6},{4,7},{9,8},{10,9},{11,1... | collective-permute-start | bytes 1007624 | tf_op jit(solution)/shard_map/ppermute | solution.py:473
  23.2 19.7 %collective-permute-start.12 = (bf16[656,256]{1,0:T(8,128)(2,1)}, bf16[656,256]{1,0:T(8,128)(2,1)S(1)}, u32[]{:S(2)}, u32[]{:S(2)}) collective-permute-start(bf16[656,256]{1,0:T(8,128)(2,1)} %get-tuple-element.143.w_in.sharp.in0.s0.refs_5_.refs_9_.refs_13_.refs_11_.refs_15_), channel_id=1, source_target_pairs={{3,0},{0,1},{1,2},{2,3},{7,4},{4,5},{5,6},{6,7},{11,8},{8,9},{9,10... | collective-permute-start | bytes 1007624 | tf_op jit(solution)/shard_map/ppermute | solution.py:473
  23.2 19.7 %collective-permute-start.11 = (bf16[656,256]{1,0:T(8,128)(2,1)}, bf16[656,256]{1,0:T(8,128)(2,1)S(1)}, u32[]{:S(2)}, u32[]{:S(2)}) collective-permute-start(bf16[656,256]{1,0:T(8,128)(2,1)} %get-tuple-element.143.w_in.sharp.in0.s0.refs_5_.refs_9_.refs_13_.refs_11_.refs_15_), channel_id=1, source_target_pairs={{2,0},{3,1},{0,2},{1,3},{6,4},{7,5},{4,6},{5,7},{10,8},{11,9},{8,1... | collective-permute-start | bytes 1007624 | tf_op jit(solution)/shard_map/ppermute | solution.py:473
  25.2 4.5 %collective-permute-start.4 = (f32[40,128]{1,0:T(8,128)S(1)}, f32[40,128]{1,0:T(8,128)S(1)}, u32[]{:S(2)}, u32[]{:S(2)}) collective-permute-start(f32[40,128]{1,0:T(8,128)S(1)} %add_add_fusion.3.a), channel_id=1, source_target_pairs={{8,0},{9,1},{10,2},{11,3},{12,4},{13,5},{14,6},{15,7},{16,8},{17,9... | collective-permute-start | bytes 61448 | tf_op jit(solution)/shard_map/ppermute | solution.py:473
  28.2 5.3 %collective-permute-start.5 = (f32[40,128]{1,0:T(8,128)S(1)}, f32[40,128]{1,0:T(8,128)S(1)}, u32[]{:S(2)}, u32[]{:S(2)}) collective-permute-start(f32[40,128]{1,0:T(8,128)S(1)} %add_add_fusion.3.a), channel_id=1, source_target_pairs={{16,0},{17,1},{18,2},{19,3},{20,4},{21,5},{22,6},{23,7},{24,8},{25... | collective-permute-start | bytes 61448 | tf_op jit(solution)/shard_map/ppermute | solution.py:473
  29.7 5.3 %collective-permute-start.6 = (f32[40,128]{1,0:T(8,128)S(1)}, f32[40,128]{1,0:T(8,128)S(1)}, u32[]{:S(2)}, u32[]{:S(2)}) collective-permute-start(f32[40,128]{1,0:T(8,128)S(1)} %add_add_fusion.3.a), channel_id=1, source_target_pairs={{24,0},{25,1},{26,2},{27,3},{28,4},{29,5},{30,6},{31,7},{0,8},{1,9... | collective-permute-start | bytes 61448 | tf_op jit(solution)/shard_map/ppermute | solution.py:473
  37.9 12.1 %collective-permute-start.7 = (f32[32,128]{1,0:T(8,128)}, f32[32,128]{1,0:T(8,128)S(1)}, u32[]{:S(2)}, u32[]{:S(2)}) collective-permute-start(f32[32,128]{1,0:T(8,128)} %get-tuple-element.150.refs_0_), channel_id=1, source_target_pairs={{1,0},{2,1},{3,2},{0,3},{5,4},{6,5},{7,6},{4,7},{9,8},{10,9},{11,1... | collective-permute-start | bytes 49160 | tf_op jit(solution)/shard_map/ppermute | solution.py:473
  39.4 10.7 %collective-permute-start.8 = (f32[32,128]{1,0:T(8,128)}, f32[32,128]{1,0:T(8,128)S(1)}, u32[]{:S(2)}, u32[]{:S(2)}) collective-permute-start(f32[32,128]{1,0:T(8,128)} %get-tuple-element.150.refs_0_), channel_id=1, source_target_pairs={{2,0},{3,1},{0,2},{1,3},{6,4},{7,5},{4,6},{5,7},{10,8},{11,9},{8,1... | collective-permute-start | bytes 49160 | tf_op jit(solution)/shard_map/ppermute | solution.py:473
  42.2 7.8 %collective-permute-start.9 = (f32[32,128]{1,0:T(8,128)}, f32[32,128]{1,0:T(8,128)S(1)}, u32[]{:S(2)}, u32[]{:S(2)}) collective-permute-start(f32[32,128]{1,0:T(8,128)} %get-tuple-element.150.refs_0_), channel_id=1, source_target_pairs={{3,0},{0,1},{1,2},{2,3},{7,4},{4,5},{5,6},{6,7},{11,8},{8,9},{9,10... | collective-permute-start | bytes 49160 | tf_op jit(solution)/shard_map/ppermute | solution.py:473
  66.4 9.4 %collective-permute-start.14 = (f32[32,128]{1,0:T(8,128)}, f32[32,128]{1,0:T(8,128)S(1)}, u32[]{:S(2)}, u32[]{:S(2)}) collective-permute-start(f32[32,128]{1,0:T(8,128)} %get-tuple-element.160), channel_id=1, source_target_pairs={{1,0},{2,1},{3,2},{0,3},{5,4},{6,5},{7,6},{4,7},{9,8},{10,9},{11,1... | collective-permute-start | bytes 49160 | tf_op jit(solution)/shard_map/ppermute | solution.py:473
  69.6 6.2 %collective-permute-start.15 = (f32[32,128]{1,0:T(8,128)}, f32[32,128]{1,0:T(8,128)S(1)}, u32[]{:S(2)}, u32[]{:S(2)}) collective-permute-start(f32[32,128]{1,0:T(8,128)} %get-tuple-element.161), channel_id=1, source_target_pairs={{3,0},{0,1},{1,2},{2,3},{7,4},{4,5},{5,6},{6,7},{11,8},{8,9},{9,10... | collective-permute-start | bytes 49160 | tf_op jit(solution)/shard_map/ppermute | solution.py:473
  69.6 6.2 %collective-permute-start.13 = (f32[32,128]{1,0:T(8,128)}, f32[32,128]{1,0:T(8,128)S(1)}, u32[]{:S(2)}, u32[]{:S(2)}) collective-permute-start(f32[32,128]{1,0:T(8,128)} %get-tuple-element.159), channel_id=1, source_target_pairs={{2,0},{3,1},{0,2},{1,3},{6,4},{7,5},{4,6},{5,7},{10,8},{11,9},{8,1... | collective-permute-start | bytes 49160 | tf_op jit(solution)/shard_map/ppermute | solution.py:473
  71.2 15.3 %collective-permute-start.20 = (bf16[512,256]{1,0:T(8,128)(2,1)}, bf16[512,256]{1,0:T(8,128)(2,1)S(1)}, u32[]{:S(2)}, u32[]{:S(2)}) collective-permute-start(bf16[512,256]{1,0:T(8,128)(2,1)} %get-tuple-element.166), channel_id=1, source_target_pairs={{1,0},{2,1},{3,2},{0,3},{5,4},{6,5},{7,6},{4,7},{9,8},{10,9},{11,1... | collective-permute-start | bytes 786440 | tf_op jit(solution)/shard_map/ppermute | solution.py:473
  72.9 13.6 %collective-permute-start.21 = (bf16[512,256]{1,0:T(8,128)(2,1)}, bf16[512,256]{1,0:T(8,128)(2,1)S(1)}, u32[]{:S(2)}, u32[]{:S(2)}) collective-permute-start(bf16[512,256]{1,0:T(8,128)(2,1)} %get-tuple-element.167), channel_id=1, source_target_pairs={{2,0},{3,1},{0,2},{1,3},{6,4},{7,5},{4,6},{5,7},{10,8},{11,9},{8,1... | collective-permute-start | bytes 786440 | tf_op jit(solution)/shard_map/ppermute | solution.py:473
  76.5 9.9 %collective-permute-start.22 = (bf16[512,256]{1,0:T(8,128)(2,1)}, bf16[512,256]{1,0:T(8,128)(2,1)S(1)}, u32[]{:S(2)}, u32[]{:S(2)}) collective-permute-start(bf16[512,256]{1,0:T(8,128)(2,1)} %get-tuple-element.168), channel_id=1, source_target_pairs={{3,0},{0,1},{1,2},{2,3},{7,4},{4,5},{5,6},{6,7},{11,8},{8,9},{9,10... | collective-permute-start | bytes 786440 | tf_op jit(solution)/shard_map/ppermute | solution.py:473
  78.1 5.2 %collective-permute-start.18 = (f32[32,128]{1,0:T(8,128)S(1)}, f32[32,128]{1,0:T(8,128)S(1)}, u32[]{:S(2)}, u32[]{:S(2)}) collective-permute-start(f32[32,128]{1,0:T(8,128)S(1)} %add.90), channel_id=1, source_target_pairs={{64,0},{65,1},{66,2},{67,3},{68,4},{69,5},{70,6},{71,7},{72,8},{73... | collective-permute-start | bytes 49160 | tf_op jit(solution)/shard_map/ppermute | solution.py:473
  81.6 4.8 %collective-permute-start.19 = (f32[32,128]{1,0:T(8,128)S(1)}, f32[32,128]{1,0:T(8,128)S(1)}, u32[]{:S(2)}, u32[]{:S(2)}) collective-permute-start(f32[32,128]{1,0:T(8,128)S(1)} %add.90), channel_id=1, source_target_pairs={{96,0},{97,1},{98,2},{99,3},{100,4},{101,5},{102,6},{103,7},{104,8... | collective-permute-start | bytes 49160 | tf_op jit(solution)/shard_map/ppermute | solution.py:473
  83.3 29.0 %collective-permute-start.30 = (bf16[2048,256]{1,0:T(8,128)(2,1)}, bf16[2048,256]{1,0:T(8,128)(2,1)S(1)}, u32[]{:S(2)}, u32[]{:S(2)}) collective-permute-start(bf16[2048,256]{1,0:T(8,128)(2,1)} %get-tuple-element.183), channel_id=1, source_target_pairs={{1,0},{2,1},{3,2},{0,3},{5,4},{6,5},{7,6},{4,7},{9,8},{10,9},{11,1... | collective-permute-start | bytes 3145736 | tf_op jit(solution)/shard_map/ppermute | solution.py:473
  86.4 25.9 %collective-permute-start.31 = (bf16[2048,256]{1,0:T(8,128)(2,1)}, bf16[2048,256]{1,0:T(8,128)(2,1)S(1)}, u32[]{:S(2)}, u32[]{:S(2)}) collective-permute-start(bf16[2048,256]{1,0:T(8,128)(2,1)} %get-tuple-element.183), channel_id=1, source_target_pairs={{3,0},{0,1},{1,2},{2,3},{7,4},{4,5},{5,6},{6,7},{11,8},{8,9},{9,10... | collective-permute-start | bytes 3145736 | tf_op jit(solution)/shard_map/ppermute | solution.py:473
  88.6 5.2 %collective-permute-start.24 = (f32[32,128]{1,0:T(8,128)S(1)}, f32[32,128]{1,0:T(8,128)S(1)}, u32[]{:S(2)}, u32[]{:S(2)}) collective-permute-start(f32[32,128]{1,0:T(8,128)S(1)} %add_add_fusion.4.a), channel_id=1, source_target_pairs={{16,0},{17,1},{18,2},{19,3},{20,4},{21,5},{22,6},{23,7},{24,8},{25... | collective-permute-start | bytes 49160 | tf_op jit(solution)/shard_map/ppermute | solution.py:473
  88.7 5.1 %collective-permute-start.25 = (f32[32,128]{1,0:T(8,128)S(1)}, f32[32,128]{1,0:T(8,128)S(1)}, u32[]{:S(2)}, u32[]{:S(2)}) collective-permute-start(f32[32,128]{1,0:T(8,128)S(1)} %add_add_fusion.4.a), channel_id=1, source_target_pairs={{24,0},{25,1},{26,2},{27,3},{28,4},{29,5},{30,6},{31,7},{0,8},{1,9... | collective-permute-start | bytes 49160 | tf_op jit(solution)/shard_map/ppermute | solution.py:473
  97.7 4.9 %collective-permute-start.29 = (bf16[512,256]{1,0:T(8,128)(2,1)S(1)}, bf16[512,256]{1,0:T(8,128)(2,1)S(1)}, u32[]{:S(2)}, u32[]{:S(2)}) collective-permute-start(bf16[512,256]{1,0:T(8,128)(2,1)S(1)} %get-tuple-element.179), channel_id=1, source_target_pairs={{4,0},{5,1},{6,2},{7,3},{0,4},{1,5},{2,6},{3,7},{12,8},{13,9},{14,... | collective-permute-start | bytes 786440 | tf_op jit(solution)/shard_map/ppermute | solution.py:473
  97.7 11.2 %collective-permute-start.26 = (f32[40,128]{1,0:T(8,128)}, f32[40,128]{1,0:T(8,128)S(1)}, u32[]{:S(2)}, u32[]{:S(2)}) collective-permute-start(f32[40,128]{1,0:T(8,128)} %get-tuple-element.177.refs_4_), channel_id=1, source_target_pairs={{1,0},{2,1},{3,2},{0,3},{5,4},{6,5},{7,6},{4,7},{9,8},{10,9},{11,1... | collective-permute-start | bytes 61448 | tf_op jit(solution)/shard_map/ppermute | solution.py:473
  100.9 11.3 %collective-permute-start.27 = (f32[40,128]{1,0:T(8,128)}, f32[40,128]{1,0:T(8,128)S(1)}, u32[]{:S(2)}, u32[]{:S(2)}) collective-permute-start(f32[40,128]{1,0:T(8,128)} %get-tuple-element.177.refs_4_), channel_id=1, source_target_pairs={{2,0},{3,1},{0,2},{1,3},{6,4},{7,5},{4,6},{5,7},{10,8},{11,9},{8,1... | collective-permute-start | bytes 61448 | tf_op jit(solution)/shard_map/ppermute | solution.py:473
  102.6 9.7 %collective-permute-start.28 = (f32[40,128]{1,0:T(8,128)}, f32[40,128]{1,0:T(8,128)S(1)}, u32[]{:S(2)}, u32[]{:S(2)}) collective-permute-start(f32[40,128]{1,0:T(8,128)} %get-tuple-element.177.refs_4_), channel_id=1, source_target_pairs={{3,0},{0,1},{1,2},{2,3},{7,4},{4,5},{5,6},{6,7},{11,8},{8,9},{9,10... | collective-permute-start | bytes 61448 | tf_op jit(solution)/shard_map/ppermute | solution.py:473
  112.4 20.8 %collective-permute-start.35 = (bf16[1024,256]{1,0:T(8,128)(2,1)S(1)}, bf16[1024,256]{1,0:T(8,128)(2,1)S(1)}, u32[]{:S(2)}, u32[]{:S(2)}) collective-permute-start(bf16[1024,256]{1,0:T(8,128)(2,1)S(1)} %slice.13), channel_id=1, source_target_pairs={{1,0},{2,1},{3,2},{0,3},{5,4},{6,5},{7,6},{4,7},{9,8},{10,9},{11,1... | collective-permute-start | bytes 1572872 | tf_op jit(solution)/shard_map/ppermute | solution.py:473
  113.1 20.2 %collective-permute-start.36 = (bf16[1024,256]{1,0:T(8,128)(2,1)S(1)}, bf16[1024,256]{1,0:T(8,128)(2,1)S(1)}, u32[]{:S(2)}, u32[]{:S(2)}) collective-permute-start(bf16[1024,256]{1,0:T(8,128)(2,1)S(1)} %slice.14), channel_id=1, source_target_pairs={{3,0},{0,1},{1,2},{2,3},{7,4},{4,5},{5,6},{6,7},{11,8},{8,9},{9,10... | collective-permute-start | bytes 1572872 | tf_op jit(solution)/shard_map/ppermute | solution.py:473
  114.6 18.6 %collective-permute-start.32 = (bf16[256,256]{1,0:T(8,128)(2,1)S(1)}, bf16[256,256]{1,0:T(8,128)(2,1)S(1)}, u32[]{:S(2)}, u32[]{:S(2)}) collective-permute-start(bf16[256,256]{1,0:T(8,128)(2,1)S(1)} %fusion.1), channel_id=1, source_target_pairs={{32,0},{33,1},{34,2},{35,3},{36,4},{37,5},{38,6},{39,7},{40,8},{41... | collective-permute-start | bytes 393224 | tf_op jit(solution)/shard_map/ppermute | solution.py:473
  117.5 15.7 %collective-permute-start.33 = (bf16[256,256]{1,0:T(8,128)(2,1)S(1)}, bf16[256,256]{1,0:T(8,128)(2,1)S(1)}, u32[]{:S(2)}, u32[]{:S(2)}) collective-permute-start(bf16[256,256]{1,0:T(8,128)(2,1)S(1)} %fusion.1), channel_id=1, source_target_pairs={{64,0},{65,1},{66,2},{67,3},{68,4},{69,5},{70,6},{71,7},{72,8},{73... | collective-permute-start | bytes 393224 | tf_op jit(solution)/shard_map/ppermute | solution.py:473
  118.0 15.2 %collective-permute-start.34 = (bf16[256,256]{1,0:T(8,128)(2,1)S(1)}, bf16[256,256]{1,0:T(8,128)(2,1)S(1)}, u32[]{:S(2)}, u32[]{:S(2)}) collective-permute-start(bf16[256,256]{1,0:T(8,128)(2,1)S(1)} %fusion.1), channel_id=1, source_target_pairs={{96,0},{97,1},{98,2},{99,3},{100,4},{101,5},{102,6},{103,7},{104,8... | collective-permute-start | bytes 393224 | tf_op jit(solution)/shard_map/ppermute | solution.py:473
  133.3 10.2 %collective-permute-start.37 = (bf16[176,256]{1,0:T(8,128)(2,1)}, bf16[176,256]{1,0:T(8,128)(2,1)S(1)}, u32[]{:S(2)}, u32[]{:S(2)}) collective-permute-start(bf16[176,256]{1,0:T(8,128)(2,1)} %get-tuple-element.204), channel_id=1, source_target_pairs={{1,0},{2,1},{3,2},{0,3},{5,4},{6,5},{7,6},{4,7},{9,8},{10,9},{11,1... | collective-permute-start | bytes 270344 | tf_op jit(solution)/shard_map/ppermute | solution.py:473
  135.3 8.2 %collective-permute-start.38 = (bf16[176,256]{1,0:T(8,128)(2,1)}, bf16[176,256]{1,0:T(8,128)(2,1)S(1)}, u32[]{:S(2)}, u32[]{:S(2)}) collective-permute-start(bf16[176,256]{1,0:T(8,128)(2,1)} %get-tuple-element.203), channel_id=1, source_target_pairs={{2,0},{3,1},{0,2},{1,3},{6,4},{7,5},{4,6},{5,7},{10,8},{11,9},{8,1... | collective-permute-start | bytes 270344 | tf_op jit(solution)/shard_map/ppermute | solution.py:473
  135.5 8.0 %collective-permute-start.39 = (bf16[176,256]{1,0:T(8,128)(2,1)}, bf16[176,256]{1,0:T(8,128)(2,1)S(1)}, u32[]{:S(2)}, u32[]{:S(2)}) collective-permute-start(bf16[176,256]{1,0:T(8,128)(2,1)} %get-tuple-element.202), channel_id=1, source_target_pairs={{3,0},{0,1},{1,2},{2,3},{7,4},{4,5},{5,6},{6,7},{11,8},{8,9},{9,10... | collective-permute-start | bytes 270344 | tf_op jit(solution)/shard_map/ppermute | solution.py:473
  136.3 11.4 %collective-permute-start.41 = (bf16[1024,256]{1,0:T(8,128)(2,1)}, bf16[1024,256]{1,0:T(8,128)(2,1)S(1)}, u32[]{:S(2)}, u32[]{:S(2)}) collective-permute-start(bf16[1024,256]{1,0:T(8,128)(2,1)} %get-tuple-element.235), channel_id=1, source_target_pairs={{1,0},{2,1},{3,2},{0,3},{5,4},{6,5},{7,6},{4,7},{9,8},{10,9},{11,1... | collective-permute-start | bytes 1572872 | tf_op jit(solution)/shard_map/ppermute | solution.py:473
  138.7 11.7 %collective-permute-start.42 = (bf16[1024,256]{1,0:T(8,128)(2,1)}, bf16[1024,256]{1,0:T(8,128)(2,1)S(1)}, u32[]{:S(2)}, u32[]{:S(2)}) collective-permute-start(bf16[1024,256]{1,0:T(8,128)(2,1)} %get-tuple-element.234), channel_id=1, source_target_pairs={{3,0},{0,1},{1,2},{2,3},{7,4},{4,5},{5,6},{6,7},{11,8},{8,9},{9,10... | collective-permute-start | bytes 1572872 | tf_op jit(solution)/shard_map/ppermute | solution.py:473
  150.5 13.6 %collective-permute-start.46 = (bf16[1024,256]{1,0:T(8,128)(2,1)S(1)}, bf16[1024,256]{1,0:T(8,128)(2,1)S(1)}, u32[]{:S(2)}, u32[]{:S(2)}) collective-permute-start(bf16[1024,256]{1,0:T(8,128)(2,1)S(1)} %collective-permute-done.41.refs_0_), channel_id=1, source_target_pairs={{1,0},{2,1},{3,2},{0,3},{5,4},{6,5},{7,6},{4,7},{9,8},{10,9},{11,1... | collective-permute-start | bytes 1572872 | tf_op jit(solution)/shard_map/ppermute | solution.py:473
  150.8 13.2 %collective-permute-start.47 = (bf16[1024,256]{1,0:T(8,128)(2,1)S(1)}, bf16[1024,256]{1,0:T(8,128)(2,1)S(1)}, u32[]{:S(2)}, u32[]{:S(2)}) collective-permute-start(bf16[1024,256]{1,0:T(8,128)(2,1)S(1)} %collective-permute-done.42.refs_3_), channel_id=1, source_target_pairs={{3,0},{0,1},{1,2},{2,3},{7,4},{4,5},{5,6},{6,7},{11,8},{8,9},{9,10... | collective-permute-start | bytes 1572872 | tf_op jit(solution)/shard_map/ppermute | solution.py:473
  152.5 7.9 %collective-permute-start.43 = (bf16[432,256]{1,0:T(8,128)(2,1)S(1)}, bf16[432,256]{1,0:T(8,128)(2,1)S(1)}, u32[]{:S(2)}, u32[]{:S(2)}) collective-permute-start(bf16[432,256]{1,0:T(8,128)(2,1)S(1)} %pad_maximum_fusion), channel_id=1, source_target_pairs={{8,0},{9,1},{10,2},{11,3},{12,4},{13,5},{14,6},{15,7},{16,8},{17,9... | collective-permute-start | bytes 663560 | tf_op jit(solution)/shard_map/ppermute | solution.py:473
  154.5 7.5 %collective-permute-start.44 = (bf16[432,256]{1,0:T(8,128)(2,1)S(1)}, bf16[432,256]{1,0:T(8,128)(2,1)S(1)}, u32[]{:S(2)}, u32[]{:S(2)}) collective-permute-start(bf16[432,256]{1,0:T(8,128)(2,1)S(1)} %pad_maximum_fusion), channel_id=1, source_target_pairs={{16,0},{17,1},{18,2},{19,3},{20,4},{21,5},{22,6},{23,7},{24,8},{25... | collective-permute-start | bytes 663560 | tf_op jit(solution)/shard_map/ppermute | solution.py:473
  154.5 9.5 %collective-permute-start.45 = (bf16[432,256]{1,0:T(8,128)(2,1)S(1)}, bf16[432,256]{1,0:T(8,128)(2,1)S(1)}, u32[]{:S(2)}, u32[]{:S(2)}) collective-permute-start(bf16[432,256]{1,0:T(8,128)(2,1)S(1)} %pad_maximum_fusion), channel_id=1, source_target_pairs={{24,0},{25,1},{26,2},{27,3},{28,4},{29,5},{30,6},{31,7},{0,8},{1,9... | collective-permute-start | bytes 663560 | tf_op jit(solution)/shard_map/ppermute | solution.py:473
  164.2 13.2 %collective-permute-start.52 = (bf16[1024,256]{1,0:T(8,128)(2,1)S(1)}, bf16[1024,256]{1,0:T(8,128)(2,1)S(1)}, u32[]{:S(2)}, u32[]{:S(2)}) collective-permute-start(bf16[1024,256]{1,0:T(8,128)(2,1)S(1)} %copy-done.35), channel_id=1, source_target_pairs={{1,0},{2,1},{3,2},{0,3},{5,4},{6,5},{7,6},{4,7},{9,8},{10,9},{11,1... | collective-permute-start | bytes 1572872 | tf_op jit(solution)/shard_map/ppermute | solution.py:473
  166.5 13.1 %collective-permute-start.53 = (bf16[1024,256]{1,0:T(8,128)(2,1)S(1)}, bf16[1024,256]{1,0:T(8,128)(2,1)S(1)}, u32[]{:S(2)}, u32[]{:S(2)}) collective-permute-start(bf16[1024,256]{1,0:T(8,128)(2,1)S(1)} %copy-done.34), channel_id=1, source_target_pairs={{3,0},{0,1},{1,2},{2,3},{7,4},{4,5},{5,6},{6,7},{11,8},{8,9},{9,10... | collective-permute-start | bytes 1572872 | tf_op jit(solution)/shard_map/ppermute | solution.py:473
  168.1 9.2 %collective-permute-start.49 = (bf16[176,256]{1,0:T(8,128)(2,1)S(1)}, bf16[176,256]{1,0:T(8,128)(2,1)S(1)}, u32[]{:S(2)}, u32[]{:S(2)}) collective-permute-start(bf16[176,256]{1,0:T(8,128)(2,1)S(1)} %slice.19.t0), channel_id=1, source_target_pairs={{32,0},{33,1},{34,2},{35,3},{36,4},{37,5},{38,6},{39,7},{40,8},{41... | collective-permute-start | bytes 270344 | tf_op jit(solution)/shard_map/ppermute | solution.py:473
  168.7 8.6 %collective-permute-start.50 = (bf16[176,256]{1,0:T(8,128)(2,1)S(1)}, bf16[176,256]{1,0:T(8,128)(2,1)S(1)}, u32[]{:S(2)}, u32[]{:S(2)}) collective-permute-start(bf16[176,256]{1,0:T(8,128)(2,1)S(1)} %slice.19.t0), channel_id=1, source_target_pairs={{64,0},{65,1},{66,2},{67,3},{68,4},{69,5},{70,6},{71,7},{72,8},{73... | collective-permute-start | bytes 270344 | tf_op jit(solution)/shard_map/ppermute | solution.py:473
  171.7 5.7 %collective-permute-start.51 = (bf16[176,256]{1,0:T(8,128)(2,1)S(1)}, bf16[176,256]{1,0:T(8,128)(2,1)S(1)}, u32[]{:S(2)}, u32[]{:S(2)}) collective-permute-start(bf16[176,256]{1,0:T(8,128)(2,1)S(1)} %slice.19.t0), channel_id=1, source_target_pairs={{96,0},{97,1},{98,2},{99,3},{100,4},{101,5},{102,6},{103,7},{104,8... | collective-permute-start | bytes 270344 | tf_op jit(solution)/shard_map/ppermute | solution.py:473
  (42 other events, 267.3 us)
